TPU v7x, 32 devices: a whole 2x2x4 slice. The times are simulated.
32 devices in a mesh: pb: 2 (over x), ka: 16 (over z, y, core).
Axes of the slice: x: 2, y: 2, z: 4, core: 2. Of those that a mesh axis runs over, the one named last changes fastest.
Arguments:
- tokens: bfloat16 [4096, 768], P(('pb', 'ka')), may hold values from -6 to 6
- positions: float32 [3, 4096], replicated, may hold values from -24 to 24
- item_of_atom: int32 [4096], replicated, may hold values from 0 to 104, as said below
- item_lengths: int32 [105], replicated, may hold values from 8 to 768, as said below
- atom_types: int32 [4096], replicated, may hold values from 0 to 127, as said below
- key_mask: int32 [4096], replicated, may hold values 0 or 1
- ln1_gain: float32 [768], replicated, may hold values from 0.5 to 1.5
- ln1_bias: float32 [768], replicated, may hold values from -3 to 3
- w_qkv: bfloat16 [768, 2304], replicated, may hold values from -0.21875 to 0.21875
- kernel_means: float32 [128], replicated, may hold values from 0 to 16
- kernel_widths: float32 [128], replicated, may hold values from 0.5 to 4
- kernel_weight: bfloat16 [128, 32], replicated, may hold values from -6 to 6
- type_scale: float32 [160], replicated, may hold values from 0.5 to 1.5
- type_shift: float32 [160], replicated, may hold values from -3 to 3
- w_out: bfloat16 [768, 768], replicated, may hold values from -0.875 to 0.875
- ln2_gain: float32 [768], replicated, may hold values from 0.5 to 1.5
- ln2_bias: float32 [768], replicated, may hold values from -3 to 3
- w_up: bfloat16 [768, 3072], replicated, may hold values from -0.21875 to 0.21875
- w_down: bfloat16 [3072, 768], replicated, may hold values from -0.109375 to 0.109375
- out_cotangent: bfloat16 [4096, 768], P(('pb', 'ka')), may hold values from -6 to 6
Outputs:
- block_out: bfloat16 [4096, 768], P(('pb', 'ka'))
- grad_tokens: float32 [4096, 768], P(('pb', 'ka'))
- grad_positions: float32 [3, 4096], P(None, ('pb', 'ka'))
- grad_ln1_gain: float32 [768], replicated
- grad_ln1_bias: float32 [768], replicated
- grad_w_qkv: float32 [768, 2304], P(None, 'ka')
- grad_kernel_means: float32 [128], replicated
- grad_kernel_widths: float32 [128], replicated
- grad_kernel_weight: float32 [128, 32], replicated
- grad_type_scale: float32 [160], replicated
- grad_type_shift: float32 [160], replicated
- grad_w_out: float32 [768, 768], P(None, 'ka')
- grad_ln2_gain: float32 [768], replicated
- grad_ln2_bias: float32 [768], replicated
- grad_w_up: float32 [768, 3072], P(None, 'ka')
- grad_w_down: float32 [3072, 768], P('ka')
Inputs may be any that keep to these rules, and one draw needn't show every extreme that they name: `item_of_atom`: items are contiguous in atom order: item i holds the item_lengths[i] atoms that follow those of items 0 to i - 1; an item is a protein when it has more than 64 atoms, else a molecule. `item_lengths`: the lengths sum to 4096. `atom_types`: ids of protein atoms lie below 32.
All inputs are finite; a program needn't handle non-finite values.
Results may differ from a plain program's by a relative error of at most 0.017.
Values may be sent and summed in bfloat16 or wider, within the bound.
No kernel may reach another device: no remote copies, remote signals or barrier semaphores. Data moves between devices by JAX's collectives and lax.ppermute only.
A program may use at most 128 MiB of HBM per device.

v0:
```python
import math

import jax
import jax.numpy as jnp
from jax import lax
from jax.sharding import PartitionSpec as P

MOL_TYPES = 128
PROT_LEN = 768
MOL_MEAN = 32


LN_EPS = 1e-05
MASKED = -1e30
ROOT_TWO_PI = math.sqrt(2.0 * math.pi)


def shifted(block, axis, distance):
    devices = range(lax.axis_size(axis))
    route = [(i - distance, i) for i in devices if i - distance in devices]
    return lax.ppermute(block, axis, route)


def layer_norm(values, ln_gain, ln_shift):
    centre = jnp.mean(values, axis=-1, keepdims=True)
    offsets = values - centre
    spread = jnp.mean(offsets * offsets, axis=-1, keepdims=True)
    return offsets * lax.rsqrt(spread + LN_EPS) * ln_gain + ln_shift


def pair_geometry(
    query_pos, key_pos, query_scale, key_scale, query_shift, key_shift, centres, widths
):
    displace = query_pos[:, :, None] - key_pos[:, None, :]
    length = jnp.sqrt(jnp.sum(displace * displace, axis=0) + 1.0)
    stretched = (
        query_scale[:, None] * key_scale[None, :] * length
        + query_shift[:, None]
        + key_shift[None, :]
    )
    normed = (stretched[:, :, None] - centres) / widths
    return jnp.exp(-0.5 * normed * normed) / (ROOT_TWO_PI * widths)


def pair_allowed(query_item, key_item, key_open, query_global, key_global):
    same_item = query_item[:, None] == key_item[None, :]
    visible = (key_open[None, :] > 0) | (query_global[:, None] == key_global[None, :])
    return same_item & visible


def side_block(side, offset, extent):
    return tuple(
        (lax.dynamic_slice_in_dim(member, offset, extent, member.ndim - 1) for member in side)
    )


def scores_from(phi, query_block, key_block, query_side, key_side, kernel_weight, head_scale):
    phi_low = phi.astype(jnp.bfloat16)
    dots = jnp.einsum("qhd,khd->hqk", query_block, key_block, preferred_element_type=jnp.float32)
    bias_terms = jnp.einsum(
        "qkc,ch->hqk", phi_low, kernel_weight, preferred_element_type=jnp.float32
    )
    allowed = pair_allowed(query_side[3], key_side[3], key_side[4], query_side[5], key_side[5])
    return (jnp.where(allowed[None], dots * head_scale + bias_terms, MASKED), phi_low)


def atom_columns(pos_grad, scale_grad, shift_grad):
    return jnp.concatenate([pos_grad, scale_grad[None, :], shift_grad[None, :]], axis=0).T


def add_rows(total, term, offset):
    current = lax.dynamic_slice_in_dim(total, offset, term.shape[0], 0)
    return lax.dynamic_update_slice_in_dim(total, current + term, offset, 0)


def on_device(
    tokens,
    positions,
    item_of_atom,
    item_lengths,
    atom_types,
    key_mask,
    ln1_gain,
    ln1_bias,
    w_qkv,
    kernel_means,
    kernel_widths,
    kernel_weight,
    type_scale,
    type_shift,
    w_out,
    ln2_gain,
    ln2_bias,
    w_up,
    w_down,
    out_cotangent,
):
    own_rows = tokens.shape[0]
    model_width = tokens.shape[1]
    heads_count = kernel_weight.shape[1]
    head_size = model_width // heads_count
    head_scale = head_size ** (-0.5)
    ka_count = lax.axis_size("ka")
    flat_index = lax.axis_index("pb") * ka_count + lax.axis_index("ka")
    reach = (PROT_LEN + own_rows - 2) // own_rows
    margin = reach * own_rows
    window_rows = (2 * reach + 1) * own_rows
    atoms_total = positions.shape[1]
    own_start = flat_index * own_rows
    item_flags = (item_lengths > 2 * MOL_MEAN).astype(jnp.int32)
    table_ids = jnp.arange(type_scale.shape[0], dtype=jnp.int32)
    global_ids = jnp.arange(atoms_total, dtype=jnp.int32)

    def pick_own(member, fill):
        return lax.dynamic_slice_in_dim(member, own_start, own_rows, member.ndim - 1)

    def pick_window(member, fill):
        widths = [(0, 0)] * (member.ndim - 1) + [(margin, margin)]
        padded = jnp.pad(member, widths, constant_values=fill)
        return lax.dynamic_slice_in_dim(padded, own_start, window_rows, member.ndim - 1)

    def side_of(picker):
        items_here = picker(item_of_atom, -1)
        flags_here = jnp.where(items_here >= 0, item_flags[jnp.maximum(items_here, 0)], 0)
        index_here = picker(atom_types, 0) + MOL_TYPES * flags_here
        onehot = index_here[:, None] == table_ids[None, :]
        scale_here = jnp.sum(jnp.where(onehot, type_scale[None, :], 0.0), axis=1)
        shift_here = jnp.sum(jnp.where(onehot, type_shift[None, :], 0.0), axis=1)
        return (
            (
                picker(positions, 0.0),
                scale_here,
                shift_here,
                items_here,
                picker(key_mask, 0),
                picker(global_ids, -1),
            ),
            index_here,
        )

    query_side, query_index = side_of(pick_own)
    key_side, unused_index = side_of(pick_window)
    tokens_wide = tokens.astype(jnp.float32)
    normed_first, first_back = jax.vjp(layer_norm, tokens_wide, ln1_gain, ln1_bias)
    normed_first_low = normed_first.astype(jnp.bfloat16)
    projected = jnp.dot(normed_first_low, w_qkv, preferred_element_type=jnp.float32).astype(
        jnp.bfloat16
    )
    query_heads = projected[:, :model_width].reshape(own_rows, heads_count, head_size)
    shift_range = range(-reach, reach + 1)
    key_value_own = projected[:, model_width:]
    value_pieces = [
        key_value_own if offset == 0 else shifted(key_value_own, ("pb", "ka"), -offset)
        for offset in shift_range
    ]
    key_value_tile = jnp.concatenate(value_pieces, axis=0)
    key_heads = key_value_tile[:, :model_width].reshape(window_rows, heads_count, head_size)
    value_heads = key_value_tile[:, model_width:].reshape(window_rows, heads_count, head_size)
    block_rows = math.gcd(own_rows, 512)
    block_keys = math.gcd(window_rows, 128)
    key_steps = window_rows // block_keys

    def pair_scores(query_block, block_side, key_offset, key_block_side):
        key_block = lax.dynamic_slice_in_dim(key_heads, key_offset, block_keys, 0)
        phi = pair_geometry(
            block_side[0],
            key_block_side[0],
            block_side[1],
            key_block_side[1],
            block_side[2],
            key_block_side[2],
            kernel_means,
            kernel_widths,
        )
        return scores_from(
            phi, query_block, key_block, block_side, key_block_side, kernel_weight, head_scale
        )

    def attend_block(block_index, carry):
        row_offset = block_index * block_rows
        block_side = side_block(query_side, row_offset, block_rows)

        def stats_keys(key_index, running):
            key_offset = key_index * block_keys
            key_block_side = side_block(key_side, key_offset, block_keys)
            run_max, run_sum = running
            scores, unused_phi = pair_scores(query_heads, block_side, key_offset, key_block_side)
            new_max = jnp.maximum(run_max, jnp.max(scores, axis=2))
            new_sum = run_sum * jnp.exp(run_max - new_max) + jnp.sum(
                jnp.exp(scores - new_max[:, :, None]), axis=2
            )
            return (new_max, new_sum)

        initial = (
            jnp.full((heads_count, block_rows), MASKED, jnp.float32),
            jnp.zeros((heads_count, block_rows), jnp.float32),
        )
        block_max, block_sum = lax.fori_loop(0, key_steps, stats_keys, initial)
        block_lse = block_max + jnp.log(block_sum)

        def attend_keys(key_index, total):
            key_offset = key_index * block_keys
            key_block_side = side_block(key_side, key_offset, block_keys)
            scores, unused_phi = pair_scores(query_heads, block_side, key_offset, key_block_side)
            probs = jnp.exp(scores - block_lse[:, :, None]).astype(jnp.bfloat16)
            value_block = lax.dynamic_slice_in_dim(value_heads, key_offset, block_keys, 0)
            return total + jnp.einsum(
                "hqk,khd->qhd", probs, value_block, preferred_element_type=jnp.float32
            )

        block_out = lax.fori_loop(
            0, key_steps, attend_keys, jnp.zeros((block_rows, heads_count, head_size), jnp.float32)
        )
        output = block_out.reshape(block_rows, model_width)
        return (output, block_lse)

    forward_init = (
        jnp.zeros((own_rows, model_width), jnp.float32),
        jnp.zeros((heads_count, own_rows), jnp.float32),
    )
    attended, log_total = lax.fori_loop(0, own_rows // block_rows, attend_block, forward_init)
    attended_low = attended.astype(jnp.bfloat16)
    mixed = tokens_wide + jnp.dot(attended_low, w_out, preferred_element_type=jnp.float32)
    normed_second, second_back = jax.vjp(layer_norm, mixed, ln2_gain, ln2_bias)
    normed_second_low = normed_second.astype(jnp.bfloat16)
    up_proj = jnp.dot(normed_second_low, w_up, preferred_element_type=jnp.float32)
    activated, gelu_back = jax.vjp(jax.nn.gelu, up_proj)
    hidden_low = activated.astype(jnp.bfloat16)
    block_out = (mixed + jnp.dot(hidden_low, w_down, preferred_element_type=jnp.float32)).astype(
        jnp.bfloat16
    )
    grad_hidden = jnp.dot(out_cotangent, w_down.T, preferred_element_type=jnp.float32)
    down_columns = jnp.dot(out_cotangent.T, hidden_low, preferred_element_type=jnp.float32)
    grad_up = gelu_back(grad_hidden)[0].astype(jnp.bfloat16)
    up_grad_weight = jnp.dot(normed_second_low.T, grad_up, preferred_element_type=jnp.float32)
    grad_normed_second = jnp.dot(grad_up, w_up.T, preferred_element_type=jnp.float32)
    grad_mixed_norm, grad_gain_second, grad_shift_second = second_back(grad_normed_second)
    grad_mixed = out_cotangent.astype(jnp.float32) + grad_mixed_norm
    grad_mixed_low = grad_mixed.astype(jnp.bfloat16)
    out_grad_weight = jnp.dot(attended_low.T, grad_mixed_low, preferred_element_type=jnp.float32)
    grad_attended = jnp.dot(grad_mixed_low, w_out.T, preferred_element_type=jnp.float32).astype(
        jnp.bfloat16
    )
    row_deltas = jnp.sum(
        grad_attended.astype(jnp.float32).reshape(own_rows, heads_count, head_size)
        * attended.reshape(own_rows, heads_count, head_size),
        axis=2,
    ).T
    grad_heads = grad_attended.reshape(own_rows, heads_count, head_size)

    def back_rows(block_index, carry):
        (
            grad_query,
            grad_key_values,
            query_atoms,
            key_atoms,
            grad_kernel,
            grad_centres,
            grad_widths,
        ) = carry
        row_offset = block_index * block_rows
        block_side = side_block(query_side, row_offset, block_rows)

        def back_keys(key_index, inner):
            key_offset = key_index * block_keys
            key_block_side = side_block(key_side, key_offset, block_keys)
            (
                grad_query_block,
                grad_key_values,
                query_atoms_block,
                key_atoms,
                grad_kernel,
                grad_centres,
                grad_widths,
            ) = inner
            key_block = lax.dynamic_slice_in_dim(key_heads, key_offset, block_keys, 0)
            value_block = lax.dynamic_slice_in_dim(value_heads, key_offset, block_keys, 0)
            phi, geometry_back = jax.vjp(
                pair_geometry,
                block_side[0],
                key_block_side[0],
                block_side[1],
                key_block_side[1],
                block_side[2],
                key_block_side[2],
                kernel_means,
                kernel_widths,
            )
            scores, phi_low = scores_from(
                phi, query_heads, key_block, block_side, key_block_side, kernel_weight, head_scale
            )
            probs = jnp.exp(scores - log_total[:, :, None])
            grad_probs = jnp.einsum(
                "qhd,khd->hqk", grad_heads, value_block, preferred_element_type=jnp.float32
            )
            grad_scores = (probs * (grad_probs - row_deltas[:, :, None])).astype(jnp.bfloat16)
            grad_query_block = grad_query_block + head_scale * jnp.einsum(
                "hqk,khd->qhd", grad_scores, key_block, preferred_element_type=jnp.float32
            )
            key_term = head_scale * jnp.einsum(
                "hqk,qhd->khd", grad_scores, query_heads, preferred_element_type=jnp.float32
            )
            value_term = jnp.einsum(
                "hqk,qhd->khd",
                probs.astype(jnp.bfloat16),
                grad_heads,
                preferred_element_type=jnp.float32,
            )
            pair_term = jnp.concatenate(
                [
                    key_term.reshape(block_keys, model_width),
                    value_term.reshape(block_keys, model_width),
                ],
                axis=1,
            )
            grad_key_values = add_rows(grad_key_values, pair_term, key_offset)
            grad_kernel = grad_kernel + jnp.einsum(
                "qkc,hqk->ch", phi_low, grad_scores, preferred_element_type=jnp.float32
            )
            grad_phi = jnp.einsum(
                "hqk,ch->qkc", grad_scores, kernel_weight, preferred_element_type=jnp.float32
            )
            parts = geometry_back(grad_phi)
            query_atoms_block = query_atoms_block + atom_columns(parts[0], parts[2], parts[4])
            key_atoms = add_rows(key_atoms, atom_columns(parts[1], parts[3], parts[5]), key_offset)
            return (
                grad_query_block,
                grad_key_values,
                query_atoms_block,
                key_atoms,
                grad_kernel,
                grad_centres + parts[6],
                grad_widths + parts[7],
            )

        inner_init = (
            jnp.zeros((block_rows, heads_count, head_size), jnp.float32),
            grad_key_values,
            jnp.zeros((block_rows, 5), jnp.float32),
            key_atoms,
            grad_kernel,
            grad_centres,
            grad_widths,
        )
        result = lax.fori_loop(0, key_steps, back_keys, inner_init)
        grad_query = result[0].reshape(block_rows, model_width)
        query_atoms = result[2]
        return (grad_query, result[1], query_atoms, result[3], result[4], result[5], result[6])

    back_init = (
        jnp.zeros((own_rows, model_width), jnp.float32),
        jnp.zeros((window_rows, 2 * model_width), jnp.float32),
        jnp.zeros((own_rows, 5), jnp.float32),
        jnp.zeros((window_rows, 5), jnp.float32),
        jnp.zeros(kernel_weight.shape, jnp.float32),
        jnp.zeros(kernel_means.shape, jnp.float32),
        jnp.zeros(kernel_widths.shape, jnp.float32),
    )
    grad_query, grad_key_values, query_atoms, key_atoms, grad_kernel, grad_centres, grad_widths = (
        lax.fori_loop(0, own_rows // block_rows, back_rows, back_init)
    )
    value_parts = grad_key_values.reshape(2 * reach + 1, own_rows, 2 * model_width)
    atom_parts = key_atoms.reshape(2 * reach + 1, own_rows, 5)
    key_total = value_parts[reach]
    atom_total = atom_parts[reach]
    for offset in shift_range:
        if offset != 0:
            moved = (
                shifted(
                    value_parts[offset + reach].astype(jnp.bfloat16), ("pb", "ka"), offset
                ).astype(jnp.float32),
                shifted(
                    atom_parts[offset + reach].astype(jnp.bfloat16), ("pb", "ka"), offset
                ).astype(jnp.float32),
            )
            key_total = key_total + moved[0]
            atom_total = atom_total + moved[1]
    grad_projected = jnp.concatenate([grad_query, key_total], axis=1).astype(jnp.bfloat16)
    qkv_grad_weight = jnp.dot(
        normed_first_low.T, grad_projected, preferred_element_type=jnp.float32
    )
    grad_normed_first = jnp.dot(grad_projected, w_qkv.T, preferred_element_type=jnp.float32)
    grad_tokens_norm, grad_gain_first, grad_shift_first = first_back(grad_normed_first)
    grad_tokens = grad_mixed + grad_tokens_norm
    atom_grads = query_atoms + atom_total
    grad_positions = atom_grads[:, :3].T
    own_onehot = query_index[:, None] == table_ids[None, :]
    table_scale_grad = jnp.sum(jnp.where(own_onehot, atom_grads[:, 3:4], 0.0), axis=0)
    table_shift_grad = jnp.sum(jnp.where(own_onehot, atom_grads[:, 4:5], 0.0), axis=0)
    small = lax.psum(
        (
            grad_gain_first,
            grad_shift_first,
            grad_centres,
            grad_widths,
            grad_kernel,
            table_scale_grad,
            table_shift_grad,
            grad_gain_second,
            grad_shift_second,
        ),
        ("pb", "ka"),
    )
    pieces = (
        lax.psum_scatter(
            qkv_grad_weight.astype(jnp.bfloat16), "ka", scatter_dimension=1, tiled=True
        ).astype(jnp.float32),
        lax.psum_scatter(
            out_grad_weight.astype(jnp.bfloat16), "ka", scatter_dimension=1, tiled=True
        ).astype(jnp.float32),
        lax.psum_scatter(
            up_grad_weight.astype(jnp.bfloat16), "ka", scatter_dimension=1, tiled=True
        ).astype(jnp.float32),
        lax.psum_scatter(
            down_columns.astype(jnp.bfloat16), "ka", scatter_dimension=1, tiled=True
        ).astype(jnp.float32),
    )
    totals = (
        lax.psum(pieces[0].astype(jnp.bfloat16), "pb").astype(jnp.float32),
        lax.psum(pieces[1].astype(jnp.bfloat16), "pb").astype(jnp.float32),
        lax.psum(pieces[2].astype(jnp.bfloat16), "pb").astype(jnp.float32),
        lax.psum(pieces[3].astype(jnp.bfloat16), "pb").astype(jnp.float32),
    )
    return (
        block_out,
        grad_tokens,
        grad_positions,
        small[0],
        small[1],
        totals[0],
        small[2],
        small[3],
        small[4],
        small[5],
        small[6],
        totals[1],
        small[7],
        small[8],
        totals[2],
        totals[3].T,
    )


def solution(mesh):
    in_specs = (
        P(("pb", "ka"), None),
        P(),
        P(),
        P(),
        P(),
        P(),
        P(),
        P(),
        P(),
        P(),
        P(),
        P(),
        P(),
        P(),
        P(),
        P(),
        P(),
        P(),
        P(),
        P(("pb", "ka"), None),
    )
    out_specs = (
        P(("pb", "ka"), None),
        P(("pb", "ka"), None),
        P(None, ("pb", "ka")),
        P(),
        P(),
        P(None, "ka"),
        P(),
        P(),
        P(),
        P(),
        P(),
        P(None, "ka"),
        P(),
        P(),
        P(None, "ka"),
        P("ka", None),
    )
    return jax.shard_map(
        on_device, mesh=mesh, in_specs=in_specs, out_specs=out_specs, check_vma=False
    )
```

profile of v0, /device:TPU:0, one launch (start us, length us, event | category | flops | bytes accessed | tf_op | source)
XLA Modules:
  0.0 1876.8 jit_solution(5585691971221333399)
XLA Ops:
  48.6 13.7 gather_fusion.1
  112.9 14.4 collective-permute-done.8
  137.6 268.2 %while.90 = (s32[]{:T(128)}, f32[32,128]{1,0:T(8,128)S(1)}, f32[32,128]{1,0:T(8,128)}, s32[128]{0:T(128)}, s32[1664]{0:T(1024)}, /*index=5*/s32[1664]{0:T(1024)}...) while((s32[]{:T(128)}, f32[32,128]{1,0:T(8,128)S(1)}, ...), condition=%wide.region_10.11_spmd.clone, body=%wide.region_6.10_spmd.clone.sunk | while | flops 175411456 | bytes 13641314 | solution.py:198
  411.7 270.2 %while.91 = (s32[]{:T(128)}, f32[128,32,24]{0,2,1:T(8,128)}, bf16[1664,32,24]{0,2,1:T(8,128)(2,1)}, s32[128]{0:T(128)}, s32[1664]{0:T(1024)}, /*index=5*/s32[166...) while((s32[]{:T(128)}, f32[128,32,24]{0,2,1:T(8,128)}, ...), condition=%wide.region_13.14_spmd.clone, body=%wide.region_11.13_spmd.clone.sunk | while | flops 200229120 | bytes 10169416 | solution.py:211
  705.2 734.2 %while.92 = (s32[]{:T(128)}, f32[128,32,24]{0,2,1:T(8,128)}, f32[1664,1536]{0,1:T(8,128)}, f32[128,5]{0,1:T(8,128)}, f32[1664,5]{0,1:T(8,128)}, /*index=5*/f32[1...) while((s32[]{:T(128)}, f32[128,32,24]{0,2,1:T(8,128)}, ...), condition=%wide.region_31.32_spmd.clone, body=%wide.region_19.31_spmd.clone.sunk | while | flops 611742592 | bytes 76296272 | solution.py:345
  750.3 9.0 fusion.222
  806.7 9.0 fusion.222
  863.2 9.0 fusion.222
  919.6 9.0 fusion.222
  976.1 9.0 fusion.222
  1032.5 9.0 fusion.222
  1089.0 9.0 fusion.222
  1145.4 9.0 fusion.222
  1201.9 9.0 fusion.222
  1447.4 9.2 collective-permute-start.23
  1472.7 30.9 %collective-permute-start.19 = (bf16[128,1536]{0,1:T(8,128)(2,1)}, bf16[128,1536]{0,1:T(8,128)(2,1)S(1)}, u32[]{:S(2)}, u32[]{:S(2)}) collective-permute-start(bf16[128,1536]{0,1:T(8,128)(2,1)} %get-tuple-element.1906), channel_id=1, source_target_pairs={{0,2},{1,3},{2,4},{3,5},{4,6},{5,7},{6,8},{7,9},{8,10},{9,11},{10,... | collective-permute-start | bytes 1179656 | tf_op jit(solution)/shard_map/ppermute | solution.py:21
  1508.9 19.2 %collective-permute-done.19 = bf16[128,1536]{0,1:T(8,128)(2,1)S(1)} collective-permute-done((bf16[128,1536]{0,1:T(8,128)(2,1)}, bf16[128,1536]{0,1:T(8,128)(2,1)S(1)}, u32[]{:S(2)}, u32[]{:S(2)}) %collective-permute-start.19) | collective-permute-done | bytes 393248 | tf_op jit(solution)/shard_map/ppermute | solution.py:21
  1531.7 14.4 collective-permute-done.14
  1567.9 9.6 collective-permute-start.35
  1577.5 27.6 %collective-permute-start.34 = (bf16[128,5]{0,1:T(8,128)(2,1)S(1)}, bf16[128,5]{0,1:T(8,128)(2,1)S(1)}, u32[]{:S(2)}, u32[]{:S(2)}) collective-permute-start(bf16[128,5]{0,1:T(8,128)(2,1)S(1)} %get-tuple-element.1917), channel_id=1, source_target_pairs={{0,5},{1,6},{2,7},{3,8},{4,9},{5,10},{6,11},{7,12},{8,13},{9,14},{... | collective-permute-start | bytes 3848 | tf_op jit(solution)/shard_map/ppermute | solution.py:21
  1639.2 17.3 reduce-scatter.5.cloned.1.call-done
  1656.5 78.4 %reduce-scatter.11.cloned.1.call-done = bf16[768,192]{0,1:T(8,128)(2,1)} async-done(((bf16[768,3072]{0,1:T(8,128)(2,1)}), bf16[768,192]{0,1:T(8,128)(2,1)}) %reduce-scatter.11.cloned.1.call-update) | async-done | bytes 294928 | tf_op jit(solution)/shard_map/reduce_scatter | solution.py:414
  1734.9 78.8 %reduce-scatter.9.cloned.1.call-done = bf16[768,192]{0,1:T(8,128)(2,1)} async-done(((bf16[768,3072]{0,1:T(8,128)(2,1)}), bf16[768,192]{0,1:T(8,128)(2,1)}) %reduce-scatter.9.cloned.1.call-update) | async-done | bytes 294928 | tf_op jit(solution)/shard_map/reduce_scatter | solution.py:411
  1819.1 40.8 %all-reduce.4 = (f32[768]{0:T(1024)}, f32[768]{0:T(1024)}, f32[128]{0:T(128)}, f32[128]{0:T(128)}, f32[128,32]{0,1:T(8,128)}, /*index=5*/f32[160]{0:T(256)}, f32[160]{0:T(256)}, f32[768]{0:T(1024)}, f32[768]{0:T(1024)}) all-reduce(f32[768]{0:T(1024)} %get-tuple-element.1724, ...), channel_id=1, replica_groups=mesh['pb'=2,'ka'=16] {'pb','ka'}, use_global_device_ids=true, to_apply=%region_35.36 | all-reduce | flops 7744 | bytes 61952 | tf_op jit(solution)/shard_map/psum | solution.py:390
  (1915 shorter events, 1419.0 us)
Async XLA Ops:
  7.2 1632.0 %reduce-scatter.7.cloned.1.call-start = ((), (), s32[]{:S(2)}) async-start(), calls=%async_computation.5 | async-start | bytes 1253376 | tf_op jit(solution)/shard_map/reduce_scatter | solution.py:408
  13.4 116.0 %collective-permute-start.11 = (bf16[128,1536]{1,0:T(8,128)(2,1)}, bf16[128,1536]{1,0:T(8,128)(2,1)}, u32[]{:S(2)}, u32[]{:S(2)}) collective-permute-start(bf16[128,1536]{1,0:T(8,128)(2,1)} %slice.186), channel_id=1, source_target_pairs={{6,0},{7,1},{8,2},{9,3},{10,4},{11,5},{12,6},{13,7},{14,8},{15,9},... | collective-permute-start | bytes 1179656 | tf_op jit(solution)/shard_map/ppermute | solution.py:21
  14.7 113.7 %collective-permute-start.10 = (bf16[128,1536]{1,0:T(8,128)(2,1)}, bf16[128,1536]{1,0:T(8,128)(2,1)}, u32[]{:S(2)}, u32[]{:S(2)}) collective-permute-start(bf16[128,1536]{1,0:T(8,128)(2,1)} %slice.186), channel_id=1, source_target_pairs={{5,0},{6,1},{7,2},{8,3},{9,4},{10,5},{11,6},{12,7},{13,8},{14,9},{... | collective-permute-start | bytes 1179656 | tf_op jit(solution)/shard_map/ppermute | solution.py:21
  16.0 111.3 %collective-permute-start.9 = (bf16[128,1536]{1,0:T(8,128)(2,1)}, bf16[128,1536]{1,0:T(8,128)(2,1)}, u32[]{:S(2)}, u32[]{:S(2)}) collective-permute-start(bf16[128,1536]{1,0:T(8,128)(2,1)} %slice.186), channel_id=1, source_target_pairs={{4,0},{5,1},{6,2},{7,3},{8,4},{9,5},{10,6},{11,7},{12,8},{13,9},{1... | collective-permute-start | bytes 1179656 | tf_op jit(solution)/shard_map/ppermute | solution.py:21
  17.3 54.8 %collective-permute-start.1 = (bf16[128,1536]{1,0:T(8,128)(2,1)}, bf16[128,1536]{1,0:T(8,128)(2,1)}, u32[]{:S(2)}, u32[]{:S(2)}) collective-permute-start(bf16[128,1536]{1,0:T(8,128)(2,1)} %slice.186), channel_id=1, source_target_pairs={{0,5},{1,6},{2,7},{3,8},{4,9},{5,10},{6,11},{7,12},{8,13},{9,14},{... | collective-permute-start | bytes 1179656 | tf_op jit(solution)/shard_map/ppermute | solution.py:21
  23.7 43.5 %collective-permute-start = (bf16[128,1536]{1,0:T(8,128)(2,1)}, bf16[128,1536]{1,0:T(8,128)(2,1)}, u32[]{:S(2)}, u32[]{:S(2)}) collective-permute-start(bf16[128,1536]{1,0:T(8,128)(2,1)} %slice.186), channel_id=1, source_target_pairs={{0,6},{1,7},{2,8},{3,9},{4,10},{5,11},{6,12},{7,13},{8,14},{9,15},... | collective-permute-start | bytes 1179656 | tf_op jit(solution)/shard_map/ppermute | solution.py:21
  104.2 23.1 %collective-permute-start.8 = (bf16[128,1536]{1,0:T(8,128)(2,1)}, bf16[128,1536]{1,0:T(8,128)(2,1)S(1)}, u32[]{:S(2)}, u32[]{:S(2)}) collective-permute-start(bf16[128,1536]{1,0:T(8,128)(2,1)} %slice.186), channel_id=1, source_target_pairs={{3,0},{4,1},{5,2},{6,3},{7,4},{8,5},{9,6},{10,7},{11,8},{12,9},{13... | collective-permute-start | bytes 1179656 | tf_op jit(solution)/shard_map/ppermute | solution.py:21
  1446.1 26.6 %collective-permute-start.12 = (bf16[128,1536]{0,1:T(8,128)(2,1)}, bf16[128,1536]{0,1:T(8,128)(2,1)}, u32[]{:S(2)}, u32[]{:S(2)}) collective-permute-start(bf16[128,1536]{0,1:T(8,128)(2,1)} %get-tuple-element.1901), channel_id=1, source_target_pairs={{6,0},{7,1},{8,2},{9,3},{10,4},{11,5},{12,6},{13,7},{14,8},{15,9},... | collective-permute-start | bytes 1179656 | tf_op jit(solution)/shard_map/ppermute | solution.py:21
  1447.4 56.2 %collective-permute-start.23 = (bf16[128,1536]{0,1:T(8,128)(2,1)}, bf16[128,1536]{0,1:T(8,128)(2,1)}, u32[]{:S(2)}, u32[]{:S(2)}) collective-permute-start(bf16[128,1536]{0,1:T(8,128)(2,1)} %get-tuple-element.1902), channel_id=1, source_target_pairs={{0,6},{1,7},{2,8},{3,9},{4,10},{5,11},{6,12},{7,13},{8,14},{9,15},... | collective-permute-start | bytes 1179656 | tf_op jit(solution)/shard_map/ppermute | solution.py:21
  1458.2 198.3 %reduce-scatter.5.cloned.1.call-start = ((), (), s32[]{:S(2)}) async-start(), calls=%async_computation.4 | async-start | bytes 3760128 | tf_op jit(solution)/shard_map/reduce_scatter | solution.py:405
  1458.3 46.7 %collective-permute-start.22 = (bf16[128,1536]{0,1:T(8,128)(2,1)}, bf16[128,1536]{0,1:T(8,128)(2,1)S(1)}, u32[]{:S(2)}, u32[]{:S(2)}) collective-permute-start(bf16[128,1536]{0,1:T(8,128)(2,1)} %get-tuple-element.1903), channel_id=1, source_target_pairs={{0,5},{1,6},{2,7},{3,8},{4,9},{5,10},{6,11},{7,12},{8,13},{9,14},{... | collective-permute-start | bytes 1179656 | tf_op jit(solution)/shard_map/ppermute | solution.py:21
  1462.1 44.2 %collective-permute-start.21 = (bf16[128,1536]{0,1:T(8,128)(2,1)}, bf16[128,1536]{0,1:T(8,128)(2,1)S(1)}, u32[]{:S(2)}, u32[]{:S(2)}) collective-permute-start(bf16[128,1536]{0,1:T(8,128)(2,1)} %get-tuple-element.1904), channel_id=1, source_target_pairs={{0,4},{1,5},{2,6},{3,7},{4,8},{5,9},{6,10},{7,11},{8,12},{9,13},{1... | collective-permute-start | bytes 1179656 | tf_op jit(solution)/shard_map/ppermute | solution.py:21
  1468.2 39.4 %collective-permute-start.20 = (bf16[128,1536]{0,1:T(8,128)(2,1)}, bf16[128,1536]{0,1:T(8,128)(2,1)S(1)}, u32[]{:S(2)}, u32[]{:S(2)}) collective-permute-start(bf16[128,1536]{0,1:T(8,128)(2,1)} %get-tuple-element.1905), channel_id=1, source_target_pairs={{0,3},{1,4},{2,5},{3,6},{4,7},{5,8},{6,9},{7,10},{8,11},{9,12},{10... | collective-permute-start | bytes 1179656 | tf_op jit(solution)/shard_map/ppermute | solution.py:21
  1472.7 55.3 %collective-permute-start.19 = (bf16[128,1536]{0,1:T(8,128)(2,1)}, bf16[128,1536]{0,1:T(8,128)(2,1)S(1)}, u32[]{:S(2)}, u32[]{:S(2)}) collective-permute-start(bf16[128,1536]{0,1:T(8,128)(2,1)} %get-tuple-element.1906), channel_id=1, source_target_pairs={{0,2},{1,3},{2,4},{3,5},{4,6},{5,7},{6,8},{7,9},{8,10},{9,11},{10,... | collective-permute-start | bytes 1179656 | tf_op jit(solution)/shard_map/ppermute | solution.py:21
  1503.7 25.7 %collective-permute-start.18 = (bf16[128,1536]{0,1:T(8,128)(2,1)}, bf16[128,1536]{0,1:T(8,128)(2,1)S(1)}, u32[]{:S(2)}, u32[]{:S(2)}) collective-permute-start(bf16[128,1536]{0,1:T(8,128)(2,1)} %get-tuple-element.1907), channel_id=1, source_target_pairs={{0,1},{1,2},{2,3},{3,4},{4,5},{5,6},{6,7},{7,8},{8,9},{9,10},{10,1... | collective-permute-start | bytes 1179656 | tf_op jit(solution)/shard_map/ppermute | solution.py:21
  1505.0 26.7 %collective-permute-start.17 = (bf16[128,1536]{0,1:T(8,128)(2,1)}, bf16[128,1536]{0,1:T(8,128)(2,1)S(1)}, u32[]{:S(2)}, u32[]{:S(2)}) collective-permute-start(bf16[128,1536]{0,1:T(8,128)(2,1)} %get-tuple-element.1908), channel_id=1, source_target_pairs={{1,0},{2,1},{3,2},{4,3},{5,4},{6,5},{7,6},{8,7},{9,8},{10,9},{11,1... | collective-permute-start | bytes 1179656 | tf_op jit(solution)/shard_map/ppermute | solution.py:21
  1506.3 25.4 %collective-permute-start.16 = (bf16[128,1536]{0,1:T(8,128)(2,1)}, bf16[128,1536]{0,1:T(8,128)(2,1)S(1)}, u32[]{:S(2)}, u32[]{:S(2)}) collective-permute-start(bf16[128,1536]{0,1:T(8,128)(2,1)} %get-tuple-element.1909), channel_id=1, source_target_pairs={{2,0},{3,1},{4,2},{5,3},{6,4},{7,5},{8,6},{9,7},{10,8},{11,9},{12,... | collective-permute-start | bytes 1179656 | tf_op jit(solution)/shard_map/ppermute | solution.py:21
  1507.6 24.1 %collective-permute-start.15 = (bf16[128,1536]{0,1:T(8,128)(2,1)}, bf16[128,1536]{0,1:T(8,128)(2,1)S(1)}, u32[]{:S(2)}, u32[]{:S(2)}) collective-permute-start(bf16[128,1536]{0,1:T(8,128)(2,1)} %get-tuple-element.1910), channel_id=1, source_target_pairs={{3,0},{4,1},{5,2},{6,3},{7,4},{8,5},{9,6},{10,7},{11,8},{12,9},{13... | collective-permute-start | bytes 1179656 | tf_op jit(solution)/shard_map/ppermute | solution.py:21
  1554.8 180.1 %reduce-scatter.11.cloned.1.call-start = ((), (), s32[]{:S(2)}) async-start(), calls=%async_computation.7 | async-start | bytes 5013504 | tf_op jit(solution)/shard_map/reduce_scatter | solution.py:414
  1560.1 253.6 %reduce-scatter.9.cloned.1.call-start = ((), (), s32[]{:S(2)}) async-start(), calls=%async_computation.6 | async-start | bytes 5013504 | tf_op jit(solution)/shard_map/reduce_scatter | solution.py:411
  1565.7 297.2 %all-reduce.8.cloned.1.call-start = ((), (), s32[]{:S(2)}) async-start(), calls=%async_computation.8 | async-start | bytes 1769472 | tf_op jit(solution)/shard_map/psum | solution.py:419
  1566.6 47.5 %collective-permute-start.24 = (bf16[128,5]{0,1:T(8,128)(2,1)S(1)}, bf16[128,5]{0,1:T(8,128)(2,1)S(1)}, u32[]{:S(2)}, u32[]{:S(2)}) collective-permute-start(bf16[128,5]{0,1:T(8,128)(2,1)S(1)} %get-tuple-element.1915), channel_id=1, source_target_pairs={{6,0},{7,1},{8,2},{9,3},{10,4},{11,5},{12,6},{13,7},{14,8},{15,9},... | collective-permute-start | bytes 3848 | tf_op jit(solution)/shard_map/ppermute | solution.py:21
  1567.9 50.2 %collective-permute-start.35 = (bf16[128,5]{0,1:T(8,128)(2,1)S(1)}, bf16[128,5]{0,1:T(8,128)(2,1)S(1)}, u32[]{:S(2)}, u32[]{:S(2)}) collective-permute-start(bf16[128,5]{0,1:T(8,128)(2,1)S(1)} %get-tuple-element.1916), channel_id=1, source_target_pairs={{0,6},{1,7},{2,8},{3,9},{4,10},{5,11},{6,12},{7,13},{8,14},{9,15},... | collective-permute-start | bytes 3848 | tf_op jit(solution)/shard_map/ppermute | solution.py:21
  1577.5 45.9 %collective-permute-start.34 = (bf16[128,5]{0,1:T(8,128)(2,1)S(1)}, bf16[128,5]{0,1:T(8,128)(2,1)S(1)}, u32[]{:S(2)}, u32[]{:S(2)}) collective-permute-start(bf16[128,5]{0,1:T(8,128)(2,1)S(1)} %get-tuple-element.1917), channel_id=1, source_target_pairs={{0,5},{1,6},{2,7},{3,8},{4,9},{5,10},{6,11},{7,12},{8,13},{9,14},{... | collective-permute-start | bytes 3848 | tf_op jit(solution)/shard_map/ppermute | solution.py:21
  (519 other events, 4106.3 us)
Sparse Core Ops, SparseCore 0:
  1458.3 91.6 reduce-scatter.6
  1554.9 101.5 reduce-scatter.4
  1660.3 74.5 reduce-scatter.10
  1739.1 74.5 reduce-scatter.8
  1816.1 36.8 all-reduce.7
where the time goes:
time: 1900 us; the launch traced here: 1880 us
  matrix products  630 us (33%)
  other arithmetic  386 us (20%)
  local copies, waits for them, and re-layouts  383 us (20%)
  waiting for transfers between devices  248 us (13%)
  starting transfers between devices  166 us (9%)
  blocking collectives  40.8 us (2%)
    dot_general x39, matrix products, scores_from(): jnp.einsum('qkc,ch->hqk', phi_low, kernel_weight, preferred_element_type=...  238 us
    ppermute x36, starting transfers between devices, shifted(): return lax.ppermute(block, axis, route)  166 us
    dynamic_slice x195, local copies, waits for them, and re-layouts, side_block(): lax.dynamic_slice_in_dim(member, offset, extent, member.ndim - 1)  143 us
    reduce_sum x13, other arithmetic, pair_geometry(): normed = (stretched[:, :, None] - centres) / widths  117 us
    dot_general x39, local copies, waits for them, and re-layouts, scores_from(): jnp.einsum('qkc,ch->hqk', phi_low, kernel_weight, preferred_element_type=...  116 us
    dot_general x13, matrix products, back_keys(): jnp.einsum('qkc,hqk->ch', phi_low, grad_scores, preferred_element_type=jn...  81.5 us
    reduce_scatter x1, waiting for transfers between devices, on_device(): lax.psum_scatter(up_grad_weight.astype(jnp.bfloat16), 'ka', scatter_dimen...  78.8 us
    reduce_scatter x1, waiting for transfers between devices, on_device(): lax.psum_scatter(down_columns.astype(jnp.bfloat16), 'ka', scatter_dimensi...  78.4 us
  transfers between devices with their start and end apart: 41, of which 12 were waited for; matrix products, arithmetic and copies ran while one was open for 4% of the time, Pallas kernels for 0%

commit v1 on v0

v1 whole, which is shorter than its diff:
```python
import functools
import math

import jax
import jax.numpy as jnp
from jax import lax
from jax.experimental import pallas as pl
from jax.experimental.pallas import tpu as pltpu
from jax.sharding import PartitionSpec as P

MOL_TYPES = 128
PROT_LEN = 768
MOL_MEAN = 32

LN_EPS = 1e-05
MASKED = -1e30
ROOT_TWO_PI = math.sqrt(2.0 * math.pi)
LOG2E = math.log2(math.e)
KAPPA = math.sqrt(0.5 * LOG2E)

PAD = 32
GROUP = 8
SPAN = PAD * GROUP
PIECES = 3
CHUNK = 32
MESH = ("pb", "ka")

BF = jnp.bfloat16
F32 = jnp.float32


def shifted(block, axis, distance):
    devices = range(lax.axis_size(axis))
    route = [(i - distance, i) for i in devices if i - distance in devices]
    return lax.ppermute(block, axis, route)


def core_flip(block):
    devices = range(lax.axis_size(MESH))
    return lax.ppermute(block, MESH, [(i, i ^ 1) for i in devices])


def window_of(block, chips):
    pieces = [
        block if step == 0 else shifted(block, MESH, -2 * step) for step in range(-chips, chips + 1)
    ]
    mine = jnp.stack(pieces, axis=0)
    return mine, core_flip(mine)


def layer_norm(values, ln_gain, ln_shift):
    centre = jnp.mean(values, axis=-1, keepdims=True)
    offsets = values - centre
    spread = jnp.mean(offsets * offsets, axis=-1, keepdims=True)
    return offsets * lax.rsqrt(spread + LN_EPS) * ln_gain + ln_shift


def dot_nn(left, right):
    return lax.dot_general(left, right, (((1,), (0,)), ((), ())), preferred_element_type=F32)


def dot_nt(left, right):
    return lax.dot_general(left, right, (((1,), (1,)), ((), ())), preferred_element_type=F32)


def stretched_of(own, other):
    delta = [own[:, i : i + 1] - other[i : i + 1, :] for i in range(3)]
    square = delta[0] * delta[0] + delta[1] * delta[1] + delta[2] * delta[2]
    dist = jnp.sqrt(square + 1.0)
    scales = own[:, 3:4] * other[3:4, :]
    stretched = scales * dist + own[:, 4:5] + other[4:5, :]
    return delta, dist, scales, stretched


def mask_of(own, other, key_is_own):
    same = own[:, 5:6] == other[5:6, :]
    itself = own[:, 7:8] == other[7:8, :]
    is_open = (own[:, 6:7] > 0.5) if key_is_own else (other[6:7, :] > 0.5)
    return jnp.where(same & (is_open | itself), 0.0, MASKED)


def head_mask():
    head = lax.broadcasted_iota(jnp.int32, (GROUP, SPAN), 0)
    column = lax.broadcasted_iota(jnp.int32, (GROUP, SPAN), 1)
    return jnp.where(column // PAD == head, 1.0, 0.0)


def expand_into(out_ref, padded, groups):
    rows = padded.shape[0]
    keep = head_mask()
    for g in range(groups):
        part = padded[:, g * SPAN : (g + 1) * SPAN].astype(F32)
        wide = jnp.broadcast_to(part[:, None, :], (rows, GROUP, SPAN)) * keep[None]
        out_ref[g] = wide.reshape(rows * GROUP, SPAN).astype(BF)


def collapse(values):
    rows = values.shape[0] // GROUP
    return jnp.sum(values.reshape(rows, GROUP, SPAN) * head_mask()[None], axis=1)


def spread_mask(mask_ref, mask):
    mask_ref[...] = jnp.broadcast_to(mask[:, None, :], mask_ref.shape)


def bias_kernel(span_ref, own_ref, other_ref, tab_ref, kwt_ref, out_ref, str_ref):
    rows, keys = str_ref.shape
    kernels = tab_ref.shape[1]
    str_ref[...] = stretched_of(own_ref[...], other_ref[...])[3]

    def step(i, carry):
        block = str_ref[pl.ds(i * 8, 8), :]
        for r in range(8):
            parts = []
            for half in range(keys // 128):
                line = jnp.broadcast_to(
                    block[r : r + 1, half * 128 : (half + 1) * 128], (kernels, 128)
                )
                z = (line - tab_ref[0]) * tab_ref[1]
                parts.append(jnp.exp2(tab_ref[2] - z * z).astype(BF))
            phi = jnp.concatenate(parts, axis=1)
            out_ref[0, i * 8 + r] = dot_nn(kwt_ref[...], phi) * LOG2E
        return carry

    lax.fori_loop(0, rows // 8, step, 0)


def forward_kernel(
    scale2,
    groups,
    span_ref,
    own_ref,
    other_ref,
    mine_ref,
    sib_ref,
    tok_ref,
    ln_ref,
    w_ref,
    ones_ref,
    place_ref,
    bias_ref,
    att_ref,
    qaug_ref,
    lse_ref,
    now_ref,
    kvq_ref,
    qexp_ref,
    mask_ref,
    max_ref,
    sum_ref,
    acc_ref,
    lane_ref,
):
    step = pl.program_id(0)
    width = groups * SPAN
    rows = tok_ref.shape[0]
    gain, shift = ln_ref[0:1, :], ln_ref[1:2, :]

    @pl.when(step == 0)
    def _():
        normed = layer_norm(tok_ref[...].astype(F32), gain, shift).astype(BF)
        now_ref[...] = normed
        query = dot_nn(normed, w_ref[:, 2 * width :]).astype(BF)
        qaug_ref[...] = query
        expand_into(qexp_ref, query, groups)
        max_ref[...] = jnp.full(max_ref.shape, 2.0 * MASKED, F32)
        sum_ref[...] = jnp.zeros(sum_ref.shape, F32)
        acc_ref[...] = jnp.zeros(acc_ref.shape, F32)

    tokens = jnp.concatenate([mine_ref[0], sib_ref[0]], axis=0).astype(F32)
    normed = layer_norm(tokens, gain, shift).astype(BF)
    for part in range(3):
        value = dot_nn(normed, w_ref[:, part * width : (part + 1) * width])
        if part < 2:
            value = value + ones_ref[...]
        kvq_ref[0, :, part * width : (part + 1) * width] = value.astype(BF)
    spread_mask(mask_ref, mask_of(own_ref[...], other_ref[...], False))

    def chunk_step(i, carry):
        at = pl.multiple_of(i * CHUNK, CHUNK)
        lines = pl.ds(pl.multiple_of(i * CHUNK * GROUP, CHUNK * GROUP), CHUNK * GROUP)
        mask = mask_ref[pl.ds(at, CHUNK)]
        for g in range(groups):
            columns = slice(g * SPAN, (g + 1) * SPAN)
            dots = dot_nt(qexp_ref[g, lines, :], kvq_ref[0, :, columns])
            bias = bias_ref[0, pl.ds(at, CHUNK), g * GROUP : (g + 1) * GROUP, :] + mask
            scores = dots * scale2 + bias.reshape(dots.shape)
            old = max_ref[g, lines, :]
            top = jnp.maximum(scores[:, :128], scores[:, 128:])
            new = jnp.maximum(old, jnp.max(top, axis=1, keepdims=True))
            alpha = jnp.exp2(old - new)
            low = jnp.exp2(scores[:, :128] - new)
            high = jnp.exp2(scores[:, 128:] - new)
            max_ref[g, lines, :] = new
            sum_ref[g, lines, :] = sum_ref[g, lines, :] * alpha + (low + high)
            probs = jnp.concatenate([low, high], axis=1).astype(BF)
            values = dot_nn(probs, kvq_ref[0, :, width + g * SPAN : width + (g + 1) * SPAN])
            wide = jnp.concatenate([alpha, alpha], axis=1)
            acc_ref[g, lines, :] = acc_ref[g, lines, :] * wide + values
        return carry

    lax.fori_loop(0, rows // CHUNK, chunk_step, 0)

    @pl.when(step == span_ref[1] - span_ref[0])
    def _():
        lane = lax.broadcasted_iota(jnp.int32, (GROUP, 128), 1)
        head = lax.broadcasted_iota(jnp.int32, (GROUP, 128), 0)

        def finish(i, carry):
            at = pl.multiple_of(i * CHUNK, CHUNK)
            lines = pl.ds(pl.multiple_of(i * CHUNK * GROUP, CHUNK * GROUP), CHUNK * GROUP)
            lanes = jnp.zeros((CHUNK, 128), F32)
            for g in range(groups):
                total = jnp.sum(sum_ref[g, lines, :], axis=1, keepdims=True)
                attended = collapse(acc_ref[g, lines, :] / total)
                att_ref[pl.ds(at, CHUNK), g * SPAN : (g + 1) * SPAN] = attended
                lse = max_ref[g, lines, :] + jnp.log(total) * LOG2E
                own_lane = jnp.where(lane == head + g * GROUP, 1.0, 0.0)
                lanes = lanes + jnp.sum(
                    lse.reshape(CHUNK, GROUP, 128) * own_lane[None], axis=1
                )
            lane_ref[pl.ds(at, CHUNK), :] = lanes
            return carry

        lax.fori_loop(0, rows // CHUNK, finish, 0)
        rest = lane_ref[...] * (-1.0 / scale2)
        query = qaug_ref[...].astype(F32)
        for p in range(PIECES):
            piece = rest.astype(BF)
            rest = rest - piece.astype(F32)
            lse_ref[p] = piece
            query = query + dot_nn(piece, place_ref[p])
        qaug_ref[...] = query.astype(BF)


def query_grad_kernel(
    scale2,
    head_scale,
    groups,
    span_ref,
    own_ref,
    other_ref,
    qaug_ref,
    doaug_ref,
    kv_ref,
    bias_ref,
    tab_ref,
    kw_ref,
    dq_ref,
    gkw_ref,
    moment_ref,
    atom_ref,
    key_ref,
    qexp_ref,
    doexp_ref,
    mask_ref,
    str_ref,
    ds_ref,
    dqacc_ref,
    dphi_ref,
    phi_ref,
    gs_ref,
    own_acc_ref,
):
    step = pl.program_id(0)
    width = groups * SPAN
    rows, keys = str_ref.shape
    kernels = tab_ref.shape[1]

    @pl.when(step == 0)
    def _():
        expand_into(qexp_ref, qaug_ref[...], groups)
        expand_into(doexp_ref, doaug_ref[...], groups)
        dqacc_ref[...] = jnp.zeros(dqacc_ref.shape, F32)
        gkw_ref[...] = jnp.zeros(gkw_ref.shape, F32)
        moment_ref[...] = jnp.zeros(moment_ref.shape, F32)
        own_acc_ref[...] = jnp.zeros(own_acc_ref.shape, F32)

    own, other = own_ref[...], other_ref[...]
    str_ref[...] = stretched_of(own, other)[3]
    spread_mask(mask_ref, mask_of(own, other, False))

    def chunk_step(i, carry):
        at = pl.multiple_of(i * CHUNK, CHUNK)
        lines = pl.ds(pl.multiple_of(i * CHUNK * GROUP, CHUNK * GROUP), CHUNK * GROUP)
        mask = mask_ref[pl.ds(at, CHUNK)]
        for g in range(groups):
            key_block = kv_ref[0, :, g * SPAN : (g + 1) * SPAN]
            value_block = kv_ref[0, :, width + g * SPAN : width + (g + 1) * SPAN]
            dots = dot_nt(qexp_ref[g, lines, :], key_block)
            grads = dot_nt(doexp_ref[g, lines, :], value_block)
            bias = bias_ref[0, pl.ds(at, CHUNK), g * GROUP : (g + 1) * GROUP, :] + mask
            probs = jnp.exp2(dots * scale2 + bias.reshape(dots.shape))
            grad_scores = probs * grads
            ds_ref[pl.ds(at, CHUNK), g * GROUP : (g + 1) * GROUP, :] = grad_scores.reshape(
                CHUNK, GROUP, keys
            )
            dqacc_ref[g, lines, :] += dot_nn(grad_scores.astype(BF), key_block)
        return carry

    lax.fori_loop(0, rows // CHUNK, chunk_step, 0)

    tile = 32

    def pair_step(i, carry):
        block = str_ref[pl.ds(pl.multiple_of(i * 8, 8), 8), :]
        lows = []
        for r in range(8):
            low = ds_ref[i * 8 + r].astype(BF)
            lows.append(low)
            dphi_ref[:, r * keys : (r + 1) * keys] = dot_nn(kw_ref[...], low)
        halves = keys // 128
        partial = [[None] * halves for _ in range(8)]
        for c in range(kernels // tile):
            cs = slice(c * tile, (c + 1) * tile)
            first = jnp.zeros((tile, 128), F32)
            second = jnp.zeros((tile, 128), F32)
            for r in range(8):
                for half in range(halves):
                    line = jnp.broadcast_to(
                        block[r : r + 1, half * 128 : (half + 1) * 128], (tile, 128)
                    )
                    columns = slice(r * keys + half * 128, r * keys + (half + 1) * 128)
                    z = (line - tab_ref[0, cs, :]) * tab_ref[1, cs, :]
                    phi = jnp.exp2(tab_ref[2, cs, :] - z * z)
                    phi_ref[cs, columns] = phi.astype(BF)
                    ez = dphi_ref[cs, columns] * phi * z
                    first = first + ez
                    second = second + ez * z
                    term = jnp.sum((ez * tab_ref[3, cs, :]).reshape(tile // 8, 8, 128), axis=0)
                    partial[r][half] = term if c == 0 else partial[r][half] + term
            moment_ref[0, cs, :] += first
            moment_ref[1, cs, :] += second
        lines = [
            jnp.concatenate(
                [jnp.sum(partial[r][half], axis=0, keepdims=True) for half in range(halves)], axis=1
            )
            for r in range(8)
        ]
        gs_ref[pl.ds(pl.multiple_of(i * 8, 8), 8), :] = jnp.concatenate(lines, axis=0)
        gkw_ref[...] += dot_nt(phi_ref[...], jnp.concatenate(lows, axis=1))
        return carry

    lax.fori_loop(0, rows // 8, pair_step, 0)

    delta, dist, scales, _ = stretched_of(own, other)
    grad = -gs_ref[...]
    by_scale = grad * dist
    pull = grad * scales / dist
    terms = [pull * delta[0], pull * delta[1], pull * delta[2], by_scale * other[3:4, :], grad]
    for k, term in enumerate(terms):
        own_acc_ref[k] += term[:, :128] + term[:, 128:]
    lines = [-jnp.sum(terms[k], axis=0, keepdims=True) for k in range(3)]
    lines.append(jnp.sum(by_scale * own[:, 3:4], axis=0, keepdims=True))
    lines.append(jnp.sum(grad, axis=0, keepdims=True))
    lines.append(jnp.zeros((3, keys), F32))
    key_ref[...] = jnp.concatenate(lines, axis=0)

    @pl.when(step == span_ref[1] - span_ref[0])
    def _():
        lane = lax.broadcasted_iota(jnp.int32, (rows, 128), 1)
        total = jnp.zeros((rows, 128), F32)
        for k in range(5):
            column = jnp.sum(own_acc_ref[k], axis=1, keepdims=True)
            total = total + jnp.where(lane == k, column, 0.0)
        atom_ref[...] = total

        def finish(i, carry):
            at = pl.multiple_of(i * CHUNK, CHUNK)
            lines = pl.ds(pl.multiple_of(i * CHUNK * GROUP, CHUNK * GROUP), CHUNK * GROUP)
            for g in range(groups):
                value = collapse(dqacc_ref[g, lines, :]) * head_scale
                dq_ref[pl.ds(at, CHUNK), g * SPAN : (g + 1) * SPAN] = value.astype(BF)
            return carry

        lax.fori_loop(0, rows // CHUNK, finish, 0)


def key_grad_kernel(
    scale2,
    head_scale,
    groups,
    model_width,
    span_ref,
    own_ref,
    other_ref,
    kv_ref,
    q_ref,
    mine_ref,
    sib_ref,
    wout_ref,
    place_ref,
    bias_ref,
    dkv_ref,
    kexp_ref,
    vexp_ref,
    mask_ref,
    qb_ref,
    dob_ref,
    dk_ref,
    dv_ref,
):
    step = pl.program_id(0)
    width = groups * SPAN
    rows = own_ref.shape[0]

    @pl.when(step == 0)
    def _():
        expand_into(kexp_ref, kv_ref[0, :, :width], groups)
        expand_into(vexp_ref, kv_ref[0, :, width:], groups)
        dk_ref[...] = jnp.zeros(dk_ref.shape, F32)
        dv_ref[...] = jnp.zeros(dv_ref.shape, F32)

    payload = jnp.concatenate([mine_ref[0], sib_ref[0]], axis=0)
    tail = payload[:, model_width:]
    grads = dot_nt(payload[:, :model_width], wout_ref[...]).astype(BF).astype(F32)
    dob_ref[...] = (grads + dot_nn(tail, place_ref[1])).astype(BF)
    qb_ref[...] = (q_ref[0].astype(F32) + dot_nn(tail, place_ref[0])).astype(BF)
    spread_mask(mask_ref, mask_of(own_ref[...], other_ref[...], True))

    def chunk_step(i, carry):
        at = pl.multiple_of(i * CHUNK, CHUNK)
        lines = pl.ds(pl.multiple_of(i * CHUNK * GROUP, CHUNK * GROUP), CHUNK * GROUP)
        mask = mask_ref[pl.ds(at, CHUNK)]
        for g in range(groups):
            query_block = qb_ref[:, g * SPAN : (g + 1) * SPAN]
            grad_block = dob_ref[:, g * SPAN : (g + 1) * SPAN]
            dots = dot_nt(kexp_ref[g, lines, :], query_block)
            grads = dot_nt(vexp_ref[g, lines, :], grad_block)
            bias = bias_ref[0, pl.ds(at, CHUNK), g * GROUP : (g + 1) * GROUP, :] + mask
            probs = jnp.exp2(dots * scale2 + bias.reshape(dots.shape))
            grad_scores = (probs * grads).astype(BF)
            dk_ref[g, lines, :] += dot_nn(grad_scores, query_block)
            dv_ref[g, lines, :] += dot_nn(probs.astype(BF), grad_block)
        return carry

    lax.fori_loop(0, rows // CHUNK, chunk_step, 0)

    @pl.when(step == span_ref[1] - span_ref[0])
    def _():
        def finish(i, carry):
            at = pl.multiple_of(i * CHUNK, CHUNK)
            lines = pl.ds(pl.multiple_of(i * CHUNK * GROUP, CHUNK * GROUP), CHUNK * GROUP)
            for g in range(groups):
                key = collapse(dk_ref[g, lines, :]) * head_scale
                value = collapse(dv_ref[g, lines, :])
                dkv_ref[pl.ds(at, CHUNK), g * SPAN : (g + 1) * SPAN] = key.astype(BF)
                dkv_ref[pl.ds(at, CHUNK), width + g * SPAN : width + (g + 1) * SPAN] = (
                    value.astype(BF)
                )
            return carry

        lax.fori_loop(0, rows // CHUNK, finish, 0)


def fixed(shape, *index):
    at = index or (0,) * len(shape)
    return pl.BlockSpec(shape, lambda j, span: at, pipeline_mode=pl.Buffered(1))


def moving(shape, rank_at=0, last=0):
    def index(j, span):
        at = [0] * len(shape)
        at[rank_at] = jnp.minimum(span[0] + j, span[1])
        if last:
            at[-1] = last
        return tuple(at)

    return pl.BlockSpec(shape, index)


def while_inside(kernel):
    def body(span_ref, *refs):
        @pl.when(pl.program_id(0) <= span_ref[1] - span_ref[0])
        def _():
            kernel(span_ref, *refs)

    return body


def call(kernel, steps, in_specs, out_specs, out_shapes, scratch, flops, name):
    return pl.pallas_call(
        while_inside(kernel),
        grid_spec=pltpu.PrefetchScalarGridSpec(
            num_scalar_prefetch=1,
            grid=(steps,),
            in_specs=in_specs,
            out_specs=out_specs,
            scratch_shapes=scratch,
        ),
        out_shape=out_shapes,
        compiler_params=pltpu.CompilerParams(
            dimension_semantics=("arbitrary",), vmem_limit_bytes=60 * 1024 * 1024
        ),
        cost_estimate=pl.CostEstimate(flops=flops, bytes_accessed=20_000_000, transcendentals=0),
        name=name,
    )


def shape_of(shape, dtype=F32):
    return jax.ShapeDtypeStruct(shape, dtype)


def pad_heads(values, heads, size):
    rows = values.shape[0]
    wide = jnp.pad(values.reshape(rows, heads, size), ((0, 0), (0, 0), (0, PAD - size)))
    return wide.reshape(rows, heads * PAD)


def drop_pad(values, heads, size):
    rows = values.shape[0]
    return values.reshape(rows, heads, PAD)[:, :, :size].reshape(rows, heads * size)


def pieces_of(values):
    rest, out = values, []
    for _ in range(PIECES):
        piece = rest.astype(BF)
        rest = rest - piece.astype(F32)
        out.append(piece)
    return out


def on_device(
    tokens,
    positions,
    item_of_atom,
    item_lengths,
    atom_types,
    key_mask,
    ln1_gain,
    ln1_bias,
    w_qkv,
    kernel_means,
    kernel_widths,
    kernel_weight,
    type_scale,
    type_shift,
    w_out,
    ln2_gain,
    ln2_bias,
    w_up,
    w_down,
    out_cotangent,
):
    own_rows, model_width = tokens.shape
    kernels, heads = kernel_weight.shape
    head_size = model_width // heads
    head_scale = head_size ** (-0.5)
    scale2 = head_scale * LOG2E
    groups = heads // GROUP
    width = groups * SPAN
    ka_count = lax.axis_size("ka")
    flat = lax.axis_index("pb") * ka_count + lax.axis_index("ka")
    core = flat % 2
    reach = (PROT_LEN + own_rows - 2) // own_rows
    chips = (reach + 1) // 2
    pairs = 2 * chips + 1
    keys = 2 * own_rows
    atoms = positions.shape[1]
    chip_start = (flat // 2) * keys
    margin = chips * keys

    table = jnp.concatenate(
        [
            positions,
            item_of_atom.astype(F32)[None],
            key_mask.astype(F32)[None],
            jnp.arange(atoms, dtype=jnp.int32).astype(F32)[None],
            atom_types.astype(F32)[None],
        ],
        axis=0,
    )
    table = jnp.pad(table, ((0, 0), (margin, margin)), constant_values=-1.0)
    table = lax.dynamic_slice_in_dim(table, chip_start, pairs * keys, 1)
    table = table.reshape(table.shape[0], pairs, 2, own_rows)
    table = jnp.where(core == 0, table, table[:, :, ::-1, :]).reshape(-1, pairs * keys)
    item_row = table[3]
    item_ids = jnp.arange(item_lengths.shape[0], dtype=F32)
    flags = jnp.where(item_lengths > 2 * MOL_MEAN, float(MOL_TYPES), 0.0)
    protein = jnp.sum(
        jnp.where(item_row[None, :] == item_ids[:, None], flags[:, None], 0.0), axis=0
    )
    table_row = table[6] + protein
    onehot = table_row[None, :] == jnp.arange(type_scale.shape[0], dtype=F32)[:, None]
    scale_row = jnp.sum(jnp.where(onehot, type_scale[:, None], 0.0), axis=0)
    shift_row = jnp.sum(jnp.where(onehot, type_shift[:, None], 0.0), axis=0)
    other = jnp.stack(
        [table[0], table[1], table[2], scale_row, shift_row, item_row, table[4], table[5]], axis=0
    )
    own = other[:, margin : margin + own_rows].T
    first_item = item_row[margin].astype(jnp.int32)
    last_item = item_row[margin + own_rows - 1].astype(jnp.int32)
    low_atom = jnp.sum((item_of_atom < first_item).astype(jnp.int32))
    high_atom = jnp.sum((item_of_atom <= last_item).astype(jnp.int32))
    first_pair = (low_atom - chip_start + margin) // keys
    last_pair = (high_atom - 1 - chip_start + margin) // keys
    span = jnp.stack([first_pair, last_pair]).astype(jnp.int32)

    lanes = (kernels, 128)
    tabs = jnp.stack(
        [
            jnp.broadcast_to(kernel_means[:, None], lanes),
            jnp.broadcast_to((KAPPA / kernel_widths)[:, None], lanes),
            jnp.broadcast_to((-LOG2E * jnp.log(ROOT_TWO_PI * kernel_widths))[:, None], lanes),
            jnp.broadcast_to((1.0 / (KAPPA * kernel_widths))[:, None], lanes),
        ]
    )
    column = jnp.arange(width)
    ones_row = ((column % PAD >= head_size) & (column % PAD < head_size + PIECES)).astype(F32)
    piece_of_column = column % PAD - head_size
    place_lane = jnp.arange(128)
    place_own = jnp.stack(
        [
            (
                (place_lane[:, None] == (column // PAD)[None, :]) & (piece_of_column == p)[None, :]
            ).astype(BF)
            for p in range(PIECES)
        ]
    )
    tail_width = 256
    tail_lane = jnp.arange(tail_width)
    column_lane = jnp.where(
        (piece_of_column >= 0) & (piece_of_column < PIECES),
        piece_of_column * heads + column // PAD,
        -1,
    )
    place_lse = (tail_lane[:, None] == column_lane[None, :]).astype(BF)
    place_delta = (
        (tail_lane[:, None] - PIECES * heads == column_lane[None, :])
        & (tail_lane[:, None] >= PIECES * heads)
    ).astype(BF)
    place_tail = jnp.stack([place_lse, place_delta])

    w_pad = jnp.concatenate(
        [
            pad_heads(w_qkv[:, model_width : 2 * model_width], heads, head_size),
            pad_heads(w_qkv[:, 2 * model_width :], heads, head_size),
            pad_heads(w_qkv[:, :model_width], heads, head_size),
        ],
        axis=1,
    )
    w_out_pad = jnp.pad(
        w_out.reshape(heads, head_size, model_width), ((0, 0), (0, PAD - head_size), (0, 0))
    ).reshape(width, model_width)

    mine, sib = window_of(tokens, chips)

    own_spec = fixed((own_rows, 8))
    other_spec = moving((8, keys), 1)
    bias_spec = moving((1, own_rows, heads, keys))
    bias = call(
        bias_kernel,
        pairs,
        [own_spec, other_spec, fixed((4, kernels, 128)), fixed((heads, kernels))],
        bias_spec,
        shape_of((pairs, own_rows, heads, keys)),
        [pltpu.VMEM((own_rows, keys), F32)],
        2 * own_rows * 4 * keys * kernels * 256,
        "pair_bias",
    )(span, own, other, tabs, kernel_weight.T)

    ln1 = jnp.stack([ln1_gain, ln1_bias])
    expanded = pltpu.VMEM((groups, own_rows * GROUP, SPAN), BF)
    summed = pltpu.VMEM((groups, own_rows * GROUP, SPAN), F32)
    mask_scratch = pltpu.VMEM((own_rows, GROUP, keys), F32)
    attended, q_aug, lse_pieces, normed_first_low, kvq = call(
        functools.partial(forward_kernel, scale2, groups),
        pairs,
        [
            own_spec,
            other_spec,
            moving((1, own_rows, model_width)),
            moving((1, own_rows, model_width)),
            fixed((own_rows, model_width)),
            fixed((2, model_width)),
            fixed((model_width, 3 * width)),
            fixed((1, width)),
            fixed((PIECES, 128, width)),
            bias_spec,
        ],
        [
            fixed((own_rows, width)),
            fixed((own_rows, width)),
            fixed((PIECES, own_rows, 128)),
            fixed((own_rows, model_width)),
            moving((1, keys, 3 * width)),
        ],
        [
            shape_of((own_rows, width)),
            shape_of((own_rows, width), BF),
            shape_of((PIECES, own_rows, 128), BF),
            shape_of((own_rows, model_width), BF),
            shape_of((pairs, keys, 3 * width), BF),
        ],
        [
            expanded,
            mask_scratch,
            pltpu.VMEM((groups, own_rows * GROUP, 128), F32),
            pltpu.VMEM((groups, own_rows * GROUP, 128), F32),
            summed,
            pltpu.VMEM((own_rows, 128), F32),
        ],
        2 * own_rows * GROUP * groups * 4 * keys * SPAN * 3,
        "attention_forward",
    )(span, own, other, mine, sib, tokens, ln1, w_pad, ones_row[None], place_own, bias)

    tokens_wide = tokens.astype(F32)
    attended_low_pad = attended.astype(BF)
    mixed = tokens_wide + dot_nn(attended_low_pad, w_out_pad)
    normed_second, second_back = jax.vjp(layer_norm, mixed, ln2_gain, ln2_bias)
    normed_second_low = normed_second.astype(BF)
    up_proj = dot_nn(normed_second_low, w_up)
    activated, gelu_back = jax.vjp(jax.nn.gelu, up_proj)
    hidden_low = activated.astype(BF)
    block_out = (mixed + dot_nn(hidden_low, w_down)).astype(BF)
    grad_hidden = dot_nt(out_cotangent, w_down)
    grad_up = gelu_back(grad_hidden)[0].astype(BF)
    grad_normed_second = dot_nt(grad_up, w_up)
    grad_mixed_norm, grad_gain_second, grad_shift_second = second_back(grad_normed_second)
    grad_mixed = out_cotangent.astype(F32) + grad_mixed_norm
    grad_mixed_low = grad_mixed.astype(BF)
    grad_attended = dot_nt(grad_mixed_low, w_out_pad).astype(BF)
    row_deltas = jnp.sum(
        (grad_attended.astype(F32) * attended).reshape(own_rows, heads, PAD), axis=2
    )
    delta_pieces = pieces_of(-row_deltas)
    do_aug = jnp.concatenate(
        [grad_attended.reshape(own_rows, heads, PAD)[:, :, :head_size]]
        + [piece[:, :, None] for piece in delta_pieces]
        + [jnp.zeros((own_rows, heads, PAD - head_size - PIECES), BF)],
        axis=2,
    ).reshape(own_rows, width)
    payload = jnp.concatenate(
        [grad_mixed_low]
        + [lse_pieces[p, :, :heads] for p in range(PIECES)]
        + delta_pieces
        + [jnp.zeros((own_rows, tail_width - 2 * PIECES * heads), BF)],
        axis=1,
    )
    payload_mine, payload_sib = window_of(payload, chips)

    dq_pad, grad_kernel, moments, own_atoms, key_atoms = call(
        functools.partial(query_grad_kernel, scale2, head_scale, groups),
        pairs,
        [
            own_spec,
            other_spec,
            fixed((own_rows, width)),
            fixed((own_rows, width)),
            moving((1, keys, 2 * width)),
            bias_spec,
            fixed((4, kernels, 128)),
            fixed((kernels, heads)),
        ],
        [
            fixed((own_rows, width)),
            fixed((kernels, heads)),
            fixed((2, kernels, 128)),
            fixed((own_rows, 128)),
            other_spec,
        ],
        [
            shape_of((own_rows, width), BF),
            shape_of((kernels, heads)),
            shape_of((2, kernels, 128)),
            shape_of((own_rows, 128)),
            shape_of((8, pairs * keys)),
        ],
        [
            expanded,
            expanded,
            mask_scratch,
            pltpu.VMEM((own_rows, keys), F32),
            pltpu.VMEM((own_rows, heads, keys), F32),
            summed,
            pltpu.VMEM((kernels, 8 * keys), F32),
            pltpu.VMEM((kernels, 8 * keys), BF),
            pltpu.VMEM((own_rows, keys), F32),
            pltpu.VMEM((5, own_rows, 128), F32),
        ],
        2 * own_rows * GROUP * groups * 4 * keys * SPAN * 8,
        "query_gradients",
    )(span, own, other, q_aug, do_aug, kvq, bias, tabs, kernel_weight)

    dkv_pad = call(
        functools.partial(key_grad_kernel, scale2, head_scale, groups, model_width),
        pairs,
        [
            own_spec,
            other_spec,
            fixed((1, own_rows, 2 * width), chips, 0, 0),
            moving((1, keys, width), 0, 2),
            moving((1, own_rows, model_width + tail_width)),
            moving((1, own_rows, model_width + tail_width)),
            fixed((width, model_width)),
            fixed((2, tail_width, width)),
            bias_spec,
        ],
        fixed((own_rows, 2 * width)),
        shape_of((own_rows, 2 * width), BF),
        [
            expanded,
            expanded,
            mask_scratch,
            pltpu.VMEM((keys, width), BF),
            pltpu.VMEM((keys, width), BF),
            summed,
            summed,
        ],
        2 * own_rows * GROUP * groups * 4 * keys * SPAN * 4,
        "key_gradients",
    )(
        span,
        own,
        other,
        kvq,
        kvq,
        payload_mine,
        payload_sib,
        w_out_pad,
        place_tail,
        bias,
    )

    grad_projected = jnp.concatenate(
        [
            drop_pad(dq_pad, heads, head_size),
            drop_pad(dkv_pad[:, :width], heads, head_size),
            drop_pad(dkv_pad[:, width:], heads, head_size),
        ],
        axis=1,
    )
    qkv_grad_weight = dot_nn(normed_first_low.T, grad_projected)
    grad_normed_first = dot_nt(grad_projected, w_qkv)
    unused, first_back = jax.vjp(layer_norm, tokens_wide, ln1_gain, ln1_bias)
    grad_tokens_norm, grad_gain_first, grad_shift_first = first_back(grad_normed_first)
    grad_tokens = grad_mixed + grad_tokens_norm

    pair_at = jnp.arange(pairs * keys) // keys
    visited = (pair_at >= first_pair) & (pair_at <= last_pair)
    key_atoms = jnp.where(visited[None, :], key_atoms[:5], 0.0)
    own_part = own_atoms[:, :5].T
    key_atoms = lax.dynamic_update_slice(
        key_atoms, key_atoms[:, margin : margin + own_rows] + own_part, (0, margin)
    )
    table_scale_grad = jnp.sum(jnp.where(onehot, key_atoms[3][None, :], 0.0), axis=1)
    table_shift_grad = jnp.sum(jnp.where(onehot, key_atoms[4][None, :], 0.0), axis=1)
    spots = key_atoms[:3].reshape(3, pairs, 2, own_rows)
    spots = jnp.where(core == 0, spots, spots[:, :, ::-1, :]).reshape(3, pairs * keys)
    everywhere = lax.dynamic_update_slice(
        jnp.zeros((3, atoms + 2 * margin), F32), spots, (0, chip_start)
    )[:, margin : margin + atoms]
    centre_sum = jnp.sum(moments[0], axis=1) / (KAPPA * kernel_widths)
    plain_sum = jnp.sum(grad_kernel * kernel_weight.astype(F32), axis=1)
    width_sum = (jnp.sum(moments[1], axis=1) / (KAPPA * KAPPA) - plain_sum) / kernel_widths

    small = lax.psum(
        (
            grad_gain_first,
            grad_shift_first,
            centre_sum,
            width_sum,
            grad_kernel,
            table_scale_grad,
            table_shift_grad,
            grad_gain_second,
            grad_shift_second,
            everywhere,
        ),
        MESH,
    )
    grad_positions = lax.dynamic_slice_in_dim(small[9], flat * own_rows, own_rows, 1)

    attended_low = drop_pad(attended_low_pad, heads, head_size)
    down_columns = dot_nn(out_cotangent.T, hidden_low)
    up_grad_weight = dot_nn(normed_second_low.T, grad_up)
    out_grad_weight = dot_nn(attended_low.T, grad_mixed_low)

    def over_ka(values):
        return lax.psum_scatter(values.astype(BF), "ka", scatter_dimension=1, tiled=True)

    pieces = tuple(
        over_ka(values)
        for values in (qkv_grad_weight, out_grad_weight, up_grad_weight, down_columns)
    )
    totals = tuple(lax.psum(piece, "pb").astype(F32) for piece in pieces)
    return (
        block_out,
        grad_tokens,
        grad_positions,
        small[0],
        small[1],
        totals[0],
        small[2],
        small[3],
        small[4],
        small[5],
        small[6],
        totals[1],
        small[7],
        small[8],
        totals[2],
        totals[3].T,
    )


def solution(mesh):
    rows = P(MESH, None)
    in_specs = (rows,) + (P(),) * 18 + (rows,)
    out_specs = (
        rows,
        rows,
        P(None, MESH),
        P(),
        P(),
        P(None, "ka"),
        P(),
        P(),
        P(),
        P(),
        P(),
        P(None, "ka"),
        P(),
        P(),
        P(None, "ka"),
        P("ka", None),
    )
    return jax.shard_map(
        on_device, mesh=mesh, in_specs=in_specs, out_specs=out_specs, check_vma=False
    )
```

time: 1900 us -> 539 us (0.28); the launches traced: 1880 us -> 547 us
  matrix products: 630 us -> 37.1 us
  other arithmetic: 386 us -> 25.2 us
  local copies, waits for them, and re-layouts: 383 us -> 48.1 us
  starting transfers between devices: 166 us -> 47.5 us
  Pallas kernels: 0 us -> 65.7 us
  waiting for transfers between devices: 248 us -> 305 us
  blocking collectives: 40.8 us -> 0 us
    dot_general x168 -> x11, matrix products: 630 us -> 37.1 us  [the longest x7 23.9 us: dot_nn(): lax.dot_general(left, right, (((1,), (0,)), ((), ())), preferred_element_...]
    reduce_sum x95 -> x7, other arithmetic: 163 us -> 3.67 us  [the longest x1 1.36 us: on_device(): low_atom = jnp.sum((item_of_atom < first_item).astype(jnp.int32))]
    dynamic_slice x198 -> x2, local copies, waits for them, and re-layouts: 147 us -> 1.29 us  [the longest x1 1.25 us: on_device(): lax.dynamic_slice_in_dim(small[9], flat * own_rows, own_rows, 1)]
    ppermute x36 -> x12, starting transfers between devices: 166 us -> 47.1 us  [shifted(): return lax.ppermute(block, axis, route)]
    dot_general x39 -> x0, local copies, waits for them, and re-layouts: 116 us -> none  [scores_from(): jnp.einsum('qkc,ch->hqk', phi_low, kernel_weight, preferred_element_type=...]
    pallas_call x0 -> x4, Pallas kernels: none -> 65.7 us  [the longest x1 23.8 us: on_device(): call(functools.partial(query_grad_kernel, scale2, head_scale, groups), pa...]
    psum x1 -> x2, waiting for transfers between devices: 0.01 us -> 62.9 us  [the longest x1 39 us: on_device(): totals = tuple((lax.psum(piece, 'pb').astype(F32) for piece in pieces))]
    add x81 -> x1, other arithmetic: 49.9 us -> 0.01 us  [on_device(): table_row = table[6] + protein]
  transfers between devices with their start and end apart: 41 -> 20, of which waited for: 12 -> 10; matrix products, arithmetic and copies ran while one was open for 4% -> 15% of each run, Pallas kernels for 0% -> 9%
where the time goes in v1:
time: 539 us; the launch traced here: 547 us
  waiting for transfers between devices  305 us (57%)
  Pallas kernels  65.7 us (12%)
  local copies, waits for them, and re-layouts  48.1 us (9%)
  starting transfers between devices  47.5 us (9%)
  matrix products  37.1 us (7%)
  other arithmetic  25.2 us (5%)
  between operations  18.9 us (4%)
    reduce_scatter x4, waiting for transfers between devices, over_ka(): lax.psum_scatter(values.astype(BF), 'ka', scatter_dimension=1, tiled=True)  191 us
    ppermute x12, waiting for transfers between devices, shifted(): return lax.ppermute(block, axis, route)  50.6 us
    ppermute x12, starting transfers between devices, shifted(): return lax.ppermute(block, axis, route)  47.1 us
    psum x1, waiting for transfers between devices, on_device(): totals = tuple((lax.psum(piece, 'pb').astype(F32) for piece in pieces))  39 us
    unnamed x133, local copies, waits for them, and re-layouts  24.5 us
    psum x1, waiting for transfers between devices, on_device(): lax.psum((grad_gain_first, grad_shift_first, centre_sum, width_sum, grad_...  23.9 us
    dot_general x7, matrix products, dot_nn(): lax.dot_general(left, right, (((1,), (0,)), ((), ())), preferred_element_...  23.9 us
    pallas_call x1, Pallas kernels, on_device(): call(functools.partial(query_grad_kernel, scale2, head_scale, groups), pa...  23.8 us
  transfers between devices with their start and end apart: 20, of which 10 were waited for; matrix products, arithmetic and copies ran while one was open for 15% of the time, Pallas kernels for 9%

profile of v1, /device:TPU:0, one launch (start us, length us, event | category | flops | bytes accessed | tf_op | source)
XLA Modules:
  0.0 547.3 jit_solution(6869494943088740822)
XLA Ops:
  8.1 5.9 %collective-permute-start = (bf16[128,768]{1,0:T(8,128)(2,1)}, bf16[128,768]{1,0:T(8,128)(2,1)S(1)}, u32[]{:S(2)}, u32[]{:S(2)}) collective-permute-start(bf16[128,768]{1,0:T(8,128)(2,1)} %refs_4_.1), channel_id=1, source_target_pairs={{0,6},{1,7},{2,8},{3,9},{4,10},{5,11},{6,12},{7,13},{8,14},{9,15},... | collective-permute-start | bytes 589832 | tf_op jit(solution)/shard_map/ppermute | solution.py:35
  14.0 4.2 collective-permute-start.1
  18.1 4.1 collective-permute-start.2
  54.7 5.2 fusion.62
  68.2 3.8 collective-permute-done.5
  75.5 9.7 %pair_bias.1.refs_9_.refs_5_.refs_8_ = f32[7,128,32,256]{3,2,1,0:T(8,128)} custom-call(s32[2]{0:T(128)} %pad_add_fusion.span_ref, f32[128,8]{1,0:T(8,128)} %copy.128.refs_0_, f32[8,1792]{1,0:T(8,128)} %copy-done.16, f32[4,128,128]{2,1,0:T(8,128)} %pad_maximum_fusion.2.refs_2_.refs_6_, bf16[32,128]{1,0:T(8,128)(2,1)} %bitcast.147), custom_call_target="tpu_custom_call" | custom-call | flops 8589934592 | bytes 20000000 | tf_op jit(solution)/shard_map/pair_bias/pallas_call | solution.py:652
  85.2 16.7 %attention_forward.1 = (f32[128,1024]{1,0:T(8,128)}, bf16[128,1024]{1,0:T(8,128)(2,1)}, bf16[3,128,128]{2,1,0:T(8,128)(2,1)}, bf16[128,768]{1,0:T(8,128)(2,1)}, bf16[7,256,3072]{2,1,0:T(8,128)(2,1)}) custom-call(s32[2]{0:T(128)} %pad_add_fusion.span_ref, f32[128,8]{1,0:T(8,128)} %copy.128.refs_0_, f32[8,1792]{1,0:T(8,128)} %copy-done.16, ...), custom_call_target="tpu_custom_call" | custom-call | flops 6442450944 | bytes 20000000 | tf_op jit(solution)/shard_map/attention_forward/pallas_call | solution.py:667
  105.3 5.6 %fusion.7 = (bf16[128,3072]{1,0:T(8,128)(2,1)S(1)}, f32[128,3072]{1,0:T(8,128)}) fusion(f32[128,3072]{1,0:T(8,128)S(1)} %copy-done.12, bf16[768,3072]{1,0:T(8,128)(2,1)} %param.37, f32[128,768]{1,0:T(8,128)S(1)} %get-tuple-element.187, f32[768]{0:T(1024)S(1)} %copy-done.26, f32[768]{0:T(1024)S(1)} %copy-done.21, f32[128]{0:T(128)S(1)} %fusion.49, ...), kind=kOutput, calls=%fused_computation.14 | convolution fusion | flops 612335616 | bytes 9051136 | tf_op jit(solution)/shard_map/dot_general | solution.py:59
  115.9 4.3 convolution_convert_fusion.2
  121.1 5.1 fusion
  130.5 17.0 %collective-permute-start.7 = (bf16[128,1024]{1,0:T(8,128)(2,1)S(1)}, bf16[128,1024]{1,0:T(8,128)(2,1)S(1)}, u32[]{:S(2)}, u32[]{:S(2)}) collective-permute-start(bf16[128,1024]{1,0:T(8,128)(2,1)S(1)} %concatenate.18), channel_id=1, source_target_pairs={{0,6},{1,7},{2,8},{3,9},{4,10},{5,11},{6,12},{7,13},{8,14},{9,15},... | collective-permute-start | bytes 786440 | tf_op jit(solution)/shard_map/ppermute | solution.py:35
  153.0 4.7 collective-permute-start.9
  164.8 5.1 collective-permute-done.10
  170.6 33.4 %collective-permute-done.11 = bf16[128,1024]{1,0:T(8,128)(2,1)S(1)} collective-permute-done((bf16[128,1024]{1,0:T(8,128)(2,1)S(1)}, bf16[128,1024]{1,0:T(8,128)(2,1)S(1)}, u32[]{:S(2)}, u32[]{:S(2)}) %collective-permute-start.11) | collective-permute-done | bytes 262176 | tf_op jit(solution)/shard_map/ppermute | solution.py:35
  204.8 8.2 %collective-permute-done.12 = bf16[128,1024]{1,0:T(8,128)(2,1)S(1)} collective-permute-done((bf16[128,1024]{1,0:T(8,128)(2,1)S(1)}, bf16[128,1024]{1,0:T(8,128)(2,1)S(1)}, u32[]{:S(2)}, u32[]{:S(2)}) %collective-permute-start.12) | collective-permute-done | bytes 262176 | tf_op jit(solution)/shard_map/ppermute | solution.py:35
  215.0 23.8 %query_gradients.1 = (bf16[128,1024]{1,0:T(8,128)(2,1)}, f32[128,32]{1,0:T(8,128)}, f32[2,128,128]{2,1,0:T(8,128)}, f32[128,128]{1,0:T(8,128)}, f32[8,1792]{1,0:T(8,128)}) custom-call(s32[2]{0:T(128)} %pad_add_fusion.span_ref, f32[128,8]{1,0:T(8,128)} %copy.128.refs_0_, f32[8,1792]{1,0:T(8,128)} %copy-done.16, bf16[128,1024]{1,0:T(8,128)(2,1)} %get-tuple-element.27.refs_2_, ...), custom_call_target="tpu_custom_call" | custom-call | flops 17179869184 | bytes 20000000 | tf_op jit(solution)/shard_map/query_gradients/pallas_call | solution.py:743
  239.9 15.5 %key_gradients.1 = bf16[128,2048]{1,0:T(8,128)(2,1)} custom-call(s32[2]{0:T(128)} %pad_add_fusion.span_ref, f32[128,8]{1,0:T(8,128)} %copy.128.refs_0_, f32[8,1792]{1,0:T(8,128)} %copy-done.16, bf16[7,256,3072]{2,1,0:T(8,128)(2,1)} %get-tuple-element.28.refs_4_.refs_2_.refs_3_, bf16[7,256,3072]{2,1,0:T(8,128)(2,1)} %get-tuple-element.28.refs_4_.refs_2_.refs_3_, ...), custom_call_target="tpu_custom_call" | custom-call | flops 8589934592 | bytes 20000000 | tf_op jit(solution)/shard_map/key_gradients/pallas_call | solution.py:786
  263.3 4.2 fusion.55
  268.5 41.1 %reduce-scatter.9.cloned.1.call-done = bf16[768,192]{0,1:T(8,128)(2,1)} async-done(((bf16[768,3072]{0,1:T(8,128)(2,1)}), bf16[768,192]{0,1:T(8,128)(2,1)}) %reduce-scatter.9.cloned.1.call-update) | async-done | bytes 294928 | tf_op jit(solution)/shard_map/reduce_scatter | solution.py:881
  309.6 78.6 %reduce-scatter.11.cloned.1.call-done = bf16[768,192]{0,1:T(8,128)(2,1)} async-done(((bf16[768,3072]{0,1:T(8,128)(2,1)}), bf16[768,192]{0,1:T(8,128)(2,1)}) %reduce-scatter.11.cloned.1.call-update) | async-done | bytes 294928 | tf_op jit(solution)/shard_map/reduce_scatter | solution.py:881
  388.2 71.6 %reduce-scatter.5.cloned.1.call-done = bf16[768,144]{0,1:T(8,128)(2,1)} async-done(((bf16[768,2304]{0,1:T(8,128)(2,1)}), bf16[768,144]{0,1:T(8,128)(2,1)}) %reduce-scatter.5.cloned.1.call-update) | async-done | bytes 221200 | tf_op jit(solution)/shard_map/reduce_scatter | solution.py:881
  459.8 4.1 fusion.8
  464.8 23.9 %all-reduce.10.cloned.1.call-done = (f32[3,4096]{1,0:T(4,128)}, f32[768]{0:T(1024)}, f32[768]{0:T(1024)}, f32[128]{0:T(128)}, f32[128]{0:T(128)}, /*index=5*/f32...) async-done(((f32[3,4096]{1,0:T(4,128)}, f32[768]{0:T(1024)}, f32[768]{0:T(1024)}, f32[128]{0:T(128)}, f32[128]{0:T(128)}, ...) | async-done | bytes 80144 | tf_op jit(solution)/shard_map/psum | solution.py:858
  491.5 39.0 %all-reduce.12.cloned.1.call-done = (bf16[768,144]{0,1:T(8,128)(2,1)}, bf16[768,48]{0,1:T(8,128)(2,1)}, bf16[768,192]{0,1:T(8,128)(2,1)}, bf16[192,768]{1,0:T(8,128)(2,1)}) async-done(((bf16[768,144]{0,1:T(8,128)(2,1)}, bf16[768,48]{0,1:T(8,128)(2,1)}, bf16[768,192]{0,1:T(8,128)(2,1)}, bf16[192,768]{1,0:T(8,128)(2,1)}), (bf16[768,144]{0,1:T(8,128)(2,1)}, bf16[768,48]{0,1:T(8,128)(2,1)}, ...) | async-done | bytes 884752 | tf_op jit(solution)/shard_map/psum | solution.py:887
  (288 shorter events, 93.8 us)
Async XLA Ops:
  8.0 260.5 %reduce-scatter.7.cloned.1.call-start = ((), (), s32[]{:S(2)}) async-start(), calls=%async_computation.5 | async-start | bytes 1253376 | tf_op jit(solution)/shard_map/reduce_scatter | solution.py:881
  8.1 53.1 %collective-permute-start = (bf16[128,768]{1,0:T(8,128)(2,1)}, bf16[128,768]{1,0:T(8,128)(2,1)S(1)}, u32[]{:S(2)}, u32[]{:S(2)}) collective-permute-start(bf16[128,768]{1,0:T(8,128)(2,1)} %refs_4_.1), channel_id=1, source_target_pairs={{0,6},{1,7},{2,8},{3,9},{4,10},{5,11},{6,12},{7,13},{8,14},{9,15},... | collective-permute-start | bytes 589832 | tf_op jit(solution)/shard_map/ppermute | solution.py:35
  14.0 50.3 %collective-permute-start.1 = (bf16[128,768]{1,0:T(8,128)(2,1)}, bf16[128,768]{1,0:T(8,128)(2,1)}, u32[]{:S(2)}, u32[]{:S(2)}) collective-permute-start(bf16[128,768]{1,0:T(8,128)(2,1)} %refs_4_.1), channel_id=1, source_target_pairs={{0,4},{1,5},{2,6},{3,7},{4,8},{5,9},{6,10},{7,11},{8,12},{9,13},{1... | collective-permute-start | bytes 589832 | tf_op jit(solution)/shard_map/ppermute | solution.py:35
  18.1 47.2 %collective-permute-start.2 = (bf16[128,768]{1,0:T(8,128)(2,1)}, bf16[128,768]{1,0:T(8,128)(2,1)}, u32[]{:S(2)}, u32[]{:S(2)}) collective-permute-start(bf16[128,768]{1,0:T(8,128)(2,1)} %refs_4_.1), channel_id=1, source_target_pairs={{0,2},{1,3},{2,4},{3,5},{4,6},{5,7},{6,8},{7,9},{8,10},{9,11},{10,... | collective-permute-start | bytes 589832 | tf_op jit(solution)/shard_map/ppermute | solution.py:35
  22.2 44.1 %collective-permute-start.3 = (bf16[128,768]{1,0:T(8,128)(2,1)}, bf16[128,768]{1,0:T(8,128)(2,1)}, u32[]{:S(2)}, u32[]{:S(2)}) collective-permute-start(bf16[128,768]{1,0:T(8,128)(2,1)} %refs_4_.1), channel_id=1, source_target_pairs={{2,0},{3,1},{4,2},{5,3},{6,4},{7,5},{8,6},{9,7},{10,8},{11,9},{12,... | collective-permute-start | bytes 589832 | tf_op jit(solution)/shard_map/ppermute | solution.py:35
  23.5 43.8 %collective-permute-start.4 = (bf16[128,768]{1,0:T(8,128)(2,1)}, bf16[128,768]{1,0:T(8,128)(2,1)}, u32[]{:S(2)}, u32[]{:S(2)}) collective-permute-start(bf16[128,768]{1,0:T(8,128)(2,1)} %refs_4_.1), channel_id=1, source_target_pairs={{4,0},{5,1},{6,2},{7,3},{8,4},{9,5},{10,6},{11,7},{12,8},{13,9},{1... | collective-permute-start | bytes 589832 | tf_op jit(solution)/shard_map/ppermute | solution.py:35
  53.4 73.5 %copy-start = (bf16[32,32,768]{2,1,0:T(8,128)(2,1)}, bf16[32,32,768]{2,1,0:T(8,128)(2,1)S(1)}, u32[]{:S(2)}) copy-start(bf16[32,32,768]{2,1,0:T(8,128)(2,1)S(1)} %pad.22) | copy-start | bytes 4718596
  61.8 10.3 %collective-permute-start.5 = (bf16[128,768]{1,0:T(8,128)(2,1)S(1)}, bf16[128,768]{1,0:T(8,128)(2,1)S(1)}, u32[]{:S(2)}, u32[]{:S(2)}) collective-permute-start(bf16[128,768]{1,0:T(8,128)(2,1)S(1)} %copy-done.1), channel_id=1, source_target_pairs={{6,0},{7,1},{8,2},{9,3},{10,4},{11,5},{12,6},{13,7},{14,8},{15,9},... | collective-permute-start | bytes 589832 | tf_op jit(solution)/shard_map/ppermute | solution.py:35
  72.1 13.1 %collective-permute-start.6 = (bf16[7,128,768]{2,1,0:T(8,128)(2,1)S(1)}, bf16[7,128,768]{2,1,0:T(8,128)(2,1)}, u32[]{:S(2)}, u32[]{:S(2)}) collective-permute-start(bf16[7,128,768]{2,1,0:T(8,128)(2,1)S(1)} %bitcast_dynamic-update-slice_fusion.7.refs_2_), channel_id=1, source_target_pairs={{0,1},{1,0},{2,3},{3,2},{4,5},{5,4},{6,7},{7,6},{8,9},{9,8},{10,11... | collective-permute-start | bytes 4128776 | tf_op jit(solution)/shard_map/ppermute | solution.py:40
  115.8 193.8 %reduce-scatter.9.cloned.1.call-start = ((), (), s32[]{:S(2)}) async-start(), calls=%async_computation.6 | async-start | bytes 5013504 | tf_op jit(solution)/shard_map/reduce_scatter | solution.py:881
  120.2 268.0 %reduce-scatter.11.cloned.1.call-start = ((), (), s32[]{:S(2)}) async-start(), calls=%async_computation.7 | async-start | bytes 5013504 | tf_op jit(solution)/shard_map/reduce_scatter | solution.py:881
  126.2 333.5 %reduce-scatter.5.cloned.1.call-start = ((), (), s32[]{:S(2)}) async-start(), calls=%async_computation.4 | async-start | bytes 3760128 | tf_op jit(solution)/shard_map/reduce_scatter | solution.py:881
  130.5 29.8 %collective-permute-start.7 = (bf16[128,1024]{1,0:T(8,128)(2,1)S(1)}, bf16[128,1024]{1,0:T(8,128)(2,1)S(1)}, u32[]{:S(2)}, u32[]{:S(2)}) collective-permute-start(bf16[128,1024]{1,0:T(8,128)(2,1)S(1)} %concatenate.18), channel_id=1, source_target_pairs={{0,6},{1,7},{2,8},{3,9},{4,10},{5,11},{6,12},{7,13},{8,14},{9,15},... | collective-permute-start | bytes 786440 | tf_op jit(solution)/shard_map/ppermute | solution.py:35
  147.9 14.7 %collective-permute-start.8 = (bf16[128,1024]{1,0:T(8,128)(2,1)S(1)}, bf16[128,1024]{1,0:T(8,128)(2,1)S(1)}, u32[]{:S(2)}, u32[]{:S(2)}) collective-permute-start(bf16[128,1024]{1,0:T(8,128)(2,1)S(1)} %concatenate.18), channel_id=1, source_target_pairs={{0,4},{1,5},{2,6},{3,7},{4,8},{5,9},{6,10},{7,11},{8,12},{9,13},{1... | collective-permute-start | bytes 786440 | tf_op jit(solution)/shard_map/ppermute | solution.py:35
  153.0 10.4 %collective-permute-start.9 = (bf16[128,1024]{1,0:T(8,128)(2,1)S(1)}, bf16[128,1024]{1,0:T(8,128)(2,1)S(1)}, u32[]{:S(2)}, u32[]{:S(2)}) collective-permute-start(bf16[128,1024]{1,0:T(8,128)(2,1)S(1)} %concatenate.18), channel_id=1, source_target_pairs={{0,2},{1,3},{2,4},{3,5},{4,6},{5,7},{6,8},{7,9},{8,10},{9,11},{10,... | collective-permute-start | bytes 786440 | tf_op jit(solution)/shard_map/ppermute | solution.py:35
  157.7 12.2 %collective-permute-start.10 = (bf16[128,1024]{1,0:T(8,128)(2,1)S(1)}, bf16[128,1024]{1,0:T(8,128)(2,1)S(1)}, u32[]{:S(2)}, u32[]{:S(2)}) collective-permute-start(bf16[128,1024]{1,0:T(8,128)(2,1)S(1)} %concatenate.18), channel_id=1, source_target_pairs={{2,0},{3,1},{4,2},{5,3},{6,4},{7,5},{8,6},{9,7},{10,8},{11,9},{12,... | collective-permute-start | bytes 786440 | tf_op jit(solution)/shard_map/ppermute | solution.py:35
  159.0 45.1 %collective-permute-start.11 = (bf16[128,1024]{1,0:T(8,128)(2,1)S(1)}, bf16[128,1024]{1,0:T(8,128)(2,1)S(1)}, u32[]{:S(2)}, u32[]{:S(2)}) collective-permute-start(bf16[128,1024]{1,0:T(8,128)(2,1)S(1)} %concatenate.18), channel_id=1, source_target_pairs={{4,0},{5,1},{6,2},{7,3},{8,4},{9,5},{10,6},{11,7},{12,8},{13,9},{1... | collective-permute-start | bytes 786440 | tf_op jit(solution)/shard_map/ppermute | solution.py:35
  160.3 52.6 %collective-permute-start.12 = (bf16[128,1024]{1,0:T(8,128)(2,1)S(1)}, bf16[128,1024]{1,0:T(8,128)(2,1)S(1)}, u32[]{:S(2)}, u32[]{:S(2)}) collective-permute-start(bf16[128,1024]{1,0:T(8,128)(2,1)S(1)} %concatenate.18), channel_id=1, source_target_pairs={{6,0},{7,1},{8,2},{9,3},{10,4},{11,5},{12,6},{13,7},{14,8},{15,9},... | collective-permute-start | bytes 786440 | tf_op jit(solution)/shard_map/ppermute | solution.py:35
  162.6 51.2 %copy-start.14 = (bf16[128,1024]{1,0:T(8,128)(2,1)S(1)}, bf16[128,1024]{1,0:T(8,128)(2,1)}, u32[]{:S(2)}) copy-start(bf16[128,1024]{1,0:T(8,128)(2,1)} %get-tuple-element.192) | copy-start | bytes 786436
  213.7 26.3 %collective-permute-start.13 = (bf16[7,128,1024]{2,1,0:T(8,128)(2,1)}, bf16[7,128,1024]{2,1,0:T(8,128)(2,1)}, u32[]{:S(2)}, u32[]{:S(2)}) collective-permute-start(bf16[7,128,1024]{2,1,0:T(8,128)(2,1)} %bitcast_dynamic-update-slice_fusion.refs_4_), channel_id=1, source_target_pairs={{0,1},{1,0},{2,3},{3,2},{4,5},{5,4},{6,7},{7,6},{8,9},{9,8},{10,11... | collective-permute-start | bytes 5505032 | tf_op jit(solution)/shard_map/ppermute | solution.py:40
  259.9 228.8 %all-reduce.10.cloned.1.call-start = ((), (), s32[]{:S(2)}) async-start(), calls=%async_computation.8 | async-start | bytes 301056 | tf_op jit(solution)/shard_map/psum | solution.py:858
  267.6 192.2 %copy-start.6 = (f32[128,3072]{1,0:T(8,128)S(1)}, f32[128,3072]{1,0:T(8,128)}, u32[]{:S(2)}) copy-start(f32[128,3072]{1,0:T(8,128)} %get-tuple-element.189) | copy-start | bytes 4718596
  268.4 262.1 %all-reduce.12.cloned.1.call-start = ((), (), s32[]{:S(2)}) async-start(), calls=%async_computation.9 | async-start | bytes 1769472 | tf_op jit(solution)/shard_map/psum | solution.py:887
  488.7 50.9 %copy-start.37 = (f32[768]{0:T(1024)S(1)}, f32[768]{0:T(1024)}, u32[]{:S(2)}) copy-start(f32[768]{0:T(1024)} %get-tuple-element.209) | copy-start | bytes 9220
  (50 other events, 545.5 us)
Sparse Core Ops, SparseCore 0:
  116.0 114.6 reduce-scatter.6
  235.0 74.5 reduce-scatter.8
  313.5 74.6 reduce-scatter.10
  392.4 67.2 reduce-scatter.4
Sparse Core Ops, SparseCore 1:
  268.5 220.1 all-reduce.9
  491.2 39.2 all-reduce.11

commit v2 on v1

v2 whole, which is shorter than its diff:
```python
import functools
import math

import jax
import jax.numpy as jnp
import numpy as np
from jax import lax
from jax.experimental import pallas as pl
from jax.experimental.pallas import tpu as pltpu
from jax.sharding import PartitionSpec as P

MOL_TYPES = 128
PROT_LEN = 768
MOL_MEAN = 32

LN_EPS = 1e-05
GELU_SLOPE = math.sqrt(2.0 / math.pi)
GELU_CUBE = 0.044715
MASKED = -1e30
ROOT_TWO_PI = math.sqrt(2.0 * math.pi)
LOG2E = math.log2(math.e)
KAPPA = math.sqrt(0.5 * LOG2E)

PAD = 32
GROUP = 8
SPAN = PAD * GROUP
PIECES = 3
WEIGHT_PIECES = 2
CHUNK = 32
FEW = 8
MESH = ("pb", "ka")

BF = jnp.bfloat16
F32 = jnp.float32


def shifted(block, axis, distance):
    devices = range(lax.axis_size(axis))
    route = [(i - distance, i) for i in devices if i - distance in devices]
    return lax.ppermute(block, axis, route)


def core_flip(block):
    devices = range(lax.axis_size(MESH))
    return lax.ppermute(block, MESH, [(i, i ^ 1) for i in devices])


class Window:
    def __init__(self, block, sibling=None):
        devices = range(lax.axis_size(MESH))
        self.sibling = sibling
        far = [(i - 6 if (i >> 1) % 2 == 0 else i + 6, i) for i in devices]
        self.block = block
        self.before = shifted(block, MESH, 4)
        self.after = shifted(block, MESH, -4)
        self.far = lax.ppermute(block, MESH, [(i, j) for i, j in far if i in devices])
        self.beside = lax.ppermute(block, MESH, [(i, i ^ 2) for i in devices])

    def first(self):
        return [self.before, self.after, self.far, self.beside]

    def finish(self):
        devices = range(lax.axis_size(MESH))
        others = [lax.ppermute(x, MESH, [(i, i ^ 2) for i in devices]) for x in (self.before, self.after)]
        mine = [self.far, self.before, others[0], self.block, self.beside, self.after, others[1]]
        came = [core_flip(x) for x in mine if x is not self.block]
        own = core_flip(self.block) if self.sibling is None else self.sibling
        return mine + came[:3] + [own] + came[3:]


SLOTS = ((0, 1, 2, 3, 4, 5, 6), (2, 1, 4, 3, 6, 5, 0))
SPAN_FIRST, SPAN_LAST, SPAN_CORE, SPAN_CHIP, SPAN_SLOT = 0, 1, 2, 3, 4
SPAN_LOW = 16
SPAN_HIGH = 32
SPAN_ROWS = 48
LANES = 128
SIDE = 16


def flip_bit(block, axis, bit):
    devices = range(lax.axis_size(axis))
    return lax.ppermute(block, axis, [(i, i ^ (1 << bit)) for i in devices])


def bit_of(axis, bit):
    return (lax.axis_index(axis) >> bit) & 1


def bits_of(axis):
    return (lax.axis_size(axis) - 1).bit_length()


def halves_of(values, dim, at):
    return (
        lax.dynamic_index_in_dim(values, at, dim, keepdims=False),
        lax.dynamic_index_in_dim(values, 1 - at, dim, keepdims=False),
    )


def add_low(kept, came):
    return (kept.astype(F32) + came.astype(F32)).astype(BF)


class Slices:
    def __init__(self, kept, sent, order, skip=0):
        self.tail = kept.shape[-2:]
        count = 2 * kept.size // (self.tail[0] * self.tail[1])
        self.left = [bit for bit in range(count.bit_length() - 1) if bit != order[0]]
        self.todo = [("ka", bit) for bit in order]
        self.todo += [("pb", bit) for bit in range(skip, bits_of("pb"))]
        self.kept, self.sent = kept, sent

    def step(self):
        axis, bit = self.todo.pop(0)
        values = add_low(self.kept, flip_bit(self.sent, axis, bit + (axis == "ka")))
        if not self.todo:
            self.kept = values
        elif self.todo[0][0] == "pb":
            self.kept = self.sent = values.reshape(self.tail)
        else:
            bit = self.todo[0][1]
            above = sum(1 for b in self.left if b > bit)
            shape = (2**above, 2, 2 ** (len(self.left) - above - 1), *self.tail)
            self.kept, self.sent = halves_of(values.reshape(shape), 1, bit_of("ka", bit + 1))
            self.left.remove(bit)

    def result(self):
        while self.todo:
            self.step()
        return self.kept.reshape(self.tail)


class Columns:
    def __init__(self, kept, sent, order):
        self.order, self.kept, self.sent, self.inner = order, kept, sent, None

    def step(self):
        if self.inner is None:
            values = add_low(self.kept, flip_bit(self.sent, "pb", 0))
            bit = self.order[0]
            shape = (2 ** (values.shape[0].bit_length() - 2 - bit), 2, 2**bit, *values.shape[1:])
            halves = halves_of(values.reshape(shape), 1, bit_of("ka", bit + 1))
            self.inner = Slices(*halves, self.order, skip=1)
        else:
            self.inner.step()
        self.sent = self.inner.sent

    def result(self):
        if self.inner is None:
            self.step()
        mine = self.inner.result()
        other = flip_bit(mine, "pb", 0)
        return jnp.where(
            bit_of("pb", 0) == 0,
            jnp.concatenate([mine, other], axis=1),
            jnp.concatenate([other, mine], axis=1),
        )


def sum_everywhere(values):
    for axis in ("ka", "pb"):
        for bit in range(bits_of(axis)):
            values = values + flip_bit(values, axis, bit)
    return values


def layer_norm(values, ln_gain, ln_shift):
    centre = jnp.mean(values, axis=-1, keepdims=True)
    offsets = values - centre
    spread = jnp.mean(offsets * offsets, axis=-1, keepdims=True)
    return offsets * lax.rsqrt(spread + LN_EPS) * ln_gain + ln_shift


def dot_nn(left, right):
    return lax.dot_general(left, right, (((1,), (0,)), ((), ())), preferred_element_type=F32)


def dot_nt(left, right):
    return lax.dot_general(left, right, (((1,), (1,)), ((), ())), preferred_element_type=F32)


def dot_tn(left, right):
    return lax.dot_general(left, right, (((0,), (0,)), ((), ())), preferred_element_type=F32)


def select_table(head_size):
    column = np.arange(SPAN)
    source = (column // PAD) * head_size + column % PAD
    table = [
        (column[:, None] == (source + off)[None, :]) & (column % PAD < head_size)[None, :]
        for off in (0, 64)
    ]
    return np.stack(table).astype(BF)


def group_windows(groups, head_size):
    out = []
    for g in range(groups):
        start = g * GROUP * head_size
        out.append((start // LANES * LANES, (start % LANES) // 64))
    return out


def place_table(heads, head_size):
    column = np.arange(heads * PAD)
    lane = np.arange(LANES)
    return np.stack(
        [
            (lane[:, None] == (column // PAD)[None, :])
            & (column % PAD == head_size + p)[None, :]
            for p in range(PIECES)
        ]
    ).astype(BF)


def tail_tables(heads, head_size):
    lane, tail = np.arange(LANES), np.arange(2 * LANES)
    into = np.stack(
        [
            (lane[:, None] + p * heads == tail[None, :]) & (lane < heads)[:, None]
            for p in range(2 * PIECES)
        ]
    )
    column = np.arange(heads * PAD)
    piece = column % PAD - head_size
    free = (piece >= 0) & (piece < PIECES)
    lane_of = np.where(free, piece * heads + column // PAD, -1)
    out = np.stack(
        [
            (tail[:, None] == lane_of[None, :]) & free[None, :],
            (tail[:, None] - PIECES * heads == lane_of[None, :]) & free[None, :],
        ]
    )
    return into.astype(BF), out.astype(BF)


def ones_row(heads, head_size):
    column = np.arange(heads * PAD) % PAD
    return ((column >= head_size) & (column < head_size + PIECES)).astype(np.float32)[None]


def head_sum_table(heads):
    column = np.arange(heads * PAD)
    return (column[:, None] // PAD == np.arange(LANES)[None, :]).astype(BF)


def pad_columns(values, select_ref, windows):
    parts = [
        dot_nn(values[:, start : start + SPAN], select_ref[kind]).astype(BF)
        for start, kind in windows
    ]
    return jnp.concatenate(parts, axis=1)


def drop_columns(values, select_ref, windows):
    tiles = {}
    for g, (start, kind) in enumerate(windows):
        part = dot_nt(values[:, g * SPAN : (g + 1) * SPAN], select_ref[kind])
        for k in range(SPAN // LANES):
            tile = part[:, k * LANES : (k + 1) * LANES]
            at = start // LANES + k
            tiles[at] = tiles[at] + tile if at in tiles else tile
    return jnp.concatenate([tiles[at] for at in sorted(tiles)], axis=1).astype(BF)


def split(values, count):
    rest, out = values, []
    for _ in range(count):
        piece = rest.astype(BF)
        rest = rest - piece.astype(F32)
        out.append(piece)
    return out


def norm_parts(values):
    centre = jnp.mean(values, axis=-1, keepdims=True)
    offsets = values - centre
    spread = jnp.mean(offsets * offsets, axis=-1, keepdims=True)
    slope = lax.rsqrt(spread + LN_EPS)
    return offsets * slope, slope


def norm_back(grad, normal, slope, gain):
    inner = grad * gain
    mean = jnp.mean(inner, axis=-1, keepdims=True)
    tilt = jnp.mean(inner * normal, axis=-1, keepdims=True)
    by_gain = jnp.sum(grad * normal, axis=0, keepdims=True)
    by_shift = jnp.sum(grad, axis=0, keepdims=True)
    return slope * (inner - mean - normal * tilt), by_gain, by_shift


def stretched_of(own, other):
    delta = [own[:, i : i + 1] - other[i : i + 1, :] for i in range(3)]
    square = delta[0] * delta[0] + delta[1] * delta[1] + delta[2] * delta[2]
    dist = jnp.sqrt(square + 1.0)
    scales = own[:, 3:4] * other[3:4, :]
    stretched = scales * dist + own[:, 4:5] + other[4:5, :]
    return delta, dist, scales, stretched


def mask_of(own, other, key_is_own):
    same = own[:, 5:6] == other[5:6, :]
    itself = own[:, 7:8] == other[7:8, :]
    is_open = (own[:, 6:7] > 0.5) if key_is_own else (other[6:7, :] > 0.5)
    return jnp.where(same & (is_open | itself), 0.0, MASKED)


def line_atoms(lines):
    line = lax.broadcasted_iota(jnp.int32, (lines, lines // GROUP), 0)
    atom = lax.broadcasted_iota(jnp.int32, (lines, lines // GROUP), 1)
    return jnp.where(line // GROUP == atom, 1.0, 0.0).astype(BF)


def line_heads(lines):
    line = lax.broadcasted_iota(jnp.int32, (lines, SPAN), 0)
    column = lax.broadcasted_iota(jnp.int32, (lines, SPAN), 1)
    return jnp.where(column // PAD == line % GROUP, 1.0, 0.0)


def expand_into(out_ref, padded, groups):
    lines = CHUNK * GROUP
    keep = line_heads(lines).astype(BF)
    spread = line_atoms(lines)
    for g in range(groups):
        for i in range(padded.shape[0] // CHUNK):
            part = padded[i * CHUNK : (i + 1) * CHUNK, g * SPAN : (g + 1) * SPAN]
            out_ref[g, i * lines : (i + 1) * lines, :] = dot_nn(spread, part).astype(BF) * keep


def collapse(values):
    lines = values.shape[0]
    kept = values * line_heads(lines)
    high = kept.astype(BF)
    low = (kept - high.astype(F32)).astype(BF)
    line = lax.broadcasted_iota(jnp.int32, (lines // GROUP, lines), 1)
    atom = lax.broadcasted_iota(jnp.int32, (lines // GROUP, lines), 0)
    gather = jnp.where(line // GROUP == atom, 1.0, 0.0).astype(BF)
    return dot_nn(gather, high) + dot_nn(gather, low)


def fetch(span_ref, refs, out_ref):
    slot = span_ref[SPAN_SLOT + span_ref[SPAN_FIRST, 0] + pl.program_id(0), 0]
    count = len(refs) // 2
    rows = refs[0].shape[0]
    for k in range(count):

        @pl.when(slot == k)
        def _():
            out_ref[:rows] = refs[k][...]
            out_ref[rows:] = refs[count + k][...]


def spots_of(span_ref, rows):
    core = span_ref[SPAN_CORE, 0]
    return [pl.ds(pl.multiple_of(at * rows, rows), rows) for at in (core, 1 - core)]


def spread_mask(mask_ref, mask):
    mask_ref[...] = jnp.broadcast_to(mask[:, None, :], mask_ref.shape)


def reaches(span_ref, first, last, low, high):
    return (span_ref[SPAN_LOW + first, 0] <= high) & (span_ref[SPAN_HIGH + last, 0] >= low)


def head_steps(span_ref, rows, step):
    pair = span_ref[SPAN_FIRST, 0] + pl.program_id(0)
    few = CHUNK // FEW

    def one(i, carry):
        @pl.when(reaches(span_ref, i * few, i * few + few - 1, 2 * pair, 2 * pair + 1))
        def _():
            step(i)

        return carry

    lax.fori_loop(0, rows // CHUNK, one, 0)


def kernel_steps(span_ref, rows, step, skipped):
    pair = span_ref[SPAN_FIRST, 0] + pl.program_id(0)

    def one(i, carry):
        for half in range(2):
            block = 2 * pair + half
            needed = reaches(span_ref, i, i, block, block)

            @pl.when(needed)
            def _():
                step(i, half)

            @pl.when(jnp.logical_not(needed))
            def _():
                skipped(i, half)

        return carry

    lax.fori_loop(0, rows // FEW, one, 0)


def side_kernel(
    atoms_blocks,
    flat_ref,
    pos_ref,
    item_ref,
    open_ref,
    type_ref,
    length_ref,
    table_ref,
    means_ref,
    widths_ref,
    kw_ref,
    span_ref,
    other_ref,
    own_ref,
    line_ref,
    tab_ref,
    gw_ref,
    kwt_ref,
    par_ref,
):
    flat = flat_ref[0]
    chips = len(SLOTS[0]) // 2
    first_block = flat // 2 * 2 - 2 * chips
    ids = lax.broadcasted_iota(jnp.int32, (LANES, LANES), 0).astype(F32)
    lane = lax.broadcasted_iota(jnp.int32, (1, LANES), 1)
    tables = []
    for k in range(table_ref.shape[0] // 2):
        rows = split(table_ref[2 * k : 2 * k + 1, :], PIECES)
        rows += split(table_ref[2 * k + 1 : 2 * k + 2, :], PIECES)
        rows += [jnp.zeros((2, LANES), BF)]
        tables.append(jnp.concatenate([row.astype(F32) for row in rows], axis=0).astype(BF))
    flags = [
        jnp.broadcast_to(
            jnp.where(length_ref[k : k + 1, :] > 2 * MOL_MEAN, float(MOL_TYPES), 0.0), (8, LANES)
        ).astype(BF)
        for k in range(length_ref.shape[0])
    ]
    for b in range(other_ref.shape[1] // LANES):
        block = first_block + b
        inside = (block >= 0) & (block < atoms_blocks)
        source = jnp.clip(block, 0, atoms_blocks - 1)
        at = pl.ds(pl.multiple_of(source * LANES, LANES), LANES)
        item = jnp.where(inside, item_ref[pl.ds(source, 1), :].astype(F32), -1.0)
        kind = type_ref[pl.ds(source, 1), :].astype(F32)
        for k, flag in enumerate(flags):
            onehot = jnp.where(ids + float(k * LANES) == item, 1.0, 0.0).astype(BF)
            kind = kind + dot_nn(flag, onehot)[0:1, :]
        found = jnp.zeros((8, LANES), F32)
        for k, table in enumerate(tables):
            onehot = jnp.where(ids + float(k * LANES) == kind, 1.0, 0.0).astype(BF)
            found = found + dot_nn(table, onehot)
        rows = [pos_ref[k : k + 1, at] for k in range(3)]
        rows += [found[0:1] + found[1:2] + found[2:3], found[3:4] + found[4:5] + found[5:6]]
        rows += [item, open_ref[pl.ds(source, 1), :].astype(F32)]
        rows += [(block * LANES + lane).astype(F32), kind]
        rows += [jnp.zeros((SIDE - 9, LANES), F32)]
        side = jnp.concatenate(rows, axis=0)
        other_ref[:, b * LANES : (b + 1) * LANES] = side

        @pl.when(block == flat)
        def _():
            line_ref[...] = side

    line = line_ref[...]
    turned = jnp.transpose(
        jnp.concatenate([line, jnp.zeros((LANES - SIDE, LANES), F32)], axis=0)
    )
    own_ref[...] = turned
    chunks = LANES // FEW
    item_column = jnp.broadcast_to(own_ref[:, 5:6], (LANES, LANES))
    par_ref[...] = item_column
    first_item = par_ref[pl.ds(0, chunks, stride=FEW), :]
    last_item = par_ref[pl.ds(FEW - 1, chunks, stride=FEW), :]

    def count(k, carry):
        row = item_ref[pl.ds(k, 1), :].astype(F32)
        below, upto = carry
        return (
            below + jnp.where(row < first_item, 1.0, 0.0),
            upto + jnp.where(row <= last_item, 1.0, 0.0),
        )

    zero = jnp.zeros((chunks, LANES), F32)
    below, upto = lax.fori_loop(0, atoms_blocks, count, (zero, zero))
    below = jnp.sum(below, axis=1, keepdims=True).astype(jnp.int32)
    upto = jnp.sum(upto, axis=1, keepdims=True).astype(jnp.int32)
    low = jnp.right_shift(below - first_block * LANES, 7)
    high = jnp.right_shift(upto - 1 - first_block * LANES, 7)
    span_ref[SPAN_LOW : SPAN_LOW + chunks, :] = jnp.broadcast_to(low, (chunks, LANES))
    span_ref[SPAN_HIGH : SPAN_HIGH + chunks, :] = jnp.broadcast_to(high, (chunks, LANES))
    row = lax.broadcasted_iota(jnp.int32, (SPAN_LOW, LANES), 0)
    odd = (flat // 2) % 2
    head = jnp.where(row == SPAN_FIRST, jnp.right_shift(low[0:1, :], 1), 0)
    head = head + jnp.where(row == SPAN_LAST, jnp.right_shift(high[chunks - 1 :, :], 1), 0)
    head = head + jnp.where(row == SPAN_CORE, flat % 2, 0)
    head = head + jnp.where(row == SPAN_CHIP, flat // 2, 0)
    for k, (even_slot, odd_slot) in enumerate(zip(*SLOTS)):
        head = head + jnp.where(
            row == SPAN_SLOT + k, even_slot + odd * (odd_slot - even_slot), 0
        )
    span_ref[:SPAN_LOW, :] = head

    def column_of(ref):
        return jnp.transpose(jnp.broadcast_to(ref[...], (LANES, LANES)))

    means, widths = column_of(means_ref), column_of(widths_ref)
    peaks = 1.0 / (ROOT_TWO_PI * widths)
    bend = -(KAPPA * KAPPA) / (widths * widths)
    tab_ref[0] = means
    tab_ref[1] = KAPPA / widths
    tab_ref[2] = LOG2E * jnp.log(peaks)
    tab_ref[3] = bend
    weights = kw_ref[...].astype(F32)
    heads = weights.shape[1]
    scaled = weights * (peaks / (widths * widths))[:, :heads]
    gw_ref[...] = jnp.concatenate(split(scaled, WEIGHT_PIECES), axis=1)
    wide = jnp.concatenate([weights, jnp.zeros((LANES, LANES - heads), F32)], axis=1)
    kwt_ref[...] = jnp.transpose(wide)[:heads, :].astype(BF)
    lanes = lax.broadcasted_iota(jnp.int32, (LANES, LANES), 1)
    par = wide + jnp.where(lanes == heads, peaks, 0.0)
    par_ref[...] = par + jnp.where(lanes == heads + 1, 1.0 / widths, 0.0)


def bias_kernel(span_ref, own_ref, other_ref, tab_ref, kwt_ref, out_ref, str_ref):
    rows, keys = str_ref.shape
    kernels = tab_ref.shape[1]
    heads = kwt_ref.shape[0]
    half_keys = keys // 2
    str_ref[...] = stretched_of(own_ref[...], other_ref[...])[3]

    def step(i, half):
        columns = slice(half * half_keys, (half + 1) * half_keys)
        block = str_ref[pl.ds(pl.multiple_of(i * FEW, FEW), FEW), columns]
        parts = []
        for r in range(FEW):
            line = jnp.broadcast_to(block[r : r + 1], (kernels, half_keys))
            z = (line - tab_ref[0]) * tab_ref[1]
            parts.append(jnp.exp2(tab_ref[2] - z * z).astype(BF))
        for r in range(0, FEW, 2):
            phi = jnp.concatenate(parts[r : r + 2], axis=1)
            result = dot_nn(kwt_ref[...], phi) * LOG2E
            out_ref[0, i * FEW + r, :, columns] = result[:, :half_keys]
            out_ref[0, i * FEW + r + 1, :, columns] = result[:, half_keys:]

    def skipped(i, half):
        columns = slice(half * half_keys, (half + 1) * half_keys)
        out_ref[0, pl.ds(i * FEW, FEW), :, columns] = jnp.zeros((FEW, heads, half_keys), F32)

    kernel_steps(span_ref, rows, step, skipped)


def forward_kernel(
    scale2,
    groups,
    chips,
    span_ref,
    own_ref,
    other_ref,
    *refs,
):
    token_refs, refs = refs[:14], refs[14:]
    ln_ref, w_ref, select_ref, ones_ref, place_ref, bias_ref, *refs = refs
    att_ref, qaug_ref, lse_ref, now_ref, kvq_ref, *refs = refs
    qexp_ref, mask_ref, max_ref, sum_ref, acc_ref, lane_ref, both_ref = refs
    step = pl.program_id(0)
    width = groups * SPAN
    tok_ref = token_refs[3]
    rows, model_width = tok_ref.shape
    windows = group_windows(groups, model_width // (groups * GROUP))
    gain, shift = ln_ref[0:1, :], ln_ref[1:2, :]

    @pl.when(step == 0)
    def _():
        normed = layer_norm(tok_ref[...].astype(F32), gain, shift).astype(BF)
        query = dot_nn(normed, w_ref[:, :model_width]).astype(BF)
        query = pad_columns(query, select_ref, windows)
        qaug_ref[...] = query
        expand_into(qexp_ref, query, groups)
        max_ref[...] = jnp.full(max_ref.shape, 2.0 * MASKED, F32)
        sum_ref[...] = jnp.zeros(sum_ref.shape, F32)
        acc_ref[...] = jnp.zeros(acc_ref.shape, F32)

    fetch(span_ref, token_refs, both_ref)
    normed = layer_norm(both_ref[...].astype(F32), gain, shift).astype(BF)
    spots = spots_of(span_ref, rows)

    @pl.when(step + span_ref[SPAN_FIRST, 0] == chips)
    def _():
        now_ref[...] = normed

    for part in range(3):
        source = (part + 1) % 3 * model_width
        value = dot_nn(normed, w_ref[:, source : source + model_width]).astype(BF)
        value = pad_columns(value, select_ref, windows)
        if part < 2:
            value = value + ones_ref[...].astype(BF)
        for k in range(2):
            kvq_ref[0, spots[k], part * width : (part + 1) * width] = (
                value[k * rows : (k + 1) * rows]
            )
    spread_mask(mask_ref, mask_of(own_ref[...], other_ref[...], False))

    def chunk_step(i):
        at = pl.multiple_of(i * CHUNK, CHUNK)
        lines = pl.ds(pl.multiple_of(i * CHUNK * GROUP, CHUNK * GROUP), CHUNK * GROUP)
        mask = mask_ref[pl.ds(at, CHUNK)]
        for g in range(groups):
            columns = slice(g * SPAN, (g + 1) * SPAN)
            dots = dot_nt(qexp_ref[g, lines, :], kvq_ref[0, :, columns])
            bias = bias_ref[0, pl.ds(at, CHUNK), g * GROUP : (g + 1) * GROUP, :] + mask
            scores = dots * scale2 + bias.reshape(dots.shape)
            old = max_ref[g, lines, :]
            top = jnp.maximum(scores[:, :128], scores[:, 128:])
            new = jnp.maximum(old, jnp.max(top, axis=1, keepdims=True))
            alpha = jnp.exp2(old - new)
            low = jnp.exp2(scores[:, :128] - new)
            high = jnp.exp2(scores[:, 128:] - new)
            max_ref[g, lines, :] = new
            sum_ref[g, lines, :] = sum_ref[g, lines, :] * alpha + (low + high)
            probs = jnp.concatenate([low, high], axis=1).astype(BF)
            values = dot_nn(probs, kvq_ref[0, :, width + g * SPAN : width + (g + 1) * SPAN])
            wide = jnp.concatenate([alpha, alpha], axis=1)
            acc_ref[g, lines, :] = acc_ref[g, lines, :] * wide + values

    head_steps(span_ref, rows, chunk_step)

    @pl.when(step == span_ref[SPAN_LAST, 0] - span_ref[SPAN_FIRST, 0])
    def _():
        lane = lax.broadcasted_iota(jnp.int32, (GROUP, 128), 1)
        head = lax.broadcasted_iota(jnp.int32, (GROUP, 128), 0)

        def finish(i, carry):
            at = pl.multiple_of(i * CHUNK, CHUNK)
            lines = pl.ds(pl.multiple_of(i * CHUNK * GROUP, CHUNK * GROUP), CHUNK * GROUP)
            lanes = jnp.zeros((CHUNK, 128), F32)
            for g in range(groups):
                total = jnp.sum(sum_ref[g, lines, :], axis=1, keepdims=True)
                attended = collapse(acc_ref[g, lines, :] / total)
                att_ref[pl.ds(at, CHUNK), g * SPAN : (g + 1) * SPAN] = attended
                lse = max_ref[g, lines, :] + jnp.log(total) * LOG2E
                own_lane = jnp.where(lane == head + g * GROUP, 1.0, 0.0)
                lanes = lanes + jnp.sum(
                    lse.reshape(CHUNK, GROUP, 128) * own_lane[None], axis=1
                )
            lane_ref[pl.ds(at, CHUNK), :] = lanes
            return carry

        lax.fori_loop(0, rows // CHUNK, finish, 0)
        rest = lane_ref[...] * (-1.0 / scale2)
        query = qaug_ref[...].astype(F32)
        for p in range(PIECES):
            piece = rest.astype(BF)
            rest = rest - piece.astype(F32)
            lse_ref[p] = piece
            query = query + dot_nn(piece, place_ref[p])
        qaug_ref[...] = query.astype(BF)


def query_grad_kernel(
    scale2,
    head_scale,
    groups,
    span_ref,
    own_ref,
    other_ref,
    qaug_ref,
    doaug_ref,
    kv_ref,
    bias_ref,
    select_ref,
    dq_ref,
    ds_ref,
    qexp_ref,
    doexp_ref,
    mask_ref,
    dqacc_ref,
):
    step = pl.program_id(0)
    width = groups * SPAN
    rows, keys = own_ref.shape[0], other_ref.shape[1]
    windows = group_windows(groups, dq_ref.shape[1] // (groups * GROUP))

    @pl.when(step == 0)
    def _():
        expand_into(qexp_ref, qaug_ref[...], groups)
        expand_into(doexp_ref, doaug_ref[...], groups)
        dqacc_ref[...] = jnp.zeros(dqacc_ref.shape, F32)

    spread_mask(mask_ref, mask_of(own_ref[...], other_ref[...], False))

    def chunk_step(i):
        at = pl.multiple_of(i * CHUNK, CHUNK)
        lines = pl.ds(pl.multiple_of(i * CHUNK * GROUP, CHUNK * GROUP), CHUNK * GROUP)
        mask = mask_ref[pl.ds(at, CHUNK)]
        waiting = []
        for g in range(groups):
            key_block = kv_ref[0, :, g * SPAN : (g + 1) * SPAN]
            value_block = kv_ref[0, :, width + g * SPAN : width + (g + 1) * SPAN]
            dots = dot_nt(qexp_ref[g, lines, :], key_block)
            grads = dot_nt(doexp_ref[g, lines, :], value_block)
            bias = bias_ref[0, pl.ds(at, CHUNK), g * GROUP : (g + 1) * GROUP, :] + mask
            probs = jnp.exp2(dots * scale2 + bias.reshape(dots.shape))
            grad_scores = probs * grads
            dqacc_ref[g, lines, :] += dot_nn(grad_scores.astype(BF), key_block)
            waiting.append(grad_scores.reshape(CHUNK, GROUP, keys))
            if len(waiting) == 2:
                ds_ref[0, pl.ds(at, CHUNK), (g - 1) * GROUP : (g + 1) * GROUP, :] = (
                    jnp.concatenate(waiting, axis=1).astype(BF)
                )
                waiting = []

    head_steps(span_ref, rows, chunk_step)

    @pl.when(step == span_ref[SPAN_LAST, 0] - span_ref[SPAN_FIRST, 0])
    def _():
        def finish(i, carry):
            at = pl.multiple_of(i * CHUNK, CHUNK)
            lines = pl.ds(pl.multiple_of(i * CHUNK * GROUP, CHUNK * GROUP), CHUNK * GROUP)
            parts = [
                (collapse(dqacc_ref[g, lines, :]) * head_scale).astype(BF) for g in range(groups)
            ]
            dq_ref[pl.ds(at, CHUNK), :] = drop_columns(
                jnp.concatenate(parts, axis=1), select_ref, windows
            )
            return carry

        lax.fori_loop(0, rows // CHUNK, finish, 0)


def phi_grad_kernel(
    span_ref,
    own_ref,
    other_ref,
    line_ref,
    ds_ref,
    tab_ref,
    kw_ref,
    par_ref,
    small_ref,
    pos_ref,
    str_ref,
    dphi_ref,
    phi_ref,
    gs_ref,
    own_acc_ref,
    gkw_ref,
    moment_ref,
    type_ref,
):
    step = pl.program_id(0)
    rows, keys = str_ref.shape
    kernels = tab_ref.shape[1]
    heads = gkw_ref.shape[1]
    blocks = pos_ref.shape[0] // 3
    pair_block = 2 * (span_ref[SPAN_CHIP, 0] + span_ref[SPAN_FIRST, 0] + step)

    @pl.when(step == 0)
    def _():
        gkw_ref[...] = jnp.zeros(gkw_ref.shape, F32)
        moment_ref[...] = jnp.zeros(moment_ref.shape, F32)
        own_acc_ref[...] = jnp.zeros(own_acc_ref.shape, F32)
        pos_ref[...] = jnp.zeros(pos_ref.shape, F32)
        type_ref[...] = jnp.zeros(type_ref.shape, F32)

    def add_types(kind, by_scale, by_shift):
        count = type_ref.shape[1]
        onehot = lax.broadcasted_iota(jnp.int32, (count, LANES), 0).astype(F32) == kind
        type_ref[0] += jnp.where(onehot, by_scale, 0.0)
        type_ref[1] += jnp.where(onehot, by_shift, 0.0)

    own, other = own_ref[...], other_ref[...]
    str_ref[...] = stretched_of(own, other)[3]

    tile = 32
    half_keys = keys // 2

    def pair_step(i, half):
        columns = slice(half * half_keys, (half + 1) * half_keys)
        block = str_ref[pl.ds(pl.multiple_of(i * FEW, FEW), FEW), columns]

        def lows():
            return jnp.concatenate([ds_ref[0, i * FEW + r, :, columns] for r in range(FEW)], axis=1)

        low = lows()
        dphi_ref[...] = dot_nn(kw_ref[...], jnp.concatenate([low] * WEIGHT_PIECES, axis=0))
        partial = [None] * FEW
        for c in range(kernels // tile):
            cs = slice(c * tile, (c + 1) * tile)
            first = jnp.zeros((tile, half_keys), F32)
            second = jnp.zeros((tile, half_keys), F32)
            for r in range(FEW):
                spot = slice(r * half_keys, (r + 1) * half_keys)
                away = jnp.broadcast_to(block[r : r + 1], (tile, half_keys)) - tab_ref[0, cs, :]
                phi = jnp.exp2(away * away * tab_ref[3, cs, :])
                phi_ref[cs, spot] = phi.astype(BF)
                moved = dphi_ref[cs, spot] * phi * away
                first = first + moved
                second = second + moved * away
                term = jnp.sum(moved.reshape(tile // 8, 8, half_keys), axis=0)
                partial[r] = term if c == 0 else partial[r] + term
            moment_ref[0, cs, :] += first
            moment_ref[1, cs, :] += second
        lines = [jnp.sum(partial[r], axis=0, keepdims=True) for r in range(FEW)]
        gs_ref[pl.ds(pl.multiple_of(i * FEW, FEW), FEW), columns] = jnp.concatenate(lines, axis=0)
        gkw_ref[...] += dot_nt(phi_ref[...], lows())

    def skipped(i, half):
        columns = slice(half * half_keys, (half + 1) * half_keys)
        gs_ref[pl.ds(pl.multiple_of(i * FEW, FEW), FEW), columns] = jnp.zeros((FEW, half_keys), F32)

    kernel_steps(span_ref, rows, pair_step, skipped)

    delta, dist, scales, _ = stretched_of(own, other)
    grad = -gs_ref[...]
    by_scale = grad * dist
    pull = grad * scales / dist
    terms = [pull * delta[0], pull * delta[1], pull * delta[2], by_scale * other[3:4, :], grad]
    for k, term in enumerate(terms):
        own_acc_ref[k] += term[:, :128] + term[:, 128:]
    for half in range(2):
        part = slice(half * LANES, (half + 1) * LANES)
        for k in range(3):
            spot = pl.ds(k * blocks + pair_block + half, 1)
            pos_ref[spot, :] += -jnp.sum(terms[k][:, part], axis=0, keepdims=True)
        add_types(
            other[8:9, part],
            jnp.sum(by_scale[:, part] * own[:, 3:4], axis=0, keepdims=True),
            jnp.sum(grad[:, part], axis=0, keepdims=True),
        )

    @pl.when(step == span_ref[SPAN_LAST, 0] - span_ref[SPAN_FIRST, 0])
    def _():
        lane = lax.broadcasted_iota(jnp.int32, (rows, LANES), 1)
        total = jnp.zeros((rows, LANES), F32)
        for k in range(5):
            column = jnp.sum(own_acc_ref[k], axis=1, keepdims=True)
            total = total + jnp.where(lane == k, column, 0.0)
        turned = jnp.transpose(total)
        own_block = 2 * (span_ref[SPAN_CHIP, 0] + len(SLOTS[0]) // 2) + span_ref[SPAN_CORE, 0]
        for k in range(3):
            pos_ref[pl.ds(k * blocks + own_block, 1), :] += turned[k : k + 1, :]
        add_types(line_ref[8:9, :], turned[3:4, :], turned[4:5, :])

        par = par_ref[...]
        by_weight = gkw_ref[...] * par[:, heads : heads + 1]
        plain = jnp.sum(by_weight * par[:, :heads], axis=1, keepdims=True)
        by_mean = jnp.sum(moment_ref[0], axis=1, keepdims=True)
        by_width = jnp.sum(moment_ref[1], axis=1, keepdims=True) - plain
        columns = [by_mean, by_width * par[:, heads + 1 : heads + 2]]
        low, high = slice(0, LANES), slice(LANES, 2 * LANES)
        for part in (low, high):
            for k in range(2):
                columns.append(jnp.sum(type_ref[k, part, :], axis=1, keepdims=True))
        wide = jnp.concatenate([by_weight, jnp.zeros((LANES, LANES - heads), F32)], axis=1)
        for k, column in enumerate(columns):
            wide = wide + jnp.where(lane == heads + k, column, 0.0)
        small_ref[...] = wide


def middle_kernel(
    groups,
    tile,
    flat_ref,
    tok_ref,
    att_ref,
    lse_ref,
    ln_ref,
    cot_ref,
    wout_hbm,
    wup_hbm,
    wdown_hbm,
    select_ref,
    place_ref,
    sum_ref,
    into_ref,
    out_ref,
    gmix_ref,
    doaug_ref,
    payload_ref,
    attlow_ref,
    normed_ref,
    mine_ref,
    theirs_ref,
    lngrad_ref,
    wout_ref,
    wup_ref,
    wdown_ref,
    down_ref,
    back_ref,
    wout_sem,
    tile_sems,
):
    rows, model_width = tok_ref.shape
    width = groups * SPAN
    windows = group_windows(groups, model_width // (groups * GROUP))
    tiles = wup_ref.shape[1] // tile
    piece = mine_ref.shape[3]
    core = flat_ref[0] % 2

    def tile_copies(t):
        spot = pl.ds(pl.multiple_of(t * tile, LANES), tile)
        return (
            pltpu.make_async_copy(wup_hbm.at[:, spot], wup_ref.at[:, spot], tile_sems.at[0, t]),
            pltpu.make_async_copy(wdown_hbm.at[spot, :], wdown_ref.at[spot, :], tile_sems.at[1, t]),
        )

    first = pltpu.make_async_copy(wout_hbm, wout_ref, wout_sem)
    first.start()
    for t in range(tiles):
        for copy in tile_copies(t):
            copy.start()

    gain, shift = ln_ref[0:1, :], ln_ref[1:2, :]
    cotangent = cot_ref[...]
    attended = att_ref[...]
    attended_low = drop_columns(attended.astype(BF), select_ref, windows)
    attlow_ref[...] = attended_low
    first.wait()
    mixed = tok_ref[...].astype(F32) + dot_nn(attended_low, wout_ref[...])
    normal, slope = norm_parts(mixed)
    normed_ref[...] = (normal * gain + shift).astype(BF)
    down_ref[...] = mixed
    back_ref[...] = jnp.zeros(back_ref.shape, F32)

    def step(t, carry):
        for copy in tile_copies(t):
            copy.wait()
        spot = pl.ds(pl.multiple_of(t * tile, LANES), tile)
        up = dot_nn(normed_ref[...], wup_ref[:, spot])
        grad_hidden = dot_nt(cotangent, wdown_ref[spot, :])
        square = up * up
        bent = jnp.tanh(GELU_SLOPE * (up * (1.0 + GELU_CUBE * square)))
        gate = 0.5 * (1.0 + bent)
        inner = GELU_SLOPE * (1.0 + 3.0 * GELU_CUBE * square)
        hidden = (up * gate).astype(BF)
        grad_up = (grad_hidden * (gate + 0.5 * up * (1.0 - bent * bent) * inner)).astype(BF)
        for kind, value in enumerate((grad_up, hidden)):
            for q in range(tile // piece):
                part = value[:, q * piece : (q + 1) * piece]
                at = t * (tile // piece // 2) + q // 2

                @pl.when(core == q % 2)
                def _():
                    mine_ref[kind, at] = part

                @pl.when(core != q % 2)
                def _():
                    theirs_ref[kind, at] = part

        down_ref[...] += dot_nn(hidden, wdown_ref[spot, :])
        back_ref[...] += dot_nt(grad_up, wup_ref[:, spot])
        return carry

    lax.fori_loop(0, tiles, step, 0)
    out_ref[...] = down_ref[...].astype(BF)
    back, by_gain, by_shift = norm_back(back_ref[...], normal, slope, gain)
    lngrad_ref[...] = jnp.concatenate([by_gain, by_shift], axis=0)
    grad_mixed = cotangent.astype(F32) + back
    gmix_ref[...] = grad_mixed
    grad_low = grad_mixed.astype(BF)
    grad_attended = dot_nt(grad_low, wout_ref[...]).astype(BF)
    padded = pad_columns(grad_attended, select_ref, windows).astype(F32)
    high, low = split(padded * attended, 2)
    delta = dot_nn(high, sum_ref[...]) + dot_nn(low, sum_ref[...])
    pieces = split(-delta, PIECES)
    tail = jnp.zeros((rows, 2 * LANES), F32)
    for p in range(PIECES):
        padded = padded + dot_nn(pieces[p], place_ref[p])
        tail = tail + dot_nn(lse_ref[p], into_ref[p]) + dot_nn(pieces[p], into_ref[PIECES + p])
    doaug_ref[...] = padded.astype(BF)
    payload_ref[:, :model_width] = grad_low
    payload_ref[:, model_width:] = tail.astype(BF)


def weight_grads_kernel(
    ka_count,
    flat_ref,
    mine_ref,
    came_ref,
    normed_ref,
    normed_came_ref,
    cot_ref,
    cot_came_ref,
    attlow_ref,
    attlow_came_ref,
    payload_ref,
    payload_came_ref,
    up_kept_ref,
    up_sent_ref,
    rest_kept_ref,
    rest_sent_ref,
    payload_out_ref,
    product_ref,
):
    flat = flat_ref[0]
    core, bit, side = flat % 2, (flat // 2) % 2, (flat // ka_count) % 2
    model_width = normed_ref.shape[1]
    rows = up_kept_ref.shape[1]
    half = model_width // 2
    slices = up_kept_ref.shape[0] * 2
    out_rows = model_width // ka_count
    normed = jnp.concatenate([normed_ref[...], normed_came_ref[...]], axis=0)
    cotangent = jnp.concatenate([cot_ref[...], cot_came_ref[...]], axis=0)

    def columns(which):
        return pl.ds(pl.multiple_of(which * half, LANES), half)

    def step(m, carry):
        both = jnp.concatenate([mine_ref[0, m], came_ref[0, m]], axis=0)
        value = dot_tn(both, normed).astype(BF)

        @pl.when(m % 2 == bit)
        def _():
            up_kept_ref[m // 2] = value

        @pl.when(m % 2 != bit)
        def _():
            up_sent_ref[m // 2] = value

        both = jnp.concatenate([mine_ref[1, m], came_ref[1, m]], axis=0)
        product_ref[:rows, :] = dot_tn(both, cotangent)
        rest_kept_ref[m, :rows, :] = product_ref[:rows, columns(side)].astype(BF)
        rest_sent_ref[m, :rows, :] = product_ref[:rows, columns(1 - side)].astype(BF)
        return carry

    lax.fori_loop(0, slices, step, 0)
    grads = jnp.concatenate(
        [payload_ref[:, :model_width], payload_came_ref[:, :model_width]], axis=0
    )
    attended = jnp.concatenate([attlow_ref[...], attlow_came_ref[...]], axis=0)
    product_ref[...] = dot_tn(grads, attended)

    def out_step(m, carry):
        spot = pl.ds(pl.multiple_of((2 * m + core) * out_rows, 8), out_rows)
        rest_kept_ref[m, rows:, :] = product_ref[spot, columns(side)].astype(BF)
        rest_sent_ref[m, rows:, :] = product_ref[spot, columns(1 - side)].astype(BF)
        return carry

    lax.fori_loop(0, slices, out_step, 0)
    payload_out_ref[...] = payload_ref[...]


def qkv_grads_kernel(
    ka_count,
    split_at,
    flat_ref,
    dq_ref,
    dq_came_ref,
    dkv_ref,
    dkv_came_ref,
    normed_ref,
    a_kept_ref,
    a_sent_ref,
    b_kept_ref,
    b_sent_ref,
    product_ref,
):
    flat = flat_ref[0]
    core, bit, side = flat % 2, (flat // 2) % 2, (flat // ka_count) % 2
    model_width = normed_ref.shape[1]
    slices = a_kept_ref.shape[0] * 2
    rows = 3 * model_width // ka_count
    half = (model_width - split_at) // 2
    dq = jnp.concatenate([dq_ref[...], dq_came_ref[...]], axis=0)
    product_ref[:model_width, :] = dot_tn(dq, normed_ref[...])
    for part in range(2):
        spot = slice(part * model_width, (part + 1) * model_width)
        both = jnp.concatenate([dkv_ref[:, spot], dkv_came_ref[:, spot]], axis=0)
        product_ref[(part + 1) * model_width : (part + 2) * model_width, :] = dot_tn(
            both, normed_ref[...]
        )

    def step(m, carry):
        spot = pl.ds(pl.multiple_of((2 * m + core) * rows, 8), rows)
        value = product_ref[spot, :split_at].astype(BF)

        @pl.when(m % 2 == bit)
        def _():
            a_kept_ref[m // 2] = value

        @pl.when(m % 2 != bit)
        def _():
            a_sent_ref[m // 2] = value

        for which, ref in ((side, b_kept_ref), (1 - side, b_sent_ref)):
            at = pl.ds(pl.multiple_of(split_at + which * half, LANES), half)
            ref[m] = product_ref[spot, at].astype(BF)
        return carry

    lax.fori_loop(0, slices, step, 0)


def first_norm_kernel(
    tok_ref, ln_ref, dq_ref, dkv_ref, w_ref, gmix_ref, grad_ref, lngrad_ref
):
    model_width = tok_ref.shape[1]
    grad = dot_nt(dq_ref[...], w_ref[:, :model_width])
    for part in range(2):
        spot = slice(part * model_width, (part + 1) * model_width)
        after = slice((part + 1) * model_width, (part + 2) * model_width)
        grad = grad + dot_nt(dkv_ref[:, spot], w_ref[:, after])
    normal, slope = norm_parts(tok_ref[...].astype(F32))
    back, by_gain, by_shift = norm_back(grad, normal, slope, ln_ref[0:1, :])
    grad_ref[...] = gmix_ref[...] + back
    lngrad_ref[...] = jnp.concatenate([by_gain, by_shift], axis=0)


def key_grad_kernel(
    scale2,
    head_scale,
    groups,
    model_width,
    span_ref,
    own_ref,
    other_ref,
    kv_ref,
    q_ref,
    *refs,
):
    payload_refs, refs = refs[:14], refs[14:]
    wout_ref, select_ref, place_ref, bias_ref, dkv_ref, kexp_ref, vexp_ref, *refs = refs
    mask_ref, qb_ref, dob_ref, dk_ref, dv_ref, both_ref = refs
    step = pl.program_id(0)
    width = groups * SPAN
    rows = own_ref.shape[0]
    windows = group_windows(groups, model_width // (groups * GROUP))

    @pl.when(step == 0)
    def _():
        expand_into(kexp_ref, kv_ref[0, :, :width], groups)
        expand_into(vexp_ref, kv_ref[0, :, width:], groups)
        dk_ref[...] = jnp.zeros(dk_ref.shape, F32)
        dv_ref[...] = jnp.zeros(dv_ref.shape, F32)

    fetch(span_ref, payload_refs, both_ref)
    payload = both_ref[...]
    tail = payload[:, model_width:]
    grads = dot_nt(payload[:, :model_width], wout_ref[...]).astype(BF)
    grads = pad_columns(grads, select_ref, windows).astype(F32)
    grads = (grads + dot_nn(tail, place_ref[1])).astype(BF)
    shifts = dot_nn(tail, place_ref[0])
    for k, spot in enumerate(spots_of(span_ref, rows)):
        own_part = slice(k * rows, (k + 1) * rows)
        dob_ref[spot, :] = grads[own_part]
        qb_ref[spot, :] = (q_ref[0, spot, :].astype(F32) + shifts[own_part]).astype(BF)
    spread_mask(mask_ref, mask_of(own_ref[...], other_ref[...], True))

    def chunk_step(i):
        at = pl.multiple_of(i * CHUNK, CHUNK)
        lines = pl.ds(pl.multiple_of(i * CHUNK * GROUP, CHUNK * GROUP), CHUNK * GROUP)
        mask = mask_ref[pl.ds(at, CHUNK)]
        for g in range(groups):
            query_block = qb_ref[:, g * SPAN : (g + 1) * SPAN]
            grad_block = dob_ref[:, g * SPAN : (g + 1) * SPAN]
            dots = dot_nt(kexp_ref[g, lines, :], query_block)
            grads = dot_nt(vexp_ref[g, lines, :], grad_block)
            bias = bias_ref[0, pl.ds(at, CHUNK), g * GROUP : (g + 1) * GROUP, :] + mask
            probs = jnp.exp2(dots * scale2 + bias.reshape(dots.shape))
            grad_scores = (probs * grads).astype(BF)
            dk_ref[g, lines, :] += dot_nn(grad_scores, query_block)
            dv_ref[g, lines, :] += dot_nn(probs.astype(BF), grad_block)

    head_steps(span_ref, rows, chunk_step)

    @pl.when(step == span_ref[SPAN_LAST, 0] - span_ref[SPAN_FIRST, 0])
    def _():
        def finish(i, carry):
            at = pl.multiple_of(i * CHUNK, CHUNK)
            lines = pl.ds(pl.multiple_of(i * CHUNK * GROUP, CHUNK * GROUP), CHUNK * GROUP)
            for part, (ref, scale) in enumerate(((dk_ref, head_scale), (dv_ref, 1.0))):
                parts = [(collapse(ref[g, lines, :]) * scale).astype(BF) for g in range(groups)]
                dkv_ref[pl.ds(at, CHUNK), part * model_width : (part + 1) * model_width] = (
                    drop_columns(jnp.concatenate(parts, axis=1), select_ref, windows)
                )
            return carry

        lax.fori_loop(0, rows // CHUNK, finish, 0)


def fixed(shape):
    return pl.BlockSpec(shape, lambda j, span: (0,) * len(shape), pipeline_mode=pl.Buffered(1))


def pair_at(j, span):
    return jnp.minimum(span[SPAN_FIRST, 0] + j, span[SPAN_LAST, 0])


def moving(shape, rank_at=0, last=0):
    def index(j, span):
        at = [0] * len(shape)
        at[rank_at] = pair_at(j, span)
        if last:
            at[-1] = last
        return tuple(at)

    return pl.BlockSpec(shape, index)


def while_inside(kernel, extra):
    def body(span_ref, *refs):
        @pl.when(pl.program_id(0) <= span_ref[SPAN_LAST, 0] - span_ref[SPAN_FIRST, 0])
        def _():
            kernel(span_ref, *refs[extra:])

    return body


def call(kernel, steps, in_specs, out_specs, out_shapes, scratch, flops, name, after=()):
    inner = pl.pallas_call(
        while_inside(kernel, len(after)),
        grid_spec=pltpu.PrefetchScalarGridSpec(
            num_scalar_prefetch=1,
            grid=(steps,),
            in_specs=[pl.BlockSpec(memory_space=pl.ANY)] * len(after) + in_specs,
            out_specs=out_specs,
            scratch_shapes=scratch,
        ),
        out_shape=out_shapes,
        compiler_params=pltpu.CompilerParams(
            dimension_semantics=("arbitrary",), vmem_limit_bytes=56 * 1024 * 1024
        ),
        cost_estimate=pl.CostEstimate(flops=flops, bytes_accessed=20_000_000, transcendentals=0),
        name=name,
    )
    return lambda span, *operands: inner(span, *after, *operands)


def shape_of(shape, dtype=F32):
    return jax.ShapeDtypeStruct(shape, dtype)


def once(kernel, operands, out_shapes, scratch, flops, name, spaces=()):
    spaces = dict(spaces)

    def whole(shape):
        return pl.BlockSpec(shape, lambda j: (0,) * len(shape), pipeline_mode=pl.Buffered(1))

    return pl.pallas_call(
        kernel,
        grid=(1,),
        in_specs=[
            pl.BlockSpec(memory_space=spaces[k]) if k in spaces else whole(x.shape)
            for k, x in enumerate(operands)
        ],
        out_specs=[whole(x.shape) for x in out_shapes],
        out_shape=out_shapes,
        scratch_shapes=scratch,
        compiler_params=pltpu.CompilerParams(vmem_limit_bytes=56 * 1024 * 1024),
        cost_estimate=pl.CostEstimate(flops=flops, bytes_accessed=5_000_000, transcendentals=0),
        name=name,
    )(*operands)


def on_device(
    tokens,
    positions,
    item_of_atom,
    item_lengths,
    atom_types,
    key_mask,
    ln1_gain,
    ln1_bias,
    w_qkv,
    kernel_means,
    kernel_widths,
    kernel_weight,
    type_scale,
    type_shift,
    w_out,
    ln2_gain,
    ln2_bias,
    w_up,
    w_down,
    out_cotangent,
):
    own_rows, model_width = tokens.shape
    assert own_rows == LANES
    kernels, heads = kernel_weight.shape
    head_size = model_width // heads
    head_scale = head_size ** (-0.5)
    scale2 = head_scale * LOG2E
    groups = heads // GROUP
    width = groups * SPAN
    ff_width = w_up.shape[1]
    ka_count = lax.axis_size("ka")
    flat = lax.axis_index("pb") * ka_count + lax.axis_index("ka")
    flat_array = flat.astype(jnp.int32).reshape(1)
    reach = (PROT_LEN + own_rows - 2) // own_rows
    chips = (reach + 1) // 2
    pairs = 2 * chips + 1
    assert pairs == len(SLOTS[0])
    keys = 2 * own_rows
    atoms = positions.shape[1]
    atoms_blocks = atoms // LANES
    types = type_scale.shape[0]
    order = tuple(range(bits_of("ka") - 1))

    window = Window(tokens)
    cotangent_came = core_flip(out_cotangent)

    select = select_table(head_size)
    place = place_table(heads, head_size)
    into_tail, out_of_tail = tail_tables(heads, head_size)
    type_tiles = -(-types // LANES)
    tables = jnp.pad(
        jnp.stack([type_scale, type_shift]), ((0, 0), (0, type_tiles * LANES - types))
    )
    tables = tables.reshape(2, type_tiles, LANES).swapaxes(0, 1).reshape(2 * type_tiles, LANES)
    lengths = jnp.pad(item_lengths, (0, -item_lengths.shape[0] % LANES)).reshape(-1, LANES)
    span, other, own, own_line, tabs, grad_weights, weights_turned, par = once(
        functools.partial(side_kernel, atoms_blocks),
        (
            flat_array,
            positions,
            item_of_atom.reshape(-1, LANES),
            key_mask.reshape(-1, LANES),
            atom_types.reshape(-1, LANES),
            lengths,
            tables,
            kernel_means.reshape(1, LANES),
            kernel_widths.reshape(1, LANES),
            kernel_weight,
        ),
        [
            shape_of((SPAN_ROWS, LANES), jnp.int32),
            shape_of((SIDE, pairs * keys)),
            shape_of((own_rows, LANES)),
            shape_of((SIDE, LANES)),
            shape_of((4, kernels, LANES)),
            shape_of((kernels, WEIGHT_PIECES * heads), BF),
            shape_of((heads, kernels), BF),
            shape_of((LANES, LANES)),
        ],
        [],
        1_000_000_000,
        "sides",
        {0: pltpu.SMEM},
    )

    own_spec = fixed((own_rows, LANES))
    other_spec = moving((SIDE, keys), 1)
    bias_spec = moving((1, own_rows, heads, keys))
    bias = call(
        bias_kernel,
        pairs,
        [own_spec, other_spec, fixed((4, kernels, LANES)), fixed((heads, kernels))],
        bias_spec,
        shape_of((pairs, own_rows, heads, keys)),
        [pltpu.VMEM((own_rows, keys), F32)],
        30_000_000_000,
        "pair_bias",
        after=(window.before, window.after),
    )(span, own, other, tabs, weights_turned)
    token_blocks = window.finish()

    ln1 = jnp.stack([ln1_gain, ln1_bias])
    ln2 = jnp.stack([ln2_gain, ln2_bias])
    expanded = pltpu.VMEM((groups, own_rows * GROUP, SPAN), BF)
    summed = pltpu.VMEM((groups, own_rows * GROUP, SPAN), F32)
    mask_scratch = pltpu.VMEM((own_rows, GROUP, keys), F32)
    line_scratch = pltpu.VMEM((groups, own_rows * GROUP, LANES), F32)
    attended, q_aug, lse_pieces, normed_chip, kvq = call(
        functools.partial(forward_kernel, scale2, groups, chips),
        pairs,
        [own_spec, other_spec]
        + [fixed((own_rows, model_width))] * 14
        + [
            fixed((2, model_width)),
            fixed((model_width, 3 * model_width)),
            fixed(select.shape),
            fixed((1, width)),
            fixed(place.shape),
            bias_spec,
        ],
        [
            fixed((own_rows, width)),
            fixed((own_rows, width)),
            fixed((PIECES, own_rows, LANES)),
            fixed((keys, model_width)),
            moving((1, keys, 3 * width)),
        ],
        [
            shape_of((own_rows, width)),
            shape_of((own_rows, width), BF),
            shape_of((PIECES, own_rows, LANES), BF),
            shape_of((keys, model_width), BF),
            shape_of((pairs, keys, 3 * width), BF),
        ],
        [
            expanded,
            mask_scratch,
            line_scratch,
            line_scratch,
            summed,
            pltpu.VMEM((own_rows, LANES), F32),
            pltpu.VMEM((keys, model_width), BF),
        ],
        25_000_000_000,
        "attention_forward",
    )(
        span,
        own,
        other,
        *token_blocks,
        ln1,
        w_qkv,
        select,
        ones_row(heads, head_size),
        place,
        bias,
    )

    tile = 3 * LANES
    assert ff_width % tile == 0 and tile % (2 * ff_width // ka_count) == 0
    row_shape = shape_of((own_rows, model_width), BF)
    slices = ka_count // 2
    up_rows, out_rows = ff_width // ka_count, model_width // ka_count
    pieces = shape_of((2, slices, own_rows, up_rows), BF)
    block_out, grad_mixed, do_aug, payload, attended_low, normed_second, *parts, ln2_grads = once(
        functools.partial(middle_kernel, groups, tile),
        (
            flat_array,
            tokens,
            attended,
            lse_pieces,
            ln2,
            out_cotangent,
            w_out,
            w_up,
            w_down,
            select,
            place,
            head_sum_table(heads),
            into_tail,
        ),
        [
            row_shape,
            shape_of((own_rows, model_width)),
            shape_of((own_rows, width), BF),
            shape_of((own_rows, model_width + 2 * LANES), BF),
            row_shape,
            row_shape,
            pieces,
            pieces,
            shape_of((2, model_width)),
        ],
        [
            pltpu.VMEM((model_width, model_width), BF),
            pltpu.VMEM((model_width, ff_width), BF),
            pltpu.VMEM((ff_width, model_width), BF),
            pltpu.VMEM((own_rows, model_width), F32),
            pltpu.VMEM((own_rows, model_width), F32),
            pltpu.SemaphoreType.DMA,
            pltpu.SemaphoreType.DMA((2, ff_width // tile)),
        ],
        10_000_000_000,
        "feed_forward",
        {0: pltpu.SMEM, 6: pl.ANY, 7: pl.ANY, 8: pl.ANY},
    )
    came = [core_flip(x) for x in (parts[1], normed_second, attended_low, payload)]
    half = model_width // 2
    up_kept, up_sent, rest_kept, rest_sent, payload_now = once(
        functools.partial(weight_grads_kernel, ka_count),
        (
            flat_array,
            parts[0],
            came[0],
            normed_second,
            came[1],
            out_cotangent,
            cotangent_came,
            attended_low,
            came[2],
            payload,
            came[3],
        ),
        [shape_of((slices // 2, up_rows, model_width), BF)] * 2
        + [shape_of((slices, up_rows + out_rows, half), BF)] * 2
        + [shape_of(payload.shape, BF)],
        [pltpu.VMEM((model_width, model_width), F32)],
        5_000_000_000,
        "weight_gradients",
        {0: pltpu.SMEM},
    )
    window = Window(payload_now, came[3])
    up_sum, rest_sum = Slices(up_kept, up_sent, order), Columns(rest_kept, rest_sent, order)

    dq, grad_scores = call(
        functools.partial(query_grad_kernel, scale2, head_scale, groups),
        pairs,
        [
            own_spec,
            other_spec,
            fixed((own_rows, width)),
            fixed((own_rows, width)),
            moving((1, keys, 2 * width)),
            bias_spec,
            fixed(select.shape),
        ],
        [fixed((own_rows, model_width)), moving((1, own_rows, heads, keys))],
        [row_shape, shape_of((pairs, own_rows, heads, keys), BF)],
        [expanded, expanded, mask_scratch, summed],
        22_000_000_000,
        "query_gradients",
        after=(up_sum.sent, rest_sum.sent),
    )(span, own, other, q_aug, do_aug, kvq, bias, select)
    dq_came = core_flip(dq)
    up_sum.step()
    rest_sum.step()

    pos_blocks = atoms_blocks + 4 * chips
    small, pos_part = call(
        phi_grad_kernel,
        pairs,
        [
            own_spec,
            other_spec,
            fixed((SIDE, LANES)),
            moving((1, own_rows, heads, keys)),
            fixed((4, kernels, LANES)),
            fixed((kernels, WEIGHT_PIECES * heads)),
            fixed((LANES, LANES)),
        ],
        [fixed((LANES, LANES)), fixed((3 * pos_blocks, LANES))],
        [shape_of((LANES, LANES)), shape_of((3 * pos_blocks, LANES))],
        [
            pltpu.VMEM((own_rows, keys), F32),
            pltpu.VMEM((kernels, FEW * own_rows), F32),
            pltpu.VMEM((kernels, FEW * own_rows), BF),
            pltpu.VMEM((own_rows, keys), F32),
            pltpu.VMEM((5, own_rows, LANES), F32),
            pltpu.VMEM((kernels, heads), F32),
            pltpu.VMEM((2, kernels, LANES), F32),
            pltpu.VMEM((2, 2 * LANES, LANES), F32),
        ],
        45_000_000_000,
        "kernel_gradients",
        after=(*window.first(), up_sum.sent, rest_sum.sent),
    )(span, own, other, own_line, grad_scores, tabs, grad_weights, par)
    payload_blocks = window.finish()
    up_sum.step()
    rest_sum.step()

    dkv = call(
        functools.partial(key_grad_kernel, scale2, head_scale, groups, model_width),
        pairs,
        [
            own_spec,
            other_spec,
            pl.BlockSpec(
                (1, own_rows, 2 * width),
                lambda j, span: (chips, span[SPAN_CORE, 0], 0),
                pipeline_mode=pl.Buffered(1),
            ),
            moving((1, keys, width), 0, 2),
        ]
        + [fixed((own_rows, model_width + 2 * LANES))] * 14
        + [
            fixed((model_width, model_width)),
            fixed(select.shape),
            fixed(out_of_tail.shape),
            bias_spec,
        ],
        fixed((own_rows, 2 * model_width)),
        shape_of((own_rows, 2 * model_width), BF),
        [
            expanded,
            expanded,
            mask_scratch,
            pltpu.VMEM((keys, width), BF),
            pltpu.VMEM((keys, width), BF),
            summed,
            summed,
            pltpu.VMEM((keys, model_width + 2 * LANES), BF),
        ],
        28_000_000_000,
        "key_gradients",
        after=(up_sum.sent, rest_sum.sent),
    )(span, own, other, kvq, kvq, *payload_blocks, w_out, select, out_of_tail, bias)

    dkv_came = core_flip(dkv)
    split_at = model_width // 3
    qkv_rows = 3 * model_width // ka_count
    qkv_half = (model_width - split_at) // 2
    a_kept, a_sent, b_kept, b_sent = once(
        functools.partial(qkv_grads_kernel, ka_count, split_at),
        (flat_array, dq, dq_came, dkv, dkv_came, normed_chip),
        [shape_of((slices // 2, qkv_rows, split_at), BF)] * 2
        + [shape_of((slices, qkv_rows, qkv_half), BF)] * 2,
        [pltpu.VMEM((3 * model_width, model_width), F32)],
        3_000_000_000,
        "qkv_gradients",
        {0: pltpu.SMEM},
    )
    sums = [
        Slices(a_kept, a_sent, order),
        Columns(b_kept, b_sent, order),
        up_sum,
        rest_sum,
    ]
    grad_tokens, ln1_grads = once(
        first_norm_kernel,
        (tokens, ln1, dq, dkv, w_qkv, grad_mixed),
        [shape_of((own_rows, model_width)), shape_of((2, model_width))],
        [],
        2_000_000_000,
        "first_norm",
    )
    norm_rows = [x.reshape(-1, LANES) for x in (ln1_grads, ln2_grads)]
    joined = sum_everywhere(jnp.concatenate([small, *norm_rows, pos_part], axis=0))
    up_sum.step()
    rest_sum.step()
    a_total, b_total, up_total, rest_total = [part.result() for part in sums]

    small = joined[:LANES]
    count = norm_rows[0].shape[0]
    ln1_sum = joined[LANES : LANES + count].reshape(2, model_width)
    ln2_sum = joined[LANES + count : LANES + 2 * count].reshape(2, model_width)
    pos_rows = joined[LANES + 2 * count :].reshape(3, pos_blocks, LANES)
    grad_positions = lax.dynamic_index_in_dim(pos_rows, flat + 2 * chips, 1, keepdims=False)
    type_columns = small[:, heads + 2 : heads + 6]
    by_type = jnp.concatenate([type_columns[:, :2], type_columns[: types - LANES, 2:]], axis=0)
    qkv_total = jnp.concatenate([a_total, b_total], axis=1)
    return (
        block_out,
        grad_tokens,
        grad_positions,
        ln1_sum[0],
        ln1_sum[1],
        qkv_total.T.astype(F32),
        small[:, heads],
        small[:, heads + 1],
        small[:, :heads],
        by_type[:, 0],
        by_type[:, 1],
        rest_total[up_rows:].T.astype(F32),
        ln2_sum[0],
        ln2_sum[1],
        up_total.T.astype(F32),
        rest_total[:up_rows].astype(F32),
    )


def solution(mesh):
    rows = P(MESH, None)
    in_specs = (rows,) + (P(),) * 18 + (rows,)
    out_specs = (
        rows,
        rows,
        P(None, MESH),
        P(),
        P(),
        P(None, "ka"),
        P(),
        P(),
        P(),
        P(),
        P(),
        P(None, "ka"),
        P(),
        P(),
        P(None, "ka"),
        P("ka", None),
    )
    return jax.shard_map(
        on_device, mesh=mesh, in_specs=in_specs, out_specs=out_specs, check_vma=False
    )
```

time: 539 us -> 356 us (0.66); the launches traced: 547 us -> 352 us
  waiting for transfers between devices: 305 us -> 77.7 us
  starting transfers between devices: 47.5 us -> 130 us
  Pallas kernels: 65.7 us -> 116 us
  matrix products: 37.1 us -> 0 us
  local copies, waits for them, and re-layouts: 48.1 us -> 19.2 us
  between operations: 18.9 us -> 1.48 us
  other arithmetic: 25.2 us -> 8.25 us
    reduce_scatter x4 -> x0, waiting for transfers between devices: 191 us -> none  [over_ka(): lax.psum_scatter(values.astype(BF), 'ka', scatter_dimension=1, tiled=True)]
    ppermute x0 -> x31, starting transfers between devices: none -> 75.6 us  [the longest x23 61.6 us: flip_bit(): return lax.ppermute(block, axis, [(i, i ^ 1 << bit) for i in devices])]
    ppermute x0 -> x31, waiting for transfers between devices: none -> 75 us  [the longest x23 72.4 us: flip_bit(): return lax.ppermute(block, axis, [(i, i ^ 1 << bit) for i in devices])]
    psum x2 -> x0, waiting for transfers between devices: 62.9 us -> none  [the longest x1 39 us: on_device(): totals = tuple((lax.psum(piece, 'pb').astype(F32) for piece in pieces))]
    pallas_call x4 -> x10, Pallas kernels: 65.7 us -> 116 us  [the longest x5 71.1 us: call(): return lambda span, *operands: inner(span, *after, *operands)]
    ppermute x12 -> x4, waiting for transfers between devices: 50.6 us -> 1.33 us  [shifted(): return lax.ppermute(block, axis, route)]
    dot_general x11 -> x0, matrix products: 37.1 us -> none  [the longest x7 23.9 us: dot_nn(): lax.dot_general(left, right, (((1,), (0,)), ((), ())), preferred_element_...]
    unnamed x133 -> x103, local copies, waits for them, and re-layouts: 24.5 us -> 8.11 us
  transfers between devices with their start and end apart: 20 -> 55, of which waited for: 10 -> 18; matrix products, arithmetic and copies ran while one was open for 15% -> 5% of each run, Pallas kernels for 9% -> 13%
where the time goes in v2:
time: 356 us; the launch traced here: 352 us
  starting transfers between devices  130 us (37%)
  Pallas kernels  116 us (33%)
  waiting for transfers between devices  77.7 us (22%)
  local copies, waits for them, and re-layouts  19.2 us (5%)
  other arithmetic  8.25 us (2%)
    ppermute x23, waiting for transfers between devices, flip_bit(): return lax.ppermute(block, axis, [(i, i ^ 1 << bit) for i in devices])  72.4 us
    pallas_call x5, Pallas kernels, call(): return lambda span, *operands: inner(span, *after, *operands)  71.1 us
    ppermute x23, starting transfers between devices, flip_bit(): return lax.ppermute(block, axis, [(i, i ^ 1 << bit) for i in devices])  61.6 us
    ppermute x4, starting transfers between devices, shifted(): return lax.ppermute(block, axis, route)  45 us
    pallas_call x5, Pallas kernels, once(): pl.pallas_call(kernel, grid=(1,), in_specs=[pl.BlockSpec(memory_space=spa...  44.5 us
    ppermute x20, starting transfers between devices, core_flip(): return lax.ppermute(block, MESH, [(i, i ^ 1) for i in devices])  9.35 us
    unnamed x103, local copies, waits for them, and re-layouts  8.11 us
    ppermute x4, starting transfers between devices, finish(): lax.ppermute(x, MESH, [(i, i ^ 2) for i in devices])  7.43 us
  transfers between devices with their start and end apart: 55, of which 18 were waited for; matrix products, arithmetic and copies ran while one was open for 5% of the time, Pallas kernels for 13%

profile of v2, /device:TPU:0, one launch (start us, length us, event | category | flops | bytes accessed | tf_op | source)
XLA Modules:
  0.0 352.1 jit_solution(4800561409951431777)
XLA Ops:
  0.6 4.9 %collective-permute-start.1 = (bf16[128,768]{1,0:T(8,128)(2,1)}, bf16[128,768]{1,0:T(8,128)(2,1)S(1)}, u32[]{:S(2)}, u32[]{:S(2)}) collective-permute-start(bf16[128,768]{1,0:T(8,128)(2,1)} %tok_ref.3), channel_id=1, source_target_pairs={{0,4},{1,5},{2,6},{3,7},{4,8},{5,9},{6,10},{7,11},{8,12},{9,13},{1... | collective-permute-start | bytes 589832 | tf_op jit(solution)/shard_map/ppermute | solution.py:40
  17.8 5.0 %collective-permute-start.5 = (bf16[128,768]{1,0:T(8,128)(2,1)S(1)}, bf16[128,768]{1,0:T(8,128)(2,1)S(1)}, u32[]{:S(2)}, u32[]{:S(2)}) collective-permute-start(bf16[128,768]{1,0:T(8,128)(2,1)S(1)} %collective-permute-done.4.refs_1_.refs_7_), channel_id=1, source_target_pairs={{0,2},{1,3},{2,0},{3,1},{4,6},{5,7},{6,4},{7,5},{8,10},{9,11},{10,... | collective-permute-start | bytes 589832 | tf_op jit(solution)/shard_map/ppermute | solution.py:64
  23.4 6.3 %sides.1 = (s32[48,128]{1,0:T(8,128)}, f32[16,1792]{1,0:T(8,128)}, f32[128,128]{1,0:T(8,128)}, f32[16,128]{1,0:T(8,128)}, f32[4,128,128]{2,1,0:T(8,128)}, /*inde...) custom-call(s32[1]{0:T(128)} %bitcast.flat_ref, f32[3,4096]{1,0:T(4,128)} %pos_ref.1, ...), custom_call_target="tpu_custom_call" | custom-call | flops 1000000000 | bytes 5000000 | tf_op jit(solution)/shard_map/sides/pallas_call | solution.py:1239
  34.2 9.9 %pair_bias.1.refs_21_.refs_7_.refs_23_ = f32[7,128,32,256]{3,2,1,0:T(8,128)} custom-call(s32[48,128]{1,0:T(8,128)} %get-tuple-element.53.span_ref, bf16[128,768]{1,0:T(8,128)(2,1)} %copy-done.31, bf16[128,768]{1,0:T(8,128)(2,1)} %copy-done.32, f32[128,128]{1,0:T(8,128)} %get-tuple-element.54.refs_2_.refs_0_.refs_6_, ...), custom_call_target="tpu_custom_call" | custom-call | flops 30000001024 | bytes 20000000 | tf_op jit(solution)/shard_map/pair_bias/pallas_call | solution.py:1226
  45.7 18.5 %attention_forward.1 = (f32[128,1024]{1,0:T(8,128)}, bf16[128,1024]{1,0:T(8,128)(2,1)}, bf16[3,128,128]{2,1,0:T(8,128)(2,1)}, bf16[256,768]{1,0:T(8,128)(2,1)}, bf16[7,256,3072]{2,1,0:T(8,128)(2,1)}) custom-call(s32[48,128]{1,0:T(8,128)} %get-tuple-element.53.span_ref, f32[128,128]{1,0:T(8,128)} %get-tuple-element.54.refs_2_.refs_0_.refs_6_, ...), custom_call_target="tpu_custom_call" | custom-call | flops 24999999488 | bytes 20000000 | tf_op jit(solution)/shard_map/attention_forward/pallas_call | solution.py:1226
  64.2 19.0 %feed_forward.1 = (bf16[128,768]{1,0:T(8,128)(2,1)}, f32[128,768]{1,0:T(8,128)}, bf16[128,1024]{1,0:T(8,128)(2,1)}, bf16[128,1024]{1,0:T(8,128)(2,1)}, bf16[128,...) custom-call(s32[1]{0:T(128)} %bitcast.flat_ref, ...), custom_call_target="tpu_custom_call" | custom-call | flops 10000000000 | bytes 5000000 | tf_op jit(solution)/shard_map/feed_forward/pallas_call | solution.py:1239
  84.9 5.2 %collective-permute-start.13 = (bf16[2,8,128,192]{2,3,1,0:T(8,128)(2,1)S(1)}, bf16[2,8,128,192]{2,3,1,0:T(8,128)(2,1)S(1)}, u32[]{:S(2)}, u32[]{:S(2)}) collective-permute-start(bf16[2,8,128,192]{2,3,1,0:T(8,128)(2,1)S(1)} %copy.54), channel_id=1, source_target_pairs={{0,1},{1,0},{2,3},{3,2},{4,5},{5,4},{6,7},{7,6},{8,9},{9,8},{10,11... | collective-permute-start | bytes 2359304 | tf_op jit(solution)/shard_map/ppermute | solution.py:45
  94.3 10.5 %weight_gradients.1 = (bf16[4,192,768]{2,1,0:T(8,128)(2,1)}, bf16[4,192,768]{2,1,0:T(8,128)(2,1)}, bf16[8,240,384]{2,1,0:T(8,128)(2,1)}, bf16[8,240,384]{2,1,0:T(8,128)(2,1)}, bf16[128,1024]{1,0:T(8,128)(2,1)}) custom-call(s32[1]{0:T(128)} %bitcast.flat_ref, bf16[2,8,128,192]{3,2,1,0:T(8,128)(2,1)} %get-tuple-element.61.mine_ref, ...), custom_call_target="tpu_custom_call" | custom-call | flops 5000000000 | bytes 5000000 | tf_op jit(solution)/shard_map/weight_gradients/pallas_call | solution.py:1239
  105.5 37.2 %collective-permute-start.23 = (bf16[128,1024]{1,0:T(8,128)(2,1)}, bf16[128,1024]{1,0:T(8,128)(2,1)S(1)}, u32[]{:S(2)}, u32[]{:S(2)}) collective-permute-start(bf16[128,1024]{1,0:T(8,128)(2,1)} %get-tuple-element.74.refs_9_), channel_id=1, source_target_pairs={{0,4},{1,5},{2,6},{3,7},{4,8},{5,9},{6,10},{7,11},{8,12},{9,13},{1... | collective-permute-start | bytes 786440 | tf_op jit(solution)/shard_map/ppermute | solution.py:40
  144.2 4.8 %collective-permute-start.18 = (bf16[4,192,768]{2,1,0:T(8,128)(2,1)}, bf16[4,192,768]{2,1,0:T(8,128)(2,1)S(1)}, u32[]{:S(2)}, u32[]{:S(2)}) collective-permute-start(bf16[4,192,768]{2,1,0:T(8,128)(2,1)} %get-tuple-element.66.refs_0_), channel_id=1, source_target_pairs={{0,2},{1,3},{2,0},{3,1},{4,6},{5,7},{6,4},{7,5},{8,10},{9,11},{10,... | collective-permute-start | bytes 3538952 | tf_op jit(solution)/shard_map/ppermute | solution.py:82
  151.5 13.6 %query_gradients.1 = (bf16[128,768]{1,0:T(8,128)(2,1)}, bf16[7,128,32,256]{3,2,1,0:T(8,128)(2,1)}) custom-call(s32[48,128]{1,0:T(8,128)} %get-tuple-element.53.span_ref, bf16[4,192,768]{2,1,0:T(8,128)(2,1)} %get-tuple-element.66.refs_0_, bf16[8,240,384]{2,1,0:T(8,128)(2,1)} %get-tuple-element.67.refs_1_, ...), custom_call_target="tpu_custom_call" | custom-call | flops 22000001024 | bytes 20000000 | tf_op jit(solution)/shard_map/query_gradients/pallas_call | solution.py:1226
  170.8 9.5 %collective-permute-done.18 = bf16[4,192,768]{2,1,0:T(8,128)(2,1)S(1)} collective-permute-done((bf16[4,192,768]{2,1,0:T(8,128)(2,1)}, bf16[4,192,768]{2,1,0:T(8,128)(2,1)S(1)}, u32[]{:S(2)}, u32[]{:S(2)}) %collective-permute-start.18) | collective-permute-done | bytes 1179680 | tf_op jit(solution)/shard_map/ppermute | solution.py:82
  180.6 7.7 %collective-permute-done.20 = bf16[8,240,384]{2,1,0:T(8,128)(2,1)S(1)} collective-permute-done((bf16[8,240,384]{2,1,0:T(8,128)(2,1)}, bf16[8,240,384]{2,1,0:T(8,128)(2,1)S(1)}, u32[]{:S(2)}, u32[]{:S(2)}) %collective-permute-start.20) | collective-permute-done | bytes 1474592 | tf_op jit(solution)/shard_map/ppermute | solution.py:82
  189.9 11.6 %kernel_gradients.1 = (f32[128,128]{1,0:T(8,128)}, f32[132,128]{1,0:T(8,128)}) custom-call(s32[48,128]{1,0:T(8,128)} %get-tuple-element.53.span_ref, bf16[128,1024]{1,0:T(8,128)(2,1)} %copy-done.16, bf16[128,1024]{1,0:T(8,128)(2,1)} %collective-permute-done.26.refs_11_.refs_1_, bf16[128,1024]{1,0:T(8,128)(2,1)} %copy-done.15, bf16[128,1024]{1,0:T(8,128)(2,1)} %copy-done.18, ...), custom_call_target="tpu_custom_call" | custom-call | flops 44999999488 | bytes 20000000 | tf_op jit(solution)/shard_map/kernel_gradients/pallas_call | solution.py:1226
  205.1 6.6 %collective-permute-done.21 = bf16[4,1,240,384]{3,2,1,0:T(8,128)(2,1)S(1)} collective-permute-done((bf16[4,1,240,384]{3,2,1,0:T(8,128)(2,1)S(1)}, bf16[4,1,240,384]{3,2,1,0:T(8,128)(2,1)S(1)}, u32[]{:S(2)}, u32[]{:S(2)}) %collective-permute-start.21) | collective-permute-done | bytes 737312 | tf_op jit(solution)/shard_map/ppermute | solution.py:82
  214.4 17.5 %key_gradients.1.dkv_ref = bf16[128,1536]{1,0:T(8,128)(2,1)} custom-call(s32[48,128]{1,0:T(8,128)} %get-tuple-element.53.span_ref, bf16[1,1,192,768]{3,2,1,0:T(8,128)(2,1)} %constant_dynamic-slice_fusion.4.refs_0_, bf16[2,1,240,384]{3,2,1,0:T(8,128)(2,1)} %dynamic-slice_bitcast_fusion.2.refs_1_, f32[128,128]{1,0:T(8,128)} %get-tuple-element.54.refs_2_.refs_0_.refs_6_, ...), custom_call_target="tpu_custom_call" | custom-call | flops 28000000000 | bytes 20000000 | tf_op jit(solution)/shard_map/key_gradients/pallas_call | solution.py:1226
  232.0 4.6 %first_norm.1 = (f32[128,768]{1,0:T(8,128)}, f32[2,768]{1,0:T(2,128)}) custom-call(bf16[128,768]{1,0:T(8,128)(2,1)} %tok_ref.3, f32[2,768]{1,0:T(2,128)} %pad_maximum_fusion.1.refs_16_.ln_ref, bf16[128,768]{1,0:T(8,128)(2,1)} %get-tuple-element.71.dq_ref, bf16[128,1536]{1,0:T(8,128)(2,1)} %key_gradients.1.dkv_ref, bf16[768,2304]{1,0:T(8,128)(2,1)} %w_ref.1, ...), custom_call_target="tpu_custom_call" | custom-call | flops 2000000000 | bytes 5000000 | tf_op jit(solution)/shard_map/first_norm/pallas_call | solution.py:1239
  237.3 4.1 %collective-permute-start.34 = (f32[284,128]{1,0:T(8,128)S(1)}, f32[284,128]{1,0:T(8,128)S(1)}, u32[]{:S(2)}, u32[]{:S(2)}) collective-permute-start(f32[284,128]{1,0:T(8,128)S(1)} %pad_maximum_fusion), channel_id=1, source_target_pairs={{0,1},{1,0},{2,3},{3,2},{4,5},{5,4},{6,7},{7,6},{8,9},{9,8},{10,11... | collective-permute-start | bytes 436232 | tf_op jit(solution)/shard_map/ppermute | solution.py:82
  241.4 37.4 %collective-permute-start.53 = (bf16[1,1,192,768]{3,2,1,0:T(8,128)(2,1)S(1)}, bf16[1,1,192,768]{3,2,1,0:T(8,128)(2,1)S(1)}, u32[]{:S(2)}, u32[]{:S(2)}) collective-permute-start(bf16[1,1,192,768]{3,2,1,0:T(8,128)(2,1)S(1)} %copy-done.7), channel_id=1, source_target_pairs={{0,8},{1,9},{2,10},{3,11},{4,12},{5,13},{6,14},{7,15},{8,0},{9,1},... | collective-permute-start | bytes 884744 | tf_op jit(solution)/shard_map/ppermute | solution.py:82
  279.5 12.3 %collective-permute-done.53 = bf16[1,1,192,768]{3,2,1,0:T(8,128)(2,1)S(1)} collective-permute-done((bf16[1,1,192,768]{3,2,1,0:T(8,128)(2,1)S(1)}, bf16[1,1,192,768]{3,2,1,0:T(8,128)(2,1)S(1)}, u32[]{:S(2)}, u32[]{:S(2)}) %collective-permute-start.53) | collective-permute-done | bytes 294944 | tf_op jit(solution)/shard_map/ppermute | solution.py:82
  292.1 4.4 %collective-permute-done.50 = bf16[2,1,240,384]{3,2,1,0:T(8,128)(2,1)S(1)} collective-permute-done((bf16[2,1,240,384]{3,2,1,0:T(8,128)(2,1)S(1)}, bf16[2,1,240,384]{3,2,1,0:T(8,128)(2,1)S(1)}, u32[]{:S(2)}, u32[]{:S(2)}) %collective-permute-start.50) | collective-permute-done | bytes 368672 | tf_op jit(solution)/shard_map/ppermute | solution.py:82
  297.6 4.1 %qkv_gradients.1 = (bf16[4,144,256]{2,1,0:T(8,128)(2,1)}, bf16[4,144,256]{2,1,0:T(8,128)(2,1)}, bf16[8,144,256]{2,1,0:T(8,128)(2,1)}, bf16[8,144,256]{2,1,0:T(8,128)(2,1)}) custom-call(s32[1]{0:T(128)} %bitcast.flat_ref, bf16[128,768]{1,0:T(8,128)(2,1)} %get-tuple-element.71.dq_ref, bf16[128,768]{1,0:T(8,128)(2,1)} %copy-done.44, ...), custom_call_target="tpu_custom_call" | custom-call | flops 3000000000 | bytes 5000000 | tf_op jit(solution)/shard_map/qkv_gradients/pallas_call | solution.py:1239
  305.5 4.2 %collective-permute-done.51 = bf16[1,1,240,384]{3,2,1,0:T(8,128)(2,1)S(1)} collective-permute-done((bf16[1,1,240,384]{3,2,1,0:T(8,128)(2,1)S(1)}, bf16[1,1,240,384]{3,2,1,0:T(8,128)(2,1)S(1)}, u32[]{:S(2)}, u32[]{:S(2)}) %collective-permute-start.51) | collective-permute-done | bytes 184352 | tf_op jit(solution)/shard_map/ppermute | solution.py:82
  313.4 10.9 %collective-permute-done.38 = f32[284,128]{1,0:T(8,128)S(1)} collective-permute-done((f32[284,128]{1,0:T(8,128)S(1)}, f32[284,128]{1,0:T(8,128)S(1)}, u32[]{:S(2)}, u32[]{:S(2)}) %collective-permute-start.38) | collective-permute-done | bytes 145440 | tf_op jit(solution)/shard_map/ppermute | solution.py:82
  (259 shorter events, 80.7 us)
Async XLA Ops:
  0.6 22.2 %collective-permute-start.1 = (bf16[128,768]{1,0:T(8,128)(2,1)}, bf16[128,768]{1,0:T(8,128)(2,1)S(1)}, u32[]{:S(2)}, u32[]{:S(2)}) collective-permute-start(bf16[128,768]{1,0:T(8,128)(2,1)} %tok_ref.3), channel_id=1, source_target_pairs={{0,4},{1,5},{2,6},{3,7},{4,8},{5,9},{6,10},{7,11},{8,12},{9,13},{1... | collective-permute-start | bytes 589832 | tf_op jit(solution)/shard_map/ppermute | solution.py:40
  6.9 16.1 %collective-permute-start.3 = (bf16[128,768]{1,0:T(8,128)(2,1)}, bf16[128,768]{1,0:T(8,128)(2,1)S(1)}, u32[]{:S(2)}, u32[]{:S(2)}) collective-permute-start(bf16[128,768]{1,0:T(8,128)(2,1)} %tok_ref.3), channel_id=1, source_target_pairs={{0,2},{1,3},{2,0},{3,1},{4,6},{5,7},{6,4},{7,5},{8,10},{9,11},{10,... | collective-permute-start | bytes 589832 | tf_op jit(solution)/shard_map/ppermute | solution.py:57
  8.5 21.8 %collective-permute-start = (bf16[128,768]{1,0:T(8,128)(2,1)}, bf16[128,768]{1,0:T(8,128)(2,1)S(1)}, u32[]{:S(2)}, u32[]{:S(2)}) collective-permute-start(bf16[128,768]{1,0:T(8,128)(2,1)} %tok_ref.3), channel_id=1, source_target_pairs={{8,2},{9,3},{12,6},{13,7},{2,8},{3,9},{16,10},{17,11},{6,12},{7,13... | collective-permute-start | bytes 589832 | tf_op jit(solution)/shard_map/ppermute | solution.py:56
  9.1 21.2 %collective-permute-start.9 = (bf16[128,768]{1,0:T(8,128)(2,1)}, bf16[128,768]{1,0:T(8,128)(2,1)S(1)}, u32[]{:S(2)}, u32[]{:S(2)}) collective-permute-start(bf16[128,768]{1,0:T(8,128)(2,1)} %tok_ref.3), channel_id=1, source_target_pairs={{0,1},{1,0},{2,3},{3,2},{4,5},{5,4},{6,7},{7,6},{8,9},{9,8},{10,11... | collective-permute-start | bytes 589832 | tf_op jit(solution)/shard_map/ppermute | solution.py:45
  30.3 13.8 %collective-permute-start.7 = (bf16[128,768]{1,0:T(8,128)(2,1)S(1)}, bf16[128,768]{1,0:T(8,128)(2,1)S(1)}, u32[]{:S(2)}, u32[]{:S(2)}) collective-permute-start(bf16[128,768]{1,0:T(8,128)(2,1)S(1)} %collective-permute-done.1.refs_0_.refs_3_), channel_id=1, source_target_pairs={{0,1},{1,0},{2,3},{3,2},{4,5},{5,4},{6,7},{7,6},{8,9},{9,8},{10,11... | collective-permute-start | bytes 589832 | tf_op jit(solution)/shard_map/ppermute | solution.py:45
  104.8 60.3 %collective-permute-start.22 = (bf16[128,1024]{1,0:T(8,128)(2,1)}, bf16[128,1024]{1,0:T(8,128)(2,1)S(1)}, u32[]{:S(2)}, u32[]{:S(2)}) collective-permute-start(bf16[128,1024]{1,0:T(8,128)(2,1)} %get-tuple-element.74.refs_9_), channel_id=1, source_target_pairs={{8,2},{9,3},{12,6},{13,7},{2,8},{3,9},{16,10},{17,11},{6,12},{7,13... | collective-permute-start | bytes 786440 | tf_op jit(solution)/shard_map/ppermute | solution.py:56
  105.5 63.3 %collective-permute-start.23 = (bf16[128,1024]{1,0:T(8,128)(2,1)}, bf16[128,1024]{1,0:T(8,128)(2,1)S(1)}, u32[]{:S(2)}, u32[]{:S(2)}) collective-permute-start(bf16[128,1024]{1,0:T(8,128)(2,1)} %get-tuple-element.74.refs_9_), channel_id=1, source_target_pairs={{0,4},{1,5},{2,6},{3,7},{4,8},{5,9},{6,10},{7,11},{8,12},{9,13},{1... | collective-permute-start | bytes 786440 | tf_op jit(solution)/shard_map/ppermute | solution.py:40
  142.7 26.1 %collective-permute-start.26 = (bf16[128,1024]{1,0:T(8,128)(2,1)}, bf16[128,1024]{1,0:T(8,128)(2,1)}, u32[]{:S(2)}, u32[]{:S(2)}) collective-permute-start(bf16[128,1024]{1,0:T(8,128)(2,1)} %get-tuple-element.74.refs_9_), channel_id=1, source_target_pairs={{4,0},{5,1},{6,2},{7,3},{8,4},{9,5},{10,6},{11,7},{12,8},{13,9},{1... | collective-permute-start | bytes 786440 | tf_op jit(solution)/shard_map/ppermute | solution.py:40
  144.2 36.1 %collective-permute-start.18 = (bf16[4,192,768]{2,1,0:T(8,128)(2,1)}, bf16[4,192,768]{2,1,0:T(8,128)(2,1)S(1)}, u32[]{:S(2)}, u32[]{:S(2)}) collective-permute-start(bf16[4,192,768]{2,1,0:T(8,128)(2,1)} %get-tuple-element.66.refs_0_), channel_id=1, source_target_pairs={{0,2},{1,3},{2,0},{3,1},{4,6},{5,7},{6,4},{7,5},{8,10},{9,11},{10,... | collective-permute-start | bytes 3538952 | tf_op jit(solution)/shard_map/ppermute | solution.py:82
  149.0 39.4 %collective-permute-start.20 = (bf16[8,240,384]{2,1,0:T(8,128)(2,1)}, bf16[8,240,384]{2,1,0:T(8,128)(2,1)S(1)}, u32[]{:S(2)}, u32[]{:S(2)}) collective-permute-start(bf16[8,240,384]{2,1,0:T(8,128)(2,1)} %get-tuple-element.67.refs_1_), channel_id=1, source_target_pairs={{0,16},{16,0},{1,17},{17,1},{2,18},{18,2},{3,19},{19,3},{4,20},{20... | collective-permute-start | bytes 4423688 | tf_op jit(solution)/shard_map/ppermute | solution.py:82
  165.1 23.8 %collective-permute-start.25 = (bf16[128,1024]{1,0:T(8,128)(2,1)S(1)}, bf16[128,1024]{1,0:T(8,128)(2,1)S(1)}, u32[]{:S(2)}, u32[]{:S(2)}) collective-permute-start(bf16[128,1024]{1,0:T(8,128)(2,1)S(1)} %copy-done.14), channel_id=1, source_target_pairs={{0,2},{1,3},{2,0},{3,1},{4,6},{5,7},{6,4},{7,5},{8,10},{9,11},{10,... | collective-permute-start | bytes 786440 | tf_op jit(solution)/shard_map/ppermute | solution.py:57
  168.7 35.3 %collective-permute-start.24 = (bf16[128,1024]{1,0:T(8,128)(2,1)S(1)}, bf16[128,1024]{1,0:T(8,128)(2,1)S(1)}, u32[]{:S(2)}, u32[]{:S(2)}) collective-permute-start(bf16[128,1024]{1,0:T(8,128)(2,1)S(1)} %collective-permute-done.23.refs_7_.refs_0_), channel_id=1, source_target_pairs={{0,2},{1,3},{2,0},{3,1},{4,6},{5,7},{6,4},{7,5},{8,10},{9,11},{10,... | collective-permute-start | bytes 786440 | tf_op jit(solution)/shard_map/ppermute | solution.py:64
  168.8 35.8 %collective-permute-start.27 = (bf16[128,1024]{1,0:T(8,128)(2,1)}, bf16[128,1024]{1,0:T(8,128)(2,1)S(1)}, u32[]{:S(2)}, u32[]{:S(2)}) collective-permute-start(bf16[128,1024]{1,0:T(8,128)(2,1)} %collective-permute-done.26.refs_11_.refs_1_), channel_id=1, source_target_pairs={{0,2},{1,3},{2,0},{3,1},{4,6},{5,7},{6,4},{7,5},{8,10},{9,11},{10,... | collective-permute-start | bytes 786440 | tf_op jit(solution)/shard_map/ppermute | solution.py:64
  180.3 24.4 %collective-permute-start.28 = (bf16[128,1024]{1,0:T(8,128)(2,1)S(1)}, bf16[128,1024]{1,0:T(8,128)(2,1)S(1)}, u32[]{:S(2)}, u32[]{:S(2)}) collective-permute-start(bf16[128,1024]{1,0:T(8,128)(2,1)S(1)} %collective-permute-done.22.refs_6_.refs_2_), channel_id=1, source_target_pairs={{0,1},{1,0},{2,3},{3,2},{4,5},{5,4},{6,7},{7,6},{8,9},{9,8},{10,11... | collective-permute-start | bytes 786440 | tf_op jit(solution)/shard_map/ppermute | solution.py:45
  188.4 14.7 %collective-permute-start.19 = (bf16[2,1,192,768]{3,2,1,0:T(8,128)(2,1)S(1)}, bf16[2,1,192,768]{3,2,1,0:T(8,128)(2,1)S(1)}, u32[]{:S(2)}, u32[]{:S(2)}) collective-permute-start(bf16[2,1,192,768]{3,2,1,0:T(8,128)(2,1)S(1)} %dynamic-slice_bitcast_fusion.1.refs_4_), channel_id=1, source_target_pairs={{0,4},{1,5},{2,6},{3,7},{4,0},{5,1},{6,2},{7,3},{8,12},{9,13},{10,... | collective-permute-start | bytes 1769480 | tf_op jit(solution)/shard_map/ppermute | solution.py:82
  188.9 22.8 %collective-permute-start.21 = (bf16[4,1,240,384]{3,2,1,0:T(8,128)(2,1)S(1)}, bf16[4,1,240,384]{3,2,1,0:T(8,128)(2,1)S(1)}, u32[]{:S(2)}, u32[]{:S(2)}) collective-permute-start(bf16[4,1,240,384]{3,2,1,0:T(8,128)(2,1)S(1)} %dynamic-slice_bitcast_fusion.refs_5_), channel_id=1, source_target_pairs={{0,2},{1,3},{2,0},{3,1},{4,6},{5,7},{6,4},{7,5},{8,10},{9,11},{10,... | collective-permute-start | bytes 2211848 | tf_op jit(solution)/shard_map/ppermute | solution.py:82
  237.3 42.1 %collective-permute-start.34 = (f32[284,128]{1,0:T(8,128)S(1)}, f32[284,128]{1,0:T(8,128)S(1)}, u32[]{:S(2)}, u32[]{:S(2)}) collective-permute-start(f32[284,128]{1,0:T(8,128)S(1)} %pad_maximum_fusion), channel_id=1, source_target_pairs={{0,1},{1,0},{2,3},{3,2},{4,5},{5,4},{6,7},{7,6},{8,9},{9,8},{10,11... | collective-permute-start | bytes 436232 | tf_op jit(solution)/shard_map/ppermute | solution.py:82
  241.4 50.4 %collective-permute-start.53 = (bf16[1,1,192,768]{3,2,1,0:T(8,128)(2,1)S(1)}, bf16[1,1,192,768]{3,2,1,0:T(8,128)(2,1)S(1)}, u32[]{:S(2)}, u32[]{:S(2)}) collective-permute-start(bf16[1,1,192,768]{3,2,1,0:T(8,128)(2,1)S(1)} %copy-done.7), channel_id=1, source_target_pairs={{0,8},{1,9},{2,10},{3,11},{4,12},{5,13},{6,14},{7,15},{8,0},{9,1},... | collective-permute-start | bytes 884744 | tf_op jit(solution)/shard_map/ppermute | solution.py:82
  278.8 17.9 %collective-permute-start.39 = (bf16[128,768]{1,0:T(8,128)(2,1)S(1)}, bf16[128,768]{1,0:T(8,128)(2,1)S(1)}, u32[]{:S(2)}, u32[]{:S(2)}) collective-permute-start(bf16[128,768]{1,0:T(8,128)(2,1)S(1)} %copy-done.30), channel_id=1, source_target_pairs={{0,1},{1,0},{2,3},{3,2},{4,5},{5,4},{6,7},{7,6},{8,9},{9,8},{10,11... | collective-permute-start | bytes 589832 | tf_op jit(solution)/shard_map/ppermute | solution.py:45
  278.8 17.7 %collective-permute-start.50 = (bf16[2,1,240,384]{3,2,1,0:T(8,128)(2,1)S(1)}, bf16[2,1,240,384]{3,2,1,0:T(8,128)(2,1)S(1)}, u32[]{:S(2)}, u32[]{:S(2)}) collective-permute-start(bf16[2,1,240,384]{3,2,1,0:T(8,128)(2,1)S(1)} %copy-done.5), channel_id=1, source_target_pairs={{0,4},{1,5},{2,6},{3,7},{4,0},{5,1},{6,2},{7,3},{8,12},{9,13},{10,... | collective-permute-start | bytes 1105928 | tf_op jit(solution)/shard_map/ppermute | solution.py:82
  278.9 17.8 %collective-permute-start.40 = (bf16[128,1536]{1,0:T(8,128)(2,1)S(1)}, bf16[128,1536]{1,0:T(8,128)(2,1)S(1)}, u32[]{:S(2)}, u32[]{:S(2)}) collective-permute-start(bf16[128,1536]{1,0:T(8,128)(2,1)S(1)} %copy-done.11), channel_id=1, source_target_pairs={{0,1},{1,0},{2,3},{3,2},{4,5},{5,4},{6,7},{7,6},{8,9},{9,8},{10,11... | collective-permute-start | bytes 1179656 | tf_op jit(solution)/shard_map/ppermute | solution.py:45
  303.1 24.9 %collective-permute-start.45 = (bf16[8,144,256]{2,1,0:T(8,128)(2,1)}, bf16[8,144,256]{2,1,0:T(8,128)(2,1)S(1)}, u32[]{:S(2)}, u32[]{:S(2)}) collective-permute-start(bf16[8,144,256]{2,1,0:T(8,128)(2,1)} %get-tuple-element.89), channel_id=1, source_target_pairs={{0,16},{16,0},{1,17},{17,1},{2,18},{18,2},{3,19},{19,3},{4,20},{20... | collective-permute-start | bytes 1769480 | tf_op jit(solution)/shard_map/ppermute | solution.py:82
  309.8 18.1 %collective-permute-start.52 = (bf16[240,384]{1,0:T(8,128)(2,1)S(1)}, bf16[240,384]{1,0:T(8,128)(2,1)S(1)}, u32[]{:S(2)}, u32[]{:S(2)}) collective-permute-start(bf16[240,384]{1,0:T(8,128)(2,1)S(1)} %fusion.7), channel_id=1, source_target_pairs={{0,16},{16,0},{1,17},{17,1},{2,18},{18,2},{3,19},{19,3},{4,20},{20... | collective-permute-start | bytes 552968 | tf_op jit(solution)/shard_map/ppermute | solution.py:82
  313.3 22.8 %collective-permute-start.42 = (bf16[2,1,144,256]{3,2,1,0:T(8,128)(2,1)S(1)}, bf16[2,1,144,256]{3,2,1,0:T(8,128)(2,1)S(1)}, u32[]{:S(2)}, u32[]{:S(2)}) collective-permute-start(bf16[2,1,144,256]{3,2,1,0:T(8,128)(2,1)S(1)} %dynamic-slice_bitcast_fusion.5), channel_id=1, source_target_pairs={{0,4},{1,5},{2,6},{3,7},{4,0},{5,1},{6,2},{7,3},{8,12},{9,13},{10,... | collective-permute-start | bytes 442376 | tf_op jit(solution)/shard_map/ppermute | solution.py:82
  (81 other events, 717.1 us)
